TPU v7x, 512 devices: a whole 4x8x8 slice. The times are simulated.
512 devices in a mesh: seq: 64 (over y_lo, x, z), head: 8 (over y_hi, core).
Axes of the slice: x: 4, y: 8 (y_hi: 4, y_lo: 2; y = y_hi * 2 + y_lo), z: 8, core: 2. Of those that a mesh axis runs over, the one named last changes fastest.
Arguments:
- queries: bfloat16 [49152, 2048], P(('seq', 'head')), may hold values from -6 to 6
- keys: bfloat16 [49152, 2048], P(('seq', 'head')), may hold values from -6 to 6
- values: bfloat16 [49152, 2048], P(('seq', 'head')), may hold values from -6 to 6
- out_grad: bfloat16 [49152, 2048], P(('seq', 'head')), may hold values from -6 to 6
- window: int32 [16, 2], replicated, may hold values from 0 to 1, as said below
Outputs:
- grad_queries: bfloat16 [49152, 2048], P(('seq', 'head'))
- grad_keys: bfloat16 [49152, 2048], P(('seq', 'head'))
- grad_values: bfloat16 [49152, 2048], P(('seq', 'head'))
Inputs may be any that keep to these rules, and one draw needn't show every extreme that they name: `window`: some head reaches 1 along both time and height, some head 0 along both.
All inputs are finite; a program needn't handle non-finite values.
Results may differ from a plain program's by a relative error of at most 0.0066.
Values may be sent and summed in bfloat16 or wider, within the bound.
No kernel may reach another device: no remote copies, remote signals or barrier semaphores. Data moves between devices by JAX's collectives and lax.ppermute only.
A program may use at most 128 MiB of HBM per device.

v0:
```python
import jax
import jax.numpy as jnp
from jax import lax
from jax.sharding import PartitionSpec as P

HD = 128
GH = 4


OFFSETS = tuple(((time_off, row_off) for time_off in (-1, 0, 1) for row_off in (-1, 0, 1)))


def passed_along(block, axis, distance):
    devices = range(lax.axis_size(axis))
    route = [(i - distance, i) for i in devices if i - distance in devices]
    return lax.ppermute(block, axis, route)


def shortened(array):

    def short(part):
        return part.astype(jnp.bfloat16) if part.dtype == jnp.float32 else part

    return jax.tree.map(short, array)


def neighbour_columns(payload):
    count = len(payload)
    columns = []
    for row_off in (-1, 0, 1):
        if row_off == 0:
            middle = payload
        else:
            middle = passed_along((payload[0], payload[1]), "seq", -row_off)
        far_ends = {}
        for time_off, pick in ((-1, 1), (1, 0)):
            far_ends[time_off] = passed_along(
                shortened(tuple((member[pick] for member in payload))),
                "seq",
                -(time_off * GH + row_off),
            )
        columns.append(
            tuple(
                (
                    jnp.concatenate(
                        [
                            far_ends[-1][member_num][None],
                            middle[member_num],
                            far_ends[1][member_num][None],
                        ],
                        axis=0,
                    )
                    for member_num in range(count)
                )
            )
        )
    return tuple(
        (jnp.stack([column[member_num] for column in columns]) for member_num in range(count))
    )


def column_windows(column):
    heads_here = column.shape[3]
    picked = jnp.stack([column[:, tile_num : tile_num + 3] for tile_num in (0, 1)])
    picked = jnp.transpose(picked, (0, 4, 2, 1, 3, 5))
    return picked.reshape(2 * heads_here, 9, column.shape[2], column.shape[4])


def terms_to_columns(terms, heads_here):
    shaped = terms.reshape(2, heads_here, 3, 3, terms.shape[2], terms.shape[3])
    shaped = jnp.transpose(shaped, (0, 3, 2, 4, 1, 5))
    first = jnp.pad(shaped[0], ((0, 0), (0, 1), (0, 0), (0, 0), (0, 0)))
    second = jnp.pad(shaped[1], ((0, 0), (1, 0), (0, 0), (0, 0), (0, 0)))
    return first + second


def to_items(tiles):
    return jnp.transpose(tiles, (0, 2, 1, 3)).reshape(
        2 * tiles.shape[2], tiles.shape[1], tiles.shape[3]
    )


def items_to_rows(items, heads_here):
    shaped = items.reshape(2, heads_here, items.shape[1], items.shape[2])
    return jnp.transpose(shaped, (0, 2, 1, 3)).reshape(
        2 * items.shape[1], heads_here * items.shape[2]
    )


def window_mask(window, heads_here):
    seq_index = lax.axis_index("seq")
    grid_time = 2 * (lax.axis_size("seq") // GH)
    slab_time = 2 * (seq_index // GH)
    tile_row = seq_index % GH
    reaches = lax.dynamic_slice_in_dim(window, lax.axis_index("head") * heads_here, heads_here, 0)
    per_tile = []
    for tile_num in (0, 1):
        columns = []
        for time_off, row_off in OFFSETS:
            near_time = slab_time + tile_num + time_off
            inside = (near_time >= 0) & (near_time < grid_time)
            inside = inside & (tile_row + row_off >= 0) & (tile_row + row_off < GH)
            allowed = inside & (abs(time_off) <= reaches[:, 0]) & (abs(row_off) <= reaches[:, 1])
            columns.append(allowed)
        per_tile.append(jnp.stack(columns, axis=1))
    return jnp.stack(per_tile).reshape(2 * heads_here, 9)


def query_core(query_head, grad_head, key_head, value_head, mask_row):
    score_scale = HD ** (-0.5)
    scores = (
        jnp.einsum("qd,okd->oqk", query_head, key_head, preferred_element_type=jnp.float32)
        * score_scale
    )
    scores = jnp.where(mask_row[:, None, None], scores, -jnp.inf)
    row_max = jnp.max(scores, axis=(0, 2))
    log_total = row_max + jnp.log(jnp.sum(jnp.exp(scores - row_max[None, :, None]), axis=(0, 2)))
    weights = jnp.exp(scores - log_total[None, :, None])
    grad_scores = jnp.einsum(
        "qd,okd->oqk", grad_head, value_head, preferred_element_type=jnp.float32
    )
    row_delta = jnp.sum(weights * grad_scores, axis=(0, 2))
    dscore = (weights * (grad_scores - row_delta[None, :, None])).astype(jnp.bfloat16)
    grad_query = (
        jnp.einsum("oqk,okd->qd", dscore, key_head, preferred_element_type=jnp.float32)
        * score_scale
    )
    return (weights.astype(jnp.bfloat16), dscore, log_total, row_delta, grad_query)


def query_with_terms(operands):
    query_head, grad_head, key_head, value_head, mask_row = operands
    rounded_probs, dscore, log_total, row_delta, grad_query = query_core(
        query_head, grad_head, key_head, value_head, mask_row
    )
    value_terms = jnp.einsum(
        "oqk,qd->okd", rounded_probs, grad_head, preferred_element_type=jnp.float32
    )
    key_terms = jnp.einsum(
        "oqk,qd->okd", dscore, query_head, preferred_element_type=jnp.float32
    ) * HD ** (-0.5)
    return (grad_query, key_terms, value_terms)


def per_device(queries, keys, values, out_grad, window):
    q_all, k_all, v_all, g_all = (
        lax.all_to_all(queries, "head", split_axis=1, concat_axis=0, tiled=True),
        lax.all_to_all(keys, "head", split_axis=1, concat_axis=0, tiled=True),
        lax.all_to_all(values, "head", split_axis=1, concat_axis=0, tiled=True),
        lax.all_to_all(out_grad, "head", split_axis=1, concat_axis=0, tiled=True),
    )
    tile_rows = q_all.shape[0] // 2
    heads_here = q_all.shape[1] // HD
    tile_shape = (2, tile_rows, heads_here, HD)
    q_here = q_all.reshape(tile_shape)
    k_here = k_all.reshape(tile_shape)
    v_here = v_all.reshape(tile_shape)
    g_here = g_all.reshape(tile_shape)
    visible = window_mask(window, heads_here)
    key_column, value_column = neighbour_columns((k_here, v_here))
    query_items = to_items(q_here)
    grad_items = to_items(g_here)
    operands = (
        query_items,
        grad_items,
        column_windows(key_column),
        column_windows(value_column),
        visible,
    )
    grad_query, key_terms, value_terms = lax.map(query_with_terms, operands)
    key_back = terms_to_columns(key_terms, heads_here)
    value_back = terms_to_columns(value_terms, heads_here)
    key_own = [key_back[1, 1], key_back[1, 2]]
    value_own = [value_back[1, 1], value_back[1, 2]]
    for row_off in (-1, 1):
        arrived_key, arrived_value = passed_along(
            (key_back[row_off + 1, 1:3], value_back[row_off + 1, 1:3]), "seq", row_off
        )
        for tile_num in (0, 1):
            key_own[tile_num] = key_own[tile_num] + arrived_key[tile_num]
            value_own[tile_num] = value_own[tile_num] + arrived_value[tile_num]
    for row_off in (-1, 0, 1):
        for time_off, place, target in ((-1, 0, 1), (1, 3, 0)):
            arrived_key, arrived_value = (
                passed_along(
                    key_back[row_off + 1, place].astype(jnp.bfloat16),
                    "seq",
                    time_off * GH + row_off,
                ).astype(jnp.float32),
                passed_along(
                    value_back[row_off + 1, place].astype(jnp.bfloat16),
                    "seq",
                    time_off * GH + row_off,
                ).astype(jnp.float32),
            )
            key_own[target] = key_own[target] + arrived_key
            value_own[target] = value_own[target] + arrived_value
    grad_keys = jnp.stack(key_own).reshape(2 * tile_rows, heads_here * HD).astype(jnp.bfloat16)
    grad_values = jnp.stack(value_own).reshape(2 * tile_rows, heads_here * HD).astype(jnp.bfloat16)
    grad_queries = items_to_rows(grad_query, heads_here).astype(jnp.bfloat16)
    return (
        lax.all_to_all(grad_queries, "head", split_axis=0, concat_axis=1, tiled=True),
        lax.all_to_all(grad_keys, "head", split_axis=0, concat_axis=1, tiled=True),
        lax.all_to_all(grad_values, "head", split_axis=0, concat_axis=1, tiled=True),
    )


def solution(mesh):
    return jax.shard_map(
        per_device,
        mesh=mesh,
        in_specs=(
            P(("seq", "head"), None),
            P(("seq", "head"), None),
            P(("seq", "head"), None),
            P(("seq", "head"), None),
            P(),
        ),
        out_specs=(P(("seq", "head"), None), P(("seq", "head"), None), P(("seq", "head"), None)),
        check_vma=False,
    )
```

profile of v0, /device:TPU:14, one launch (start us, length us, event | category | flops | bytes accessed | tf_op | source)
XLA Modules:
  0.0 512.7 jit_solution(17574792128044537964)
XLA Ops:
  2.5 6.2 %all-to-all-start.2 = ((bf16[96,8,256]{2,0,1:T(8,128)(2,1)}), bf16[96,8,256]{2,0,1:T(8,128)(2,1)S(1)}, u32[]{:S(2)}, u32[]{:S(2)}) async-start(bf16[96,8,256]{2,0,1:T(8,128)(2,1)} %bitcast.313), calls=%async_computation.2 | async-start | bytes 786432 | tf_op jit(solution)/shard_map/all_to_all | solution.py:149
  10.4 13.7 %all-to-all-done.2 = bf16[96,8,256]{2,0,1:T(8,128)(2,1)S(1)} async-done(((bf16[96,8,256]{2,0,1:T(8,128)(2,1)}), bf16[96,8,256]{2,0,1:T(8,128)(2,1)S(1)}, u32[]{:S(2)}, u32[]{:S(2)}) %all-to-all-start.2) | async-done | bytes 393248 | tf_op jit(solution)/shard_map/all_to_all | solution.py:149
  24.1 3.5 all-to-all-start
  29.4 13.2 %all-to-all-done = bf16[96,8,256]{2,0,1:T(8,128)(2,1)S(1)} async-done(((bf16[96,8,256]{2,0,1:T(8,128)(2,1)}), bf16[96,8,256]{2,0,1:T(8,128)(2,1)S(1)}, u32[]{:S(2)}, u32[]{:S(2)}) %all-to-all-start) | async-done | bytes 393248 | tf_op jit(solution)/shard_map/all_to_all | solution.py:148
  42.6 3.5 all-to-all-start.1
  47.1 14.2 %all-to-all-done.1 = bf16[96,8,256]{2,0,1:T(8,128)(2,1)S(1)} async-done(((bf16[96,8,256]{2,0,1:T(8,128)(2,1)}), bf16[96,8,256]{2,0,1:T(8,128)(2,1)S(1)}, u32[]{:S(2)}, u32[]{:S(2)}) %all-to-all-start.1) | async-done | bytes 393248 | tf_op jit(solution)/shard_map/all_to_all | solution.py:147
  61.3 3.5 all-to-all-start.3
  65.9 10.9 %collective-permute-start.8 = (bf16[384,2,128]{2,1,0:T(2,128)(2,1)}, bf16[384,2,128]{2,1,0:T(2,128)(2,1)S(1)}, u32[]{:S(2)}, u32[]{:S(2)}) collective-permute-start(bf16[384,2,128]{2,1,0:T(2,128)(2,1)} %squeeze.66), channel_id=1, source_target_pairs={{0,40},{8,48},{16,56},{24,64},{32,72},{40,80},{48,88},{56,96},{64,... | collective-permute-start | bytes 589832 | tf_op jit(solution)/shard_map/ppermute | solution.py:16
  79.5 8.7 %collective-permute-start.10 = (bf16[384,2,128]{2,1,0:T(2,128)(2,1)}, bf16[384,2,128]{2,1,0:T(2,128)(2,1)S(1)}, u32[]{:S(2)}, u32[]{:S(2)}) collective-permute-start(bf16[384,2,128]{2,1,0:T(2,128)(2,1)} %squeeze.67), channel_id=1, source_target_pairs={{24,0},{32,8},{40,16},{48,24},{56,32},{64,40},{72,48},{80,56},{88,... | collective-permute-start | bytes 589832 | tf_op jit(solution)/shard_map/ppermute | solution.py:16
  90.2 3.4 collective-permute-start.9
  96.3 7.8 %collective-permute-start.3 = (bf16[384,2,128]{2,1,0:T(2,128)(2,1)}, bf16[384,2,128]{2,1,0:T(2,128)(2,1)S(1)}, u32[]{:S(2)}, u32[]{:S(2)}) collective-permute-start(bf16[384,2,128]{2,1,0:T(2,128)(2,1)} %squeeze.64), channel_id=1, source_target_pairs={{0,32},{8,40},{16,48},{24,56},{32,64},{40,72},{48,80},{56,88},{64,... | collective-permute-start | bytes 589832 | tf_op jit(solution)/shard_map/ppermute | solution.py:16
  104.1 4.3 collective-permute-done.12
  108.4 2.6 collective-permute-start.4
  112.3 14.0 %collective-permute-done.3 = bf16[384,2,128]{2,1,0:T(2,128)(2,1)S(1)} collective-permute-done((bf16[384,2,128]{2,1,0:T(2,128)(2,1)}, bf16[384,2,128]{2,1,0:T(2,128)(2,1)S(1)}, u32[]{:S(2)}, u32[]{:S(2)}) %collective-permute-start.3) | collective-permute-done | bytes 196640 | tf_op jit(solution)/shard_map/ppermute | solution.py:16
  126.3 19.6 %collective-permute-start.13 = (bf16[384,2,128]{2,1,0:T(2,128)(2,1)}, bf16[384,2,128]{2,1,0:T(2,128)(2,1)S(1)}, u32[]{:S(2)}, u32[]{:S(2)}) collective-permute-start(bf16[384,2,128]{2,1,0:T(2,128)(2,1)} %squeeze.66), channel_id=1, source_target_pairs={{0,24},{8,32},{16,40},{24,48},{32,56},{40,64},{48,72},{56,80},{64,... | collective-permute-start | bytes 589832 | tf_op jit(solution)/shard_map/ppermute | solution.py:16
  145.9 7.3 %collective-permute-start.14 = (bf16[2,384,2,128]{3,2,1,0:T(2,128)(2,1)S(1)}, bf16[2,384,2,128]{3,2,1,0:T(2,128)(2,1)S(1)}, u32[]{:S(2)}, u32[]{:S(2)}) collective-permute-start(bf16[2,384,2,128]{3,2,1,0:T(2,128)(2,1)S(1)} %reshape.110), channel_id=1, source_target_pairs={{8,0},{16,8},{24,16},{32,24},{40,32},{48,40},{56,48},{64,56},{72,6... | collective-permute-start | bytes 1179656 | tf_op jit(solution)/shard_map/ppermute | solution.py:16
  156.4 6.9 %collective-permute-start = (bf16[384,2,128]{2,1,0:T(2,128)(2,1)}, bf16[384,2,128]{2,1,0:T(2,128)(2,1)S(1)}, u32[]{:S(2)}, u32[]{:S(2)}) collective-permute-start(bf16[384,2,128]{2,1,0:T(2,128)(2,1)} %squeeze.64), channel_id=1, source_target_pairs={{0,40},{8,48},{16,56},{24,64},{32,72},{40,80},{48,88},{56,96},{64,... | collective-permute-start | bytes 589832 | tf_op jit(solution)/shard_map/ppermute | solution.py:16
  166.5 3.4 collective-permute-start.1
  169.8 16.4 %collective-permute-done.15 = bf16[384,2,128]{2,1,0:T(2,128)(2,1)S(1)} collective-permute-done((bf16[384,2,128]{2,1,0:T(2,128)(2,1)}, bf16[384,2,128]{2,1,0:T(2,128)(2,1)S(1)}, u32[]{:S(2)}, u32[]{:S(2)}) %collective-permute-start.15) | collective-permute-done | bytes 196640 | tf_op jit(solution)/shard_map/ppermute | solution.py:16
  188.2 15.5 %collective-permute-start.6 = (bf16[2,384,2,128]{3,2,1,0:T(2,128)(2,1)S(1)}, bf16[2,384,2,128]{3,2,1,0:T(2,128)(2,1)S(1)}, u32[]{:S(2)}, u32[]{:S(2)}) collective-permute-start(bf16[2,384,2,128]{3,2,1,0:T(2,128)(2,1)S(1)} %reshape.106), channel_id=1, source_target_pairs={{8,0},{16,8},{24,16},{32,24},{40,32},{48,40},{56,48},{64,56},{72,6... | collective-permute-start | bytes 1179656 | tf_op jit(solution)/shard_map/ppermute | solution.py:16
  204.9 4.0 pad_maximum_fusion.1
  208.9 3.0 slice_bitcast_fusion.5
  211.9 5.0 maximum_bitcast_fusion.1
  216.9 2.6 copy.65
  223.1 14.4 %collective-permute-done.7 = bf16[384,2,128]{2,1,0:T(2,128)(2,1)S(1)} collective-permute-done((bf16[384,2,128]{2,1,0:T(2,128)(2,1)S(1)}, bf16[384,2,128]{2,1,0:T(2,128)(2,1)S(1)}, u32[]{:S(2)}, u32[]{:S(2)}) %collective-permute-start.7) | collective-permute-done | bytes 196640 | tf_op jit(solution)/shard_map/ppermute | solution.py:16
  238.7 4.0 pad_maximum_fusion
  242.7 3.0 slice_bitcast_fusion.7
  245.8 5.0 maximum_bitcast_fusion
  251.6 56.6 %while.14 = (s32[]{:T(128)}, bf16[4,384,128]{2,1,0:T(8,128)(2,1)}, f32[4,9,384,128]{3,2,1,0:T(8,128)}, f32[4,9,384,128]{3,2,1,0:T(8,128)}, pred[4,9]{1,0:T(4,128...) while((s32[]{:T(128)}, bf16[4,384,128]{2,1,0:T(8,128)(2,1)}, ...), condition=%wide.region_4.5_spmd, body=%wide.region_0.4_spmd.sunk | while | flops 1728380160 | bytes 53502120 | solution.py:170
  254.8 2.6 fusion.98
  258.8 3.0 bitcast_dynamic-update-slice_fusion.4
  261.8 2.5 bitcast_dynamic-update-slice_fusion.5
  268.9 2.6 fusion.98
  272.9 3.0 bitcast_dynamic-update-slice_fusion.4
  275.9 2.4 bitcast_dynamic-update-slice_fusion.5
  282.9 2.6 fusion.98
  286.9 3.0 bitcast_dynamic-update-slice_fusion.4
  289.9 2.5 bitcast_dynamic-update-slice_fusion.5
  297.0 2.6 fusion.98
  301.0 3.0 bitcast_dynamic-update-slice_fusion.4
  308.2 11.4 %copy.92 = f32[2,2,3,3,384,128]{5,1,4,2,3,0:T(2,128)} copy(f32[2,2,3,3,384,128]{5,4,3,2,1,0:T(8,128)} %bitcast.360) | data formatting | bytes 14155776 | tf_op jit(solution)/shard_map/reshape | solution.py:70
  319.5 3.5 slice_bitcast_fusion.1
  323.1 2.5 fusion.41
  330.4 3.9 collective-permute-start.25
  342.1 11.4 %copy.93 = f32[2,2,3,3,384,128]{5,1,4,2,3,0:T(2,128)} copy(f32[2,2,3,3,384,128]{5,4,3,2,1,0:T(8,128)} %bitcast.359) | data formatting | bytes 14155776 | tf_op jit(solution)/shard_map/reshape | solution.py:70
  353.5 5.4 %slice_bitcast_fusion.3 = (f32[3,3,384,2,128]{4,3,2,1,0:T(2,128)S(1)}, f32[3,3,384,2,128]{4,3,2,1,0:T(2,128)}) fusion(f32[2,3,3,384,2,128]{5,4,3,2,1,0:T(2,128)} %bitcast.357), kind=kLoop, calls=%fused_computation.54 | loop fusion | bytes 14155776 | tf_op jit(solution)/shard_map/squeeze | solution.py:72
  363.0 4.6 all-to-all-start.4
  367.6 7.1 %collective-permute-start.29 = (bf16[384,2,128]{2,1,0:T(2,128)(2,1)}, bf16[384,2,128]{2,1,0:T(2,128)(2,1)S(1)}, u32[]{:S(2)}, u32[]{:S(2)}) collective-permute-start(bf16[384,2,128]{2,1,0:T(2,128)(2,1)} %get-tuple-element.99), channel_id=1, source_target_pairs={{40,0},{48,8},{56,16},{64,24},{72,32},{80,40},{88,48},{96,56},{104... | collective-permute-start | bytes 589832 | tf_op jit(solution)/shard_map/ppermute | solution.py:16
  374.7 8.7 %collective-permute-start.30 = (bf16[384,2,128]{2,1,0:T(2,128)(2,1)}, bf16[384,2,128]{2,1,0:T(2,128)(2,1)S(1)}, u32[]{:S(2)}, u32[]{:S(2)}) collective-permute-start(bf16[384,2,128]{2,1,0:T(2,128)(2,1)} %get-tuple-element.98), channel_id=1, source_target_pairs={{32,0},{40,8},{48,16},{56,24},{64,32},{72,40},{80,48},{88,56},{96,... | collective-permute-start | bytes 589832 | tf_op jit(solution)/shard_map/ppermute | solution.py:16
  383.5 5.2 %add_convert_fusion.1 = bf16[3,4,384,2,128]{4,3,2,1,0:T(2,128)(2,1)S(1)} fusion(f32[3,3,384,2,128]{4,3,2,1,0:T(2,128)} %get-tuple-element.95, f32[3,3,384,2,128]{4,3,2,1,0:T(2,128)S(1)} %get-tuple-element.94), kind=kLoop, calls=%fused_computation.50 | loop fusion | flops 2359296 | bytes 9437184 | tf_op jit(solution)/shard_map/convert.19
  390.7 7.6 %collective-permute-start.31 = (bf16[384,2,128]{2,1,0:T(2,128)(2,1)S(1)}, bf16[384,2,128]{2,1,0:T(2,128)(2,1)S(1)}, u32[]{:S(2)}, u32[]{:S(2)}) collective-permute-start(bf16[384,2,128]{2,1,0:T(2,128)(2,1)S(1)} %copy-done.9), channel_id=1, source_target_pairs={{24,0},{32,8},{40,16},{48,24},{56,32},{64,40},{72,48},{80,56},{88,... | collective-permute-start | bytes 589832 | tf_op jit(solution)/shard_map/ppermute | solution.py:16
  400.7 3.5 collective-permute-start.17
  405.7 5.8 %collective-permute-done.31 = bf16[384,2,128]{2,1,0:T(2,128)(2,1)S(1)} collective-permute-done((bf16[384,2,128]{2,1,0:T(2,128)(2,1)S(1)}, bf16[384,2,128]{2,1,0:T(2,128)(2,1)S(1)}, u32[]{:S(2)}, u32[]{:S(2)}) %collective-permute-start.31) | collective-permute-done | bytes 196640 | tf_op jit(solution)/shard_map/ppermute | solution.py:16
  417.6 2.9 fusion.73
  420.5 17.0 %collective-permute-done.18 = bf16[384,2,128]{2,1,0:T(2,128)(2,1)S(1)} collective-permute-done((bf16[384,2,128]{2,1,0:T(2,128)(2,1)S(1)}, bf16[384,2,128]{2,1,0:T(2,128)(2,1)S(1)}, u32[]{:S(2)}, u32[]{:S(2)}) %collective-permute-start.18) | collective-permute-done | bytes 196640 | tf_op jit(solution)/shard_map/ppermute | solution.py:16
  437.5 8.9 %collective-permute-start.21 = (bf16[384,2,128]{2,1,0:T(2,128)(2,1)}, bf16[384,2,128]{2,1,0:T(2,128)(2,1)}, u32[]{:S(2)}, u32[]{:S(2)}) collective-permute-start(bf16[384,2,128]{2,1,0:T(2,128)(2,1)} %get-tuple-element.105), channel_id=1, source_target_pairs={{40,0},{48,8},{56,16},{64,24},{72,32},{80,40},{88,48},{96,56},{104... | collective-permute-start | bytes 589832 | tf_op jit(solution)/shard_map/ppermute | solution.py:16
  446.5 3.0 collective-permute-done.19
  449.5 7.3 %collective-permute-start.22 = (bf16[384,2,128]{2,1,0:T(2,128)(2,1)}, bf16[384,2,128]{2,1,0:T(2,128)(2,1)}, u32[]{:S(2)}, u32[]{:S(2)}) collective-permute-start(bf16[384,2,128]{2,1,0:T(2,128)(2,1)} %get-tuple-element.104), channel_id=1, source_target_pairs={{32,0},{40,8},{48,16},{56,24},{64,32},{72,40},{80,48},{88,56},{96,... | collective-permute-start | bytes 589832 | tf_op jit(solution)/shard_map/ppermute | solution.py:16
  456.8 15.0 %collective-permute-start.23 = (bf16[384,2,128]{2,1,0:T(2,128)(2,1)}, bf16[384,2,128]{2,1,0:T(2,128)(2,1)}, u32[]{:S(2)}, u32[]{:S(2)}) collective-permute-start(bf16[384,2,128]{2,1,0:T(2,128)(2,1)} %get-tuple-element.103), channel_id=1, source_target_pairs={{24,0},{32,8},{40,16},{48,24},{56,32},{64,40},{72,48},{80,56},{88,... | collective-permute-start | bytes 589832 | tf_op jit(solution)/shard_map/ppermute | solution.py:16
  475.2 5.9 %all-to-all-start.6 = ((bf16[8,96,256]{2,1,0:T(8,128)(2,1)}), bf16[8,96,256]{2,1,0:T(8,128)(2,1)}, u32[]{:S(2)}, u32[]{:S(2)}) async-start(bf16[8,96,256]{2,1,0:T(8,128)(2,1)} %convert_element_type.148), calls=%async_computation.6 | async-start | bytes 786432 | tf_op jit(solution)/shard_map/all_to_all | solution.py:204
  482.2 2.8 fusion.75
  486.6 8.0 %all-to-all-done.6 = bf16[8,96,256]{2,1,0:T(8,128)(2,1)} async-done(((bf16[8,96,256]{2,1,0:T(8,128)(2,1)}), bf16[8,96,256]{2,1,0:T(8,128)(2,1)}, u32[]{:S(2)}, u32[]{:S(2)}) %all-to-all-start.6) | async-done | bytes 393248 | tf_op jit(solution)/shard_map/all_to_all | solution.py:204
  494.6 3.5 all-to-all-start.5
  501.6 9.8 %all-to-all-done.5 = bf16[8,96,256]{2,1,0:T(8,128)(2,1)S(1)} async-done(((bf16[8,96,256]{2,1,0:T(8,128)(2,1)}), bf16[8,96,256]{2,1,0:T(8,128)(2,1)S(1)}, u32[]{:S(2)}, u32[]{:S(2)}) %all-to-all-start.5) | async-done | bytes 393248 | tf_op jit(solution)/shard_map/all_to_all | solution.py:203
  (152 shorter events, 96.3 us)
Async XLA Ops:
  0.6 45.4 %copy-start = (s32[16,2]{0,1:T(2,128)S(1)}, s32[16,2]{0,1:T(2,128)}, u32[]{:S(2)}) copy-start(s32[16,2]{0,1:T(2,128)} %param.11) | copy-start | bytes 388
  0.6 45.7 %copy-start.8 = (bf16[96,2048]{1,0:T(8,128)(2,1)S(1)}, bf16[96,2048]{1,0:T(8,128)(2,1)}, u32[]{:S(2)}) copy-start(bf16[96,2048]{1,0:T(8,128)(2,1)} %param.10) | copy-start | bytes 1179652
  2.5 21.7 %all-to-all-start.2 = ((bf16[96,8,256]{2,0,1:T(8,128)(2,1)}), bf16[96,8,256]{2,0,1:T(8,128)(2,1)S(1)}, u32[]{:S(2)}, u32[]{:S(2)}) async-start(bf16[96,8,256]{2,0,1:T(8,128)(2,1)} %bitcast.313), calls=%async_computation.2 | async-start | bytes 786432 | tf_op jit(solution)/shard_map/all_to_all | solution.py:149
  24.1 18.4 %all-to-all-start = ((bf16[96,8,256]{2,0,1:T(8,128)(2,1)}), bf16[96,8,256]{2,0,1:T(8,128)(2,1)S(1)}, u32[]{:S(2)}, u32[]{:S(2)}) async-start(bf16[96,8,256]{2,0,1:T(8,128)(2,1)} %bitcast.315), calls=%async_computation | async-start | bytes 786432 | tf_op jit(solution)/shard_map/all_to_all | solution.py:148
  42.6 18.7 %all-to-all-start.1 = ((bf16[96,8,256]{2,0,1:T(8,128)(2,1)}), bf16[96,8,256]{2,0,1:T(8,128)(2,1)S(1)}, u32[]{:S(2)}, u32[]{:S(2)}) async-start(bf16[96,8,256]{2,0,1:T(8,128)(2,1)} %bitcast.314), calls=%async_computation.1 | async-start | bytes 786432 | tf_op jit(solution)/shard_map/all_to_all | solution.py:147
  61.3 34.1 %all-to-all-start.3 = ((bf16[96,8,256]{2,0,1:T(8,128)(2,1)}), bf16[96,8,256]{2,0,1:T(8,128)(2,1)S(1)}, u32[]{:S(2)}, u32[]{:S(2)}) async-start(bf16[96,8,256]{2,0,1:T(8,128)(2,1)} %bitcast.312), calls=%async_computation.3 | async-start | bytes 786432 | tf_op jit(solution)/shard_map/all_to_all | solution.py:150
  65.9 88.5 %collective-permute-start.8 = (bf16[384,2,128]{2,1,0:T(2,128)(2,1)}, bf16[384,2,128]{2,1,0:T(2,128)(2,1)S(1)}, u32[]{:S(2)}, u32[]{:S(2)}) collective-permute-start(bf16[384,2,128]{2,1,0:T(2,128)(2,1)} %squeeze.66), channel_id=1, source_target_pairs={{0,40},{8,48},{16,56},{24,64},{32,72},{40,80},{48,88},{56,96},{64,... | collective-permute-start | bytes 589832 | tf_op jit(solution)/shard_map/ppermute | solution.py:16
  76.9 19.4 %collective-permute-start.11 = (bf16[384,2,128]{2,1,0:T(2,128)(2,1)}, bf16[384,2,128]{2,1,0:T(2,128)(2,1)S(1)}, u32[]{:S(2)}, u32[]{:S(2)}) collective-permute-start(bf16[384,2,128]{2,1,0:T(2,128)(2,1)} %squeeze.66), channel_id=1, source_target_pairs={{0,32},{8,40},{16,48},{24,56},{32,64},{40,72},{48,80},{56,88},{64,... | collective-permute-start | bytes 589832 | tf_op jit(solution)/shard_map/ppermute | solution.py:16
  79.5 76.8 %collective-permute-start.10 = (bf16[384,2,128]{2,1,0:T(2,128)(2,1)}, bf16[384,2,128]{2,1,0:T(2,128)(2,1)S(1)}, u32[]{:S(2)}, u32[]{:S(2)}) collective-permute-start(bf16[384,2,128]{2,1,0:T(2,128)(2,1)} %squeeze.67), channel_id=1, source_target_pairs={{24,0},{32,8},{40,16},{48,24},{56,32},{64,40},{72,48},{80,56},{88,... | collective-permute-start | bytes 589832 | tf_op jit(solution)/shard_map/ppermute | solution.py:16
  88.3 20.2 %collective-permute-start.12 = (bf16[384,2,128]{2,1,0:T(2,128)(2,1)}, bf16[384,2,128]{2,1,0:T(2,128)(2,1)S(1)}, u32[]{:S(2)}, u32[]{:S(2)}) collective-permute-start(bf16[384,2,128]{2,1,0:T(2,128)(2,1)} %squeeze.67), channel_id=1, source_target_pairs={{32,0},{40,8},{48,16},{56,24},{64,32},{72,40},{80,48},{88,56},{96,... | collective-permute-start | bytes 589832 | tf_op jit(solution)/shard_map/ppermute | solution.py:16
  90.2 73.1 %collective-permute-start.9 = (bf16[2,384,2,128]{3,2,1,0:T(2,128)(2,1)S(1)}, bf16[2,384,2,128]{3,2,1,0:T(2,128)(2,1)S(1)}, u32[]{:S(2)}, u32[]{:S(2)}) collective-permute-start(bf16[2,384,2,128]{3,2,1,0:T(2,128)(2,1)S(1)} %reshape.110), channel_id=1, source_target_pairs={{0,8},{8,16},{16,24},{24,32},{32,40},{40,48},{48,56},{56,64},{64,7... | collective-permute-start | bytes 1179656 | tf_op jit(solution)/shard_map/ppermute | solution.py:16
  94.5 51.4 %copy-start.10 = (bf16[384,2,128]{2,1,0:T(2,128)(2,1)}, bf16[384,2,128]{2,1,0:T(2,128)(2,1)S(1)}, u32[]{:S(2)}) copy-start(bf16[384,2,128]{2,1,0:T(2,128)(2,1)S(1)} %squeeze.65) | copy-start | bytes 589828
  96.3 29.9 %collective-permute-start.3 = (bf16[384,2,128]{2,1,0:T(2,128)(2,1)}, bf16[384,2,128]{2,1,0:T(2,128)(2,1)S(1)}, u32[]{:S(2)}, u32[]{:S(2)}) collective-permute-start(bf16[384,2,128]{2,1,0:T(2,128)(2,1)} %squeeze.64), channel_id=1, source_target_pairs={{0,32},{8,40},{16,48},{24,56},{32,64},{40,72},{48,80},{56,88},{64,... | collective-permute-start | bytes 589832 | tf_op jit(solution)/shard_map/ppermute | solution.py:16
  108.4 37.5 %collective-permute-start.4 = (bf16[384,2,128]{2,1,0:T(2,128)(2,1)S(1)}, bf16[384,2,128]{2,1,0:T(2,128)(2,1)S(1)}, u32[]{:S(2)}, u32[]{:S(2)}) collective-permute-start(bf16[384,2,128]{2,1,0:T(2,128)(2,1)S(1)} %squeeze.65), channel_id=1, source_target_pairs={{32,0},{40,8},{48,16},{56,24},{64,32},{72,40},{80,48},{88,56},{96,... | collective-permute-start | bytes 589832 | tf_op jit(solution)/shard_map/ppermute | solution.py:16
  126.3 40.2 %collective-permute-start.13 = (bf16[384,2,128]{2,1,0:T(2,128)(2,1)}, bf16[384,2,128]{2,1,0:T(2,128)(2,1)S(1)}, u32[]{:S(2)}, u32[]{:S(2)}) collective-permute-start(bf16[384,2,128]{2,1,0:T(2,128)(2,1)} %squeeze.66), channel_id=1, source_target_pairs={{0,24},{8,32},{16,40},{24,48},{32,56},{40,64},{48,72},{56,80},{64,... | collective-permute-start | bytes 589832 | tf_op jit(solution)/shard_map/ppermute | solution.py:16
  145.9 42.3 %collective-permute-start.14 = (bf16[2,384,2,128]{3,2,1,0:T(2,128)(2,1)S(1)}, bf16[2,384,2,128]{3,2,1,0:T(2,128)(2,1)S(1)}, u32[]{:S(2)}, u32[]{:S(2)}) collective-permute-start(bf16[2,384,2,128]{3,2,1,0:T(2,128)(2,1)S(1)} %reshape.110), channel_id=1, source_target_pairs={{8,0},{16,8},{24,16},{32,24},{40,32},{48,40},{56,48},{64,56},{72,6... | collective-permute-start | bytes 1179656 | tf_op jit(solution)/shard_map/ppermute | solution.py:16
  154.4 31.8 %collective-permute-start.15 = (bf16[384,2,128]{2,1,0:T(2,128)(2,1)}, bf16[384,2,128]{2,1,0:T(2,128)(2,1)S(1)}, u32[]{:S(2)}, u32[]{:S(2)}) collective-permute-start(bf16[384,2,128]{2,1,0:T(2,128)(2,1)} %squeeze.67), channel_id=1, source_target_pairs={{40,0},{48,8},{56,16},{64,24},{72,32},{80,40},{88,48},{96,56},{104... | collective-permute-start | bytes 589832 | tf_op jit(solution)/shard_map/ppermute | solution.py:16
  156.4 63.2 %collective-permute-start = (bf16[384,2,128]{2,1,0:T(2,128)(2,1)}, bf16[384,2,128]{2,1,0:T(2,128)(2,1)S(1)}, u32[]{:S(2)}, u32[]{:S(2)}) collective-permute-start(bf16[384,2,128]{2,1,0:T(2,128)(2,1)} %squeeze.64), channel_id=1, source_target_pairs={{0,40},{8,48},{16,56},{24,64},{32,72},{40,80},{48,88},{56,96},{64,... | collective-permute-start | bytes 589832 | tf_op jit(solution)/shard_map/ppermute | solution.py:16
  163.3 58.6 %collective-permute-start.2 = (bf16[384,2,128]{2,1,0:T(2,128)(2,1)}, bf16[384,2,128]{2,1,0:T(2,128)(2,1)S(1)}, u32[]{:S(2)}, u32[]{:S(2)}) collective-permute-start(bf16[384,2,128]{2,1,0:T(2,128)(2,1)} %copy-done.10), channel_id=1, source_target_pairs={{24,0},{32,8},{40,16},{48,24},{56,32},{64,40},{72,48},{80,56},{88,... | collective-permute-start | bytes 589832 | tf_op jit(solution)/shard_map/ppermute | solution.py:16
  166.5 55.4 %collective-permute-start.1 = (bf16[2,384,2,128]{3,2,1,0:T(2,128)(2,1)S(1)}, bf16[2,384,2,128]{3,2,1,0:T(2,128)(2,1)S(1)}, u32[]{:S(2)}, u32[]{:S(2)}) collective-permute-start(bf16[2,384,2,128]{3,2,1,0:T(2,128)(2,1)S(1)} %reshape.106), channel_id=1, source_target_pairs={{0,8},{8,16},{16,24},{24,32},{32,40},{40,48},{48,56},{56,64},{64,7... | collective-permute-start | bytes 1179656 | tf_op jit(solution)/shard_map/ppermute | solution.py:16
  186.3 36.9 %collective-permute-start.5 = (bf16[384,2,128]{2,1,0:T(2,128)(2,1)}, bf16[384,2,128]{2,1,0:T(2,128)(2,1)S(1)}, u32[]{:S(2)}, u32[]{:S(2)}) collective-permute-start(bf16[384,2,128]{2,1,0:T(2,128)(2,1)} %squeeze.64), channel_id=1, source_target_pairs={{0,24},{8,32},{16,40},{24,48},{32,56},{40,64},{48,72},{56,80},{64,... | collective-permute-start | bytes 589832 | tf_op jit(solution)/shard_map/ppermute | solution.py:16
  188.2 49.3 %collective-permute-start.6 = (bf16[2,384,2,128]{3,2,1,0:T(2,128)(2,1)S(1)}, bf16[2,384,2,128]{3,2,1,0:T(2,128)(2,1)S(1)}, u32[]{:S(2)}, u32[]{:S(2)}) collective-permute-start(bf16[2,384,2,128]{3,2,1,0:T(2,128)(2,1)S(1)} %reshape.106), channel_id=1, source_target_pairs={{8,0},{16,8},{24,16},{32,24},{40,32},{48,40},{56,48},{64,56},{72,6... | collective-permute-start | bytes 1179656 | tf_op jit(solution)/shard_map/ppermute | solution.py:16
  216.9 2.6 copy-start.11
  219.6 17.9 %collective-permute-start.7 = (bf16[384,2,128]{2,1,0:T(2,128)(2,1)S(1)}, bf16[384,2,128]{2,1,0:T(2,128)(2,1)S(1)}, u32[]{:S(2)}, u32[]{:S(2)}) collective-permute-start(bf16[384,2,128]{2,1,0:T(2,128)(2,1)S(1)} %copy-done.11), channel_id=1, source_target_pairs={{40,0},{48,8},{56,16},{64,24},{72,32},{80,40},{88,48},{96,56},{104... | collective-permute-start | bytes 589832 | tf_op jit(solution)/shard_map/ppermute | solution.py:16
  253.6 1.2 copy-start.7
  267.7 1.2 copy-start.7
  281.7 1.2 copy-start.7
  295.8 1.2 copy-start.7
  323.1 2.6 copy-start.3
  323.1 3.3 copy-start.5
  328.5 84.9 %collective-permute-start.24 = (f32[2,384,2,128]{3,2,1,0:T(2,128)}, f32[2,384,2,128]{3,2,1,0:T(2,128)}, u32[]{:S(2)}, u32[]{:S(2)}) collective-permute-start(f32[2,384,2,128]{3,2,1,0:T(2,128)} %get-tuple-element.88), channel_id=1, source_target_pairs={{8,0},{16,8},{24,16},{32,24},{40,32},{48,40},{56,48},{64,56},{72,6... | collective-permute-start | bytes 2359304 | tf_op jit(solution)/shard_map/ppermute | solution.py:16
  330.4 84.9 %collective-permute-start.25 = (f32[2,384,2,128]{3,2,1,0:T(2,128)}, f32[2,384,2,128]{3,2,1,0:T(2,128)}, u32[]{:S(2)}, u32[]{:S(2)}) collective-permute-start(f32[2,384,2,128]{3,2,1,0:T(2,128)} %get-tuple-element.89), channel_id=1, source_target_pairs={{0,8},{8,16},{16,24},{24,32},{32,40},{40,48},{48,56},{56,64},{64,7... | collective-permute-start | bytes 2359304 | tf_op jit(solution)/shard_map/ppermute | solution.py:16
  336.0 31.6 %collective-permute-start.26 = (bf16[384,2,128]{2,1,0:T(2,128)(2,1)}, bf16[384,2,128]{2,1,0:T(2,128)(2,1)}, u32[]{:S(2)}, u32[]{:S(2)}) collective-permute-start(bf16[384,2,128]{2,1,0:T(2,128)(2,1)} %get-tuple-element.96), channel_id=1, source_target_pairs={{0,24},{8,32},{16,40},{24,48},{32,56},{40,64},{48,72},{56,80},{64,... | collective-permute-start | bytes 589832 | tf_op jit(solution)/shard_map/ppermute | solution.py:16
  337.9 36.8 %collective-permute-start.27 = (bf16[384,2,128]{2,1,0:T(2,128)(2,1)}, bf16[384,2,128]{2,1,0:T(2,128)(2,1)}, u32[]{:S(2)}, u32[]{:S(2)}) collective-permute-start(bf16[384,2,128]{2,1,0:T(2,128)(2,1)} %get-tuple-element.101), channel_id=1, source_target_pairs={{0,32},{8,40},{16,48},{24,56},{32,64},{40,72},{48,80},{56,88},{64,... | collective-permute-start | bytes 589832 | tf_op jit(solution)/shard_map/ppermute | solution.py:16
  339.9 50.8 %collective-permute-start.28 = (bf16[384,2,128]{2,1,0:T(2,128)(2,1)}, bf16[384,2,128]{2,1,0:T(2,128)(2,1)}, u32[]{:S(2)}, u32[]{:S(2)}) collective-permute-start(bf16[384,2,128]{2,1,0:T(2,128)(2,1)} %get-tuple-element.100), channel_id=1, source_target_pairs={{0,40},{8,48},{16,56},{24,64},{32,72},{40,80},{48,88},{56,96},{64,... | collective-permute-start | bytes 589832 | tf_op jit(solution)/shard_map/ppermute | solution.py:16
  363.0 112.1 %all-to-all-start.4 = ((bf16[8,96,256]{2,1,0:T(8,128)(2,1)}), bf16[8,96,256]{2,1,0:T(8,128)(2,1)}, u32[]{:S(2)}, u32[]{:S(2)}) async-start(bf16[8,96,256]{2,1,0:T(8,128)(2,1)} %convert_element_type.122), calls=%async_computation.4 | async-start | bytes 786432 | tf_op jit(solution)/shard_map/all_to_all | solution.py:202
  367.6 30.7 %collective-permute-start.29 = (bf16[384,2,128]{2,1,0:T(2,128)(2,1)}, bf16[384,2,128]{2,1,0:T(2,128)(2,1)S(1)}, u32[]{:S(2)}, u32[]{:S(2)}) collective-permute-start(bf16[384,2,128]{2,1,0:T(2,128)(2,1)} %get-tuple-element.99), channel_id=1, source_target_pairs={{40,0},{48,8},{56,16},{64,24},{72,32},{80,40},{88,48},{96,56},{104... | collective-permute-start | bytes 589832 | tf_op jit(solution)/shard_map/ppermute | solution.py:16
  374.7 26.0 %collective-permute-start.30 = (bf16[384,2,128]{2,1,0:T(2,128)(2,1)}, bf16[384,2,128]{2,1,0:T(2,128)(2,1)S(1)}, u32[]{:S(2)}, u32[]{:S(2)}) collective-permute-start(bf16[384,2,128]{2,1,0:T(2,128)(2,1)} %get-tuple-element.98), channel_id=1, source_target_pairs={{32,0},{40,8},{48,16},{56,24},{64,32},{72,40},{80,48},{88,56},{96,... | collective-permute-start | bytes 589832 | tf_op jit(solution)/shard_map/ppermute | solution.py:16
  383.5 5.2 %copy-start.2 = (f32[3,3,384,2,128]{4,3,2,1,0:T(2,128)S(1)}, f32[3,3,384,2,128]{4,3,2,1,0:T(2,128)}, u32[]{:S(2)}) copy-start(f32[3,3,384,2,128]{4,3,2,1,0:T(2,128)} %get-tuple-element.95) | copy-start | bytes 10616836
  388.7 2.0 copy-start.9
  388.7 28.9 %copy-start.4 = (f32[3,3,384,2,128]{4,3,2,1,0:T(2,128)S(1)}, f32[3,3,384,2,128]{4,3,2,1,0:T(2,128)}, u32[]{:S(2)}) copy-start(f32[3,3,384,2,128]{4,3,2,1,0:T(2,128)} %copy-done.3) | copy-start | bytes 10616836
  388.7 28.9 %copy-start.6 = (f32[3,3,384,2,128]{4,3,2,1,0:T(2,128)S(1)}, f32[3,3,384,2,128]{4,3,2,1,0:T(2,128)}, u32[]{:S(2)}) copy-start(f32[3,3,384,2,128]{4,3,2,1,0:T(2,128)} %copy-done.5) | copy-start | bytes 10616836
  390.7 20.8 %collective-permute-start.31 = (bf16[384,2,128]{2,1,0:T(2,128)(2,1)S(1)}, bf16[384,2,128]{2,1,0:T(2,128)(2,1)S(1)}, u32[]{:S(2)}, u32[]{:S(2)}) collective-permute-start(bf16[384,2,128]{2,1,0:T(2,128)(2,1)S(1)} %copy-done.9), channel_id=1, source_target_pairs={{24,0},{32,8},{40,16},{48,24},{56,32},{64,40},{72,48},{80,56},{88,... | collective-permute-start | bytes 589832 | tf_op jit(solution)/shard_map/ppermute | solution.py:16
  398.3 83.9 %collective-permute-start.16 = (f32[2,384,2,128]{3,2,1,0:T(2,128)}, f32[2,384,2,128]{3,2,1,0:T(2,128)}, u32[]{:S(2)}, u32[]{:S(2)}) collective-permute-start(f32[2,384,2,128]{3,2,1,0:T(2,128)} %get-tuple-element.92), channel_id=1, source_target_pairs={{8,0},{16,8},{24,16},{32,24},{40,32},{48,40},{56,48},{64,56},{72,6... | collective-permute-start | bytes 2359304 | tf_op jit(solution)/shard_map/ppermute | solution.py:16
  400.7 81.5 %collective-permute-start.17 = (f32[2,384,2,128]{3,2,1,0:T(2,128)}, f32[2,384,2,128]{3,2,1,0:T(2,128)}, u32[]{:S(2)}, u32[]{:S(2)}) collective-permute-start(f32[2,384,2,128]{3,2,1,0:T(2,128)} %get-tuple-element.93), channel_id=1, source_target_pairs={{0,8},{8,16},{16,24},{24,32},{32,40},{40,48},{48,56},{56,64},{64,7... | collective-permute-start | bytes 2359304 | tf_op jit(solution)/shard_map/ppermute | solution.py:16
  411.5 26.0 %collective-permute-start.18 = (bf16[384,2,128]{2,1,0:T(2,128)(2,1)S(1)}, bf16[384,2,128]{2,1,0:T(2,128)(2,1)S(1)}, u32[]{:S(2)}, u32[]{:S(2)}) collective-permute-start(bf16[384,2,128]{2,1,0:T(2,128)(2,1)S(1)} %get-tuple-element.102), channel_id=1, source_target_pairs={{0,24},{8,32},{16,40},{24,48},{32,56},{40,64},{48,72},{56,80},{64,... | collective-permute-start | bytes 589832 | tf_op jit(solution)/shard_map/ppermute | solution.py:16
  413.4 36.0 %collective-permute-start.19 = (bf16[384,2,128]{2,1,0:T(2,128)(2,1)S(1)}, bf16[384,2,128]{2,1,0:T(2,128)(2,1)S(1)}, u32[]{:S(2)}, u32[]{:S(2)}) collective-permute-start(bf16[384,2,128]{2,1,0:T(2,128)(2,1)S(1)} %get-tuple-element.107), channel_id=1, source_target_pairs={{0,32},{8,40},{16,48},{24,56},{32,64},{40,72},{48,80},{56,88},{64,... | collective-permute-start | bytes 589832 | tf_op jit(solution)/shard_map/ppermute | solution.py:16
  415.4 41.4 %collective-permute-start.20 = (bf16[384,2,128]{2,1,0:T(2,128)(2,1)S(1)}, bf16[384,2,128]{2,1,0:T(2,128)(2,1)S(1)}, u32[]{:S(2)}, u32[]{:S(2)}) collective-permute-start(bf16[384,2,128]{2,1,0:T(2,128)(2,1)S(1)} %get-tuple-element.106), channel_id=1, source_target_pairs={{0,40},{8,48},{16,56},{24,64},{32,72},{40,80},{48,88},{56,96},{64,... | collective-permute-start | bytes 589832 | tf_op jit(solution)/shard_map/ppermute | solution.py:16
  437.5 19.3 %copy-start.12 = (bf16[384,2,128]{2,1,0:T(2,128)(2,1)}, bf16[384,2,128]{2,1,0:T(2,128)(2,1)S(1)}, u32[]{:S(2)}) copy-start(bf16[384,2,128]{2,1,0:T(2,128)(2,1)S(1)} %collective-permute-done.18) | copy-start | bytes 589828
  437.5 43.5 %collective-permute-start.21 = (bf16[384,2,128]{2,1,0:T(2,128)(2,1)}, bf16[384,2,128]{2,1,0:T(2,128)(2,1)}, u32[]{:S(2)}, u32[]{:S(2)}) collective-permute-start(bf16[384,2,128]{2,1,0:T(2,128)(2,1)} %get-tuple-element.105), channel_id=1, source_target_pairs={{40,0},{48,8},{56,16},{64,24},{72,32},{80,40},{88,48},{96,56},{104... | collective-permute-start | bytes 589832 | tf_op jit(solution)/shard_map/ppermute | solution.py:16
  449.5 7.3 %copy-start.13 = (bf16[384,2,128]{2,1,0:T(2,128)(2,1)}, bf16[384,2,128]{2,1,0:T(2,128)(2,1)S(1)}, u32[]{:S(2)}) copy-start(bf16[384,2,128]{2,1,0:T(2,128)(2,1)S(1)} %collective-permute-done.19) | copy-start | bytes 589828
  449.5 31.6 %collective-permute-start.22 = (bf16[384,2,128]{2,1,0:T(2,128)(2,1)}, bf16[384,2,128]{2,1,0:T(2,128)(2,1)}, u32[]{:S(2)}, u32[]{:S(2)}) collective-permute-start(bf16[384,2,128]{2,1,0:T(2,128)(2,1)} %get-tuple-element.104), channel_id=1, source_target_pairs={{32,0},{40,8},{48,16},{56,24},{64,32},{72,40},{80,48},{88,56},{96,... | collective-permute-start | bytes 589832 | tf_op jit(solution)/shard_map/ppermute | solution.py:16
  456.8 15.0 %copy-start.14 = (bf16[384,2,128]{2,1,0:T(2,128)(2,1)}, bf16[384,2,128]{2,1,0:T(2,128)(2,1)S(1)}, u32[]{:S(2)}) copy-start(bf16[384,2,128]{2,1,0:T(2,128)(2,1)S(1)} %collective-permute-done.20) | copy-start | bytes 589828
  456.8 25.4 %collective-permute-start.23 = (bf16[384,2,128]{2,1,0:T(2,128)(2,1)}, bf16[384,2,128]{2,1,0:T(2,128)(2,1)}, u32[]{:S(2)}, u32[]{:S(2)}) collective-permute-start(bf16[384,2,128]{2,1,0:T(2,128)(2,1)} %get-tuple-element.103), channel_id=1, source_target_pairs={{24,0},{32,8},{40,16},{48,24},{56,32},{64,40},{72,48},{80,56},{88,... | collective-permute-start | bytes 589832 | tf_op jit(solution)/shard_map/ppermute | solution.py:16
  475.2 19.5 %all-to-all-start.6 = ((bf16[8,96,256]{2,1,0:T(8,128)(2,1)}), bf16[8,96,256]{2,1,0:T(8,128)(2,1)}, u32[]{:S(2)}, u32[]{:S(2)}) async-start(bf16[8,96,256]{2,1,0:T(8,128)(2,1)} %convert_element_type.148), calls=%async_computation.6 | async-start | bytes 786432 | tf_op jit(solution)/shard_map/all_to_all | solution.py:204
  482.2 30.0 %copy-start.1 = (s32[16,2]{0,1:T(2,128)S(1)}, s32[16,2]{0,1:T(2,128)}, u32[]{:S(2)}) copy-start(s32[16,2]{0,1:T(2,128)} %param.11) | copy-start | bytes 388
  494.6 16.8 %all-to-all-start.5 = ((bf16[8,96,256]{2,1,0:T(8,128)(2,1)}), bf16[8,96,256]{2,1,0:T(8,128)(2,1)S(1)}, u32[]{:S(2)}, u32[]{:S(2)}) async-start(bf16[8,96,256]{2,1,0:T(8,128)(2,1)} %convert_element_type.135), calls=%async_computation.5 | async-start | bytes 786432 | tf_op jit(solution)/shard_map/all_to_all | solution.py:203
where the time goes:
time: 520 us; the launch traced here: 513 us
  starting transfers between devices  207 us (40%)
  waiting for transfers between devices  135 us (26%)
  local copies, waits for them, and re-layouts  67.7 us (13%)
  other arithmetic  55.2 us (11%)
  matrix products  45.4 us (9%)
    ppermute x32, starting transfers between devices, passed_along(): return lax.ppermute(block, axis, route)  176 us
    ppermute x32, waiting for transfers between devices, passed_along(): return lax.ppermute(block, axis, route)  76.6 us
    reshape x2, local copies, waits for them, and re-layouts, terms_to_columns(): shaped = terms.reshape(2, heads_here, 3, 3, terms.shape[2], terms.shape[3])  22.8 us
    another operation x8, other arithmetic, neighbour_columns(): jnp.stack([column[member_num] for column in columns])  15.2 us
    all_to_all x1, waiting for transfers between devices, per_device(): lax.all_to_all(queries, 'head', split_axis=1, concat_axis=0, tiled=True)  14.2 us
    all_to_all x1, waiting for transfers between devices, per_device(): lax.all_to_all(values, 'head', split_axis=1, concat_axis=0, tiled=True)  13.7 us
    all_to_all x1, waiting for transfers between devices, per_device(): lax.all_to_all(keys, 'head', split_axis=1, concat_axis=0, tiled=True)  13.2 us
    dot_general x4, matrix products, query_with_terms(): jnp.einsum('oqk,qd->okd', dscore, query_head, preferred_element_type=jnp....  11.9 us
  transfers between devices with their start and end apart: 39, of which 14 were waited for; matrix products, arithmetic and copies ran while one was open for 15% of the time, Pallas kernels for 0%

commit v1 on v0

v1 whole, which is shorter than its diff:
```python
import functools

import jax
import jax.numpy as jnp
from jax import lax
from jax.experimental import pallas as pl
from jax.experimental.pallas import tpu as pltpu
from jax.sharding import Mesh, PartitionSpec as P

HD = 128
HEADS = 16
PIECE = 96
HALF = 192
TILE = 384
BF = jnp.bfloat16
F32 = jnp.float32
AXES = ("yl", "x", "zh", "zm", "zl", "yhh", "yhl", "c")
SIZES = (2, 4, 2, 2, 2, 2, 2, 2)
GROUP = ("zh", "yhh", "zl", "yhl")
Z = ("zh", "zm", "zl")
Z_PAIRS = [(1, 2), (2, 1), (5, 6), (6, 5), (0, 7), (7, 0), (4, 3), (3, 4)]
LINE = ("yl", "x")
FORTH = [(i, i + 1) for i in range(7)]
BACK = [(i + 1, i) for i in range(7)]
SWAP = [(0, 1), (1, 0)]
NEG = float("-inf")


def head_of(chip, zm):
    zh, yhh, zl, yhl = (chip // 8) % 2, (chip // 4) % 2, (chip // 2) % 2, chip % 2
    return ((zh * 2 + zl + zm) % 4) * 4 + yhh * 2 + yhl


def spread_kernel(zm_ref, a_ref, b_ref, out_ref):
    zm = zm_ref[0]
    for chip in range(HEADS):
        columns = pl.ds(pl.multiple_of(head_of(chip, zm) * HD, HD), HD)
        out_ref[chip, 0] = a_ref[:, columns]
        out_ref[chip, 1] = b_ref[:, columns]


def spread(zm, a, b):
    return pl.pallas_call(
        spread_kernel,
        out_shape=jax.ShapeDtypeStruct((HEADS, 2, PIECE, HD), BF),
        in_specs=[pl.BlockSpec(memory_space=pltpu.SMEM)] + [pl.BlockSpec(memory_space=pltpu.VMEM)] * 2,
        out_specs=pl.BlockSpec(memory_space=pltpu.VMEM),
        cost_estimate=pl.CostEstimate(flops=0, bytes_accessed=4 * 393216, transcendentals=0),
    )(zm, a, b)


def gather_kernel(count, zm_ref, in_ref, *out_refs):
    zm = zm_ref[0]
    for chip in range(HEADS):
        columns = pl.ds(pl.multiple_of(head_of(chip, zm) * HD, HD), HD)
        for n in range(count):
            out_refs[n][:, columns] = in_ref[chip, n]


def gather(zm, blocks):
    count = blocks.shape[1]
    return pl.pallas_call(
        functools.partial(gather_kernel, count),
        out_shape=[jax.ShapeDtypeStruct((PIECE, HEADS * HD), BF)] * count,
        in_specs=[pl.BlockSpec(memory_space=pltpu.SMEM), pl.BlockSpec(memory_space=pltpu.VMEM)],
        out_specs=[pl.BlockSpec(memory_space=pltpu.VMEM)] * count,
        cost_estimate=pl.CostEstimate(flops=0, bytes_accessed=2 * count * 393216, transcendentals=0),
    )(zm, blocks)


def dot(a, b, dims):
    return lax.dot_general(a, b, (dims, ((), ())), preferred_element_type=F32)


def attention_kernel(
    info, own, own_s, side, side_s, prev, prev_s, nxt, nxt_s, qg,
    dq_out, mine_out, sib_out,
    k_buf, v_buf, q_buf, g_buf, dk_acc, dv_acc, s_main, s_side, p_main, p_side, sems,
):
    zm, reach_t, reach_h = info[0], info[1], info[2]
    first_col, last_col = info[3], info[4]

    copies = []

    def copy(src, dst):
        c = pltpu.make_async_copy(src, dst, sems.at[len(copies)])
        c.start()
        copies.append(c)

    for zl in (0, 1):
        row = lax.rem(zm + zl, 2)
        copy(qg.at[:, zl, :, 0], q_buf.at[:, row])
        copy(qg.at[:, zl, :, 1], g_buf.at[:, row])
    for kv, buf in ((0, k_buf), (1, v_buf)):
        for core, (o, h, p, n) in enumerate(((own, side, prev, nxt), (own_s, side_s, prev_s, nxt_s))):
            for zl in (0, 1):
                row = lax.rem(zm + zl, 2)
                copy(o.at[:, zl, :, kv], buf.at[pl.ds(1, 4), row, core])
                copy(p.at[zl, :, kv], buf.at[0, row, core])
                copy(n.at[zl, :, kv], buf.at[5, row, core])
            copy(h.at[:, :, kv], buf.at[pl.ds(1, 4), 2, core])
            copy(p.at[2, :, kv], buf.at[0, 2, core])
            copy(n.at[2, :, kv], buf.at[5, 2, core])
    dk_acc[...] = jnp.zeros_like(dk_acc)
    dv_acc[...] = jnp.zeros_like(dv_acc)
    for c in copies:
        c.wait()

    scale2 = HD ** (-0.5) * 1.4426950408889634
    row_bias = jnp.where(reach_h >= 1, 0.0, NEG).astype(F32)
    block_row = lax.broadcasted_iota(jnp.int32, (TILE, 2 * TILE), 0) >= HALF
    block_col = lax.broadcasted_iota(jnp.int32, (TILE, 2 * TILE), 1) >= TILE
    main_bias = jnp.where(block_row == block_col, 0.0, row_bias)

    def keys(buf, col):
        return buf[col, 0:2].reshape(2 * TILE, HD), buf[col, 2].reshape(TILE, HD)

    def one_time(time, carry):
        q = q_buf[time].reshape(TILE, HD)
        g = g_buf[time].reshape(TILE, HD)
        q1, g1 = q[HALF:], g[HALF:]
        top_main, top_side = None, None
        for d in range(3):
            col = time + d
            allowed = (col >= first_col) & (col <= last_col) & ((reach_t >= 1) | (d == 1))
            time_bias = jnp.where(allowed, 0.0, NEG).astype(F32)
            k01, k2 = keys(k_buf, col)
            s = dot(q, k01, ((1,), (1,))) * scale2 + (main_bias + time_bias)
            s_main[d] = s
            t = jnp.max(s, axis=1, keepdims=True)
            top_main = t if top_main is None else jnp.maximum(top_main, t)
            s = dot(q1, k2, ((1,), (1,))) * scale2 + (row_bias + time_bias)
            s_side[d] = s
            t = jnp.max(s, axis=1, keepdims=True)
            top_side = t if top_side is None else jnp.maximum(top_side, t)
        top1 = jnp.maximum(top_main[HALF:], top_side)
        top = jnp.concatenate([top_main[:HALF], top1], axis=0)
        total = jnp.zeros((TILE, 1), F32)
        delta = jnp.zeros((TILE, 1), F32)
        total1 = jnp.zeros((HALF, 1), F32)
        delta1 = jnp.zeros((HALF, 1), F32)
        for d in range(3):
            v01, v2 = keys(v_buf, time + d)
            e = jnp.exp2(s_main[d] - top)
            p = dot(g, v01, ((1,), (1,)))
            s_main[d] = e
            p_main[d] = p
            total += jnp.sum(e, axis=1, keepdims=True)
            delta += jnp.sum(e * p, axis=1, keepdims=True)
            e = jnp.exp2(s_side[d] - top1)
            p = dot(g1, v2, ((1,), (1,)))
            s_side[d] = e
            p_side[d] = p
            total1 += jnp.sum(e, axis=1, keepdims=True)
            delta1 += jnp.sum(e * p, axis=1, keepdims=True)
        total = jnp.concatenate([total[:HALF], total[HALF:] + total1], axis=0)
        delta = jnp.concatenate([delta[:HALF], delta[HALF:] + delta1], axis=0)
        inverse = 1.0 / total
        delta = delta * inverse
        inverse1, delta1 = inverse[HALF:], delta[HALF:]
        qt, gt = q.T, g.T
        qt1, gt1 = q1.T, g1.T
        dq = jnp.zeros((TILE, HD), F32)
        dq1 = jnp.zeros((HALF, HD), F32)
        for d in range(3):
            col = time + d
            k01, k2 = keys(k_buf, col)
            w = s_main[d] * inverse
            ds = (w * (p_main[d] - delta)).astype(BF)
            w = w.astype(BF)
            dq += dot(ds, k01, ((1,), (0,)))
            dv_acc[col, :, 0 : 2 * TILE] += dot(gt, w, ((1,), (0,)))
            dk_acc[col, :, 0 : 2 * TILE] += dot(qt, ds, ((1,), (0,)))
            w = s_side[d] * inverse1
            ds = (w * (p_side[d] - delta1)).astype(BF)
            w = w.astype(BF)
            dq1 += dot(ds, k2, ((1,), (0,)))
            dv_acc[col, :, 2 * TILE : 3 * TILE] += dot(gt1, w, ((1,), (0,)))
            dk_acc[col, :, 2 * TILE : 3 * TILE] += dot(qt1, ds, ((1,), (0,)))
        dq = jnp.concatenate([dq[:HALF], dq[HALF:] + dq1], axis=0) * HD ** (-0.5)
        for row in (0, 1):
            zl = lax.rem(zm + row, 2)
            dq_out[time, zl] = dq[row * HALF : (row + 1) * HALF].astype(BF).reshape(2, PIECE, HD)
        return carry

    lax.fori_loop(0, 4, one_time, 0)

    def place(base, kv, block):
        for core, out in ((0, mine_out), (1, sib_out)):
            for yhl in (0, 1):
                start = core * HALF + yhl * PIECE
                out[base + yhl * 2 + kv] = block[start : start + PIECE]

    def finish(col, base0, base1, base2):
        for kv, acc, factor in ((0, dk_acc, HD ** (-0.5)), (1, dv_acc, 1.0)):
            whole = (acc[col] * factor).astype(BF).T
            place(base0, kv, whole[:TILE])
            place(base1, kv, whole[TILE : 2 * TILE])
            place(base2, kv, whole[2 * TILE :])

    zl0, zl1 = zm, 1 - zm

    def finish_own(time, carry):
        finish(time + 1, time * 8 + zl0 * 4, time * 8 + zl1 * 4, 32 + time * 4)
        return carry

    lax.fori_loop(0, 4, finish_own, 0)
    finish(0, 48 + zl0 * 4, 48 + zl1 * 4, 48 + 8)
    finish(5, 60 + zl0 * 4, 60 + zl1 * 4, 60 + 8)


def attention(info, *arrays):
    return pl.pallas_call(
        attention_kernel,
        out_shape=[
            jax.ShapeDtypeStruct((4, 2, 2, PIECE, HD), BF),
            jax.ShapeDtypeStruct((72, PIECE, HD), BF),
            jax.ShapeDtypeStruct((72, PIECE, HD), BF),
        ],
        in_specs=[pl.BlockSpec(memory_space=pltpu.SMEM)] + [pl.BlockSpec(memory_space=pl.ANY)] * 9,
        out_specs=[pl.BlockSpec(memory_space=pltpu.VMEM)] * 3,
        scratch_shapes=[
            pltpu.VMEM((6, 3, 2, 2, PIECE, HD), BF),
            pltpu.VMEM((6, 3, 2, 2, PIECE, HD), BF),
            pltpu.VMEM((4, 2, 2, PIECE, HD), BF),
            pltpu.VMEM((4, 2, 2, PIECE, HD), BF),
            pltpu.VMEM((6, HD, 3 * TILE), F32),
            pltpu.VMEM((6, HD, 3 * TILE), F32),
            pltpu.VMEM((3, TILE, 2 * TILE), F32),
            pltpu.VMEM((3, HALF, TILE), F32),
            pltpu.VMEM((3, TILE, 2 * TILE), F32),
            pltpu.VMEM((3, HALF, TILE), F32),
            pltpu.SemaphoreType.DMA((40,)),
        ],
        compiler_params=pltpu.CompilerParams(vmem_limit_bytes=48 * 1024 * 1024),
        cost_estimate=pl.CostEstimate(flops=6 * 10**9, bytes_accessed=9 * 10**6, transcendentals=5 * 10**6),
    )(info, *arrays)


def to_heads(blocks):
    return lax.all_to_all(blocks, GROUP, split_axis=0, concat_axis=0, tiled=True)


def swapped(block):
    return lax.ppermute(block, "c", SWAP)


def per_device(queries, keys, values, out_grad, window):
    at = {name: lax.axis_index(name) for name in AXES}
    zm = at["zm"]
    zm_arg = jnp.full((1,), zm, jnp.int32)
    place = at["yl"] * 4 + at["x"]
    chip = ((at["zh"] * 2 + at["yhh"]) * 2 + at["zl"]) * 2 + at["yhl"]
    reach = lax.dynamic_slice_in_dim(window, head_of(chip, zm), 1, 0)[0]
    info = jnp.stack(
        [zm, reach[0], reach[1], jnp.where(place == 0, 1, 0), jnp.where(place == 7, 4, 5)]
    ).astype(jnp.int32)

    own = to_heads(spread(zm_arg, keys, values)).reshape(4, 2, 2, 2, PIECE, HD)
    qg = to_heads(spread(zm_arg, queries, out_grad)).reshape(4, 2, 2, 2, PIECE, HD)
    own_s = swapped(own)
    inner = lax.dynamic_slice_in_dim(own, 1 - zm, 1, 1)[:, 0]
    side = lax.ppermute(inner, Z, Z_PAIRS)
    nxt = lax.ppermute(jnp.concatenate([own[0], side[:1]], axis=0), LINE, BACK)
    prev = lax.ppermute(jnp.concatenate([own[3], side[3:]], axis=0), LINE, FORTH)
    dq, mine, sib = attention(
        info, own, own_s, side, swapped(side), prev, swapped(prev), nxt, swapped(nxt), qg
    )
    grad_queries = gather(zm_arg, to_heads(dq.reshape(HEADS, 1, PIECE, HD)))[0]
    terms = mine.astype(F32) + swapped(sib).astype(F32)
    d_own = terms[:32].reshape(4, 2, 2, 2, PIECE, HD)
    d_side = terms[32:48].reshape(4, 2, 2, PIECE, HD)
    d_prev = terms[48:60].reshape(3, 2, 2, PIECE, HD).astype(BF)
    d_nxt = terms[60:72].reshape(3, 2, 2, PIECE, HD).astype(BF)
    to_last = lax.ppermute(d_prev, LINE, BACK).astype(F32)
    to_first = lax.ppermute(d_nxt, LINE, FORTH).astype(F32)
    d_side = d_side.at[0].add(to_first[2]).at[3].add(to_last[2])
    to_inner = lax.ppermute(d_side.astype(BF), Z, Z_PAIRS).astype(F32)
    d_own = d_own.at[0].add(to_first[:2]).at[3].add(to_last[:2])
    is_inner = (jnp.arange(2) == 1 - zm)[None, :, None, None, None, None]
    d_own = d_own + jnp.where(is_inner, to_inner[:, None], 0.0)
    d_own = d_own.astype(BF).reshape(HEADS, 2, PIECE, HD)
    grad_keys, grad_values = gather(zm_arg, to_heads(d_own))
    return grad_queries, grad_keys, grad_values


def solution(mesh):
    fine = Mesh(mesh.devices.reshape(SIZES), AXES)
    rows = P(AXES, None)
    return jax.shard_map(
        per_device,
        mesh=fine,
        in_specs=(rows, rows, rows, rows, P()),
        out_specs=(rows, rows, rows),
        check_vma=False,
    )
```

time: 520 us -> 212 us (0.41)
  the two profiles are of different devices: /device:TPU:14 before, /device:TPU:120 now
where the time goes in v1:
time: 212 us; the launch traced here: 211 us
  waiting for transfers between devices  93.1 us (44%)
  starting transfers between devices  77.4 us (37%)
  Pallas kernels  29.8 us (14%)
  other arithmetic  5.75 us (3%)
  local copies, waits for them, and re-layouts  3.98 us (2%)
    all_to_all x4, waiting for transfers between devices, to_heads(): lax.all_to_all(blocks, GROUP, split_axis=0, concat_axis=0, tiled=True)  48.8 us
    all_to_all x4, starting transfers between devices, to_heads(): lax.all_to_all(blocks, GROUP, split_axis=0, concat_axis=0, tiled=True)  43.6 us
    ppermute x1, waiting for transfers between devices, per_device(): side = lax.ppermute(inner, Z, Z_PAIRS)  22.4 us
    pallas_call x1, Pallas kernels, attention(): pl.pallas_call(attention_kernel, out_shape=[jax.ShapeDtypeStruct((4, 2, 2...  21.3 us
    ppermute x1, waiting for transfers between devices, per_device(): to_inner = lax.ppermute(d_side.astype(BF), Z, Z_PAIRS).astype(F32)  15.2 us
    ppermute x5, starting transfers between devices, swapped(): return lax.ppermute(block, 'c', SWAP)  10.1 us
    ppermute x1, starting transfers between devices, per_device(): to_last = lax.ppermute(d_prev, LINE, BACK).astype(F32)  6.03 us
    ppermute x1, starting transfers between devices, per_device(): nxt = lax.ppermute(jnp.concatenate([own[0], side[:1]], axis=0), LINE, BACK)  5.39 us
  transfers between devices with their start and end apart: 15, of which 6 were waited for; matrix products, arithmetic and copies ran while one was open for 3% of the time, Pallas kernels for 2%

profile of v1, /device:TPU:120, one launch (start us, length us, event | category | flops | bytes accessed | tf_op | source)
XLA Modules:
  0.0 211.1 jit_solution(18226576728488743889)
XLA Ops:
  0.6 0.0 copy-start
  0.7 2.2 %shard_map.76 = bf16[16,2,96,128]{3,2,1,0:T(8,128)(2,1)} custom-call(s32[1]{0:T(128)} %bitcast.zm_ref, bf16[96,2048]{1,0:T(8,128)(2,1)} %a_ref.2, bf16[96,2048]{1,0:T(8,128)(2,1)} %b_ref.2), custom_call_target="tpu_custom_call" | custom-call | bytes 1572864 | tf_op jit(solution)/shard_map/pallas_call | solution.py:43
  2.9 14.5 %all-to-all-start = ((bf16[16,2,96,128]{3,2,1,0:T(8,128)(2,1)}), bf16[16,2,96,128]{3,2,1,0:T(8,128)(2,1)S(1)}, u32[]{:S(2)}, u32[]{:S(2)}) async-start(bf16[16,2,96,128]{3,2,1,0:T(8,128)(2,1)} %shard_map.76), calls=%async_computation | async-start | bytes 1572864 | tf_op jit(solution)/shard_map/all_to_all | solution.py:241
  17.4 2.2 %shard_map.77 = bf16[16,2,96,128]{3,2,1,0:T(8,128)(2,1)} custom-call(s32[1]{0:T(128)} %bitcast.zm_ref, bf16[96,2048]{1,0:T(8,128)(2,1)} %a_ref.3, bf16[96,2048]{1,0:T(8,128)(2,1)} %b_ref.3), custom_call_target="tpu_custom_call" | custom-call | bytes 1572864 | tf_op jit(solution)/shard_map/pallas_call | solution.py:43
  19.6 19.4 %all-to-all-done = bf16[16,2,96,128]{3,2,1,0:T(8,128)(2,1)S(1)} async-done(((bf16[16,2,96,128]{3,2,1,0:T(8,128)(2,1)}), bf16[16,2,96,128]{3,2,1,0:T(8,128)(2,1)S(1)}, u32[]{:S(2)}, u32[]{:S(2)}) %all-to-all-start) | async-done | bytes 786464 | tf_op jit(solution)/shard_map/all_to_all | solution.py:241
  39.0 10.4 %all-to-all-start.1 = ((bf16[16,2,96,128]{3,2,1,0:T(8,128)(2,1)}), bf16[16,2,96,128]{3,2,1,0:T(8,128)(2,1)S(1)}, u32[]{:S(2)}, u32[]{:S(2)}) async-start(bf16[16,2,96,128]{3,2,1,0:T(8,128)(2,1)} %shard_map.77), calls=%async_computation.1 | async-start | bytes 1572864 | tf_op jit(solution)/shard_map/all_to_all | solution.py:241
  49.4 3.5 %collective-permute-start.1 = (bf16[4,2,2,96,128]{4,3,2,1,0:T(8,128)(2,1)S(1)}, bf16[4,2,2,96,128]{4,3,2,1,0:T(8,128)(2,1)S(1)}, u32[]{:S(2)}, u32[]{:S(2)}) collective-permute-start(bf16[4,2,2,96,128]{4,3,2,1,0:T(8,128)(2,1)S(1)} %dynamic-slice_bitcast_fusion), channel_id=1, source_target_pairs={{8,16},{16,8},{40,48},{48,40},{0,56},{56,0},{32,24},{24,32},{9,17}... | collective-permute-start | bytes 1179656 | tf_op jit(solution)/shard_map/ppermute | solution.py:263
  52.9 1.9 collective-permute-start
  54.9 22.4 %collective-permute-done.1.side = bf16[4,2,2,96,128]{4,3,2,1,0:T(8,128)(2,1)S(1)} collective-permute-done((bf16[4,2,2,96,128]{4,3,2,1,0:T(8,128)(2,1)S(1)}, bf16[4,2,2,96,128]{4,3,2,1,0:T(8,128)(2,1)S(1)}, u32[]{:S(2)}, u32[]{:S(2)}) %collective-permute-start.1) | collective-permute-done | bytes 393248 | tf_op jit(solution)/shard_map/ppermute | solution.py:263
  77.3 3.4 %collective-permute-start.3 = (bf16[3,2,2,96,128]{4,3,2,1,0:T(8,128)(2,1)S(1)}, bf16[3,2,2,96,128]{4,3,2,1,0:T(8,128)(2,1)S(1)}, u32[]{:S(2)}, u32[]{:S(2)}) collective-permute-start(bf16[3,2,2,96,128]{4,3,2,1,0:T(8,128)(2,1)S(1)} %pad_maximum_fusion), channel_id=1, source_target_pairs={{0,64},{64,128},{128,192},{192,256},{256,320},{320,384},{384,448},... | collective-permute-start | bytes 884744 | tf_op jit(solution)/shard_map/ppermute | solution.py:265
  80.8 5.4 %collective-permute-start.5 = (bf16[3,2,2,96,128]{4,3,2,1,0:T(8,128)(2,1)S(1)}, bf16[3,2,2,96,128]{4,3,2,1,0:T(8,128)(2,1)}, u32[]{:S(2)}, u32[]{:S(2)}) collective-permute-start(bf16[3,2,2,96,128]{4,3,2,1,0:T(8,128)(2,1)S(1)} %pad_maximum_fusion.1), channel_id=1, source_target_pairs={{64,0},{128,64},{192,128},{256,192},{320,256},{384,320},{448,384},... | collective-permute-start | bytes 884744 | tf_op jit(solution)/shard_map/ppermute | solution.py:264
  86.2 1.9 collective-permute-start.2
  88.1 2.8 %collective-permute-done.3.prev = bf16[3,2,2,96,128]{4,3,2,1,0:T(8,128)(2,1)S(1)} collective-permute-done((bf16[3,2,2,96,128]{4,3,2,1,0:T(8,128)(2,1)S(1)}, bf16[3,2,2,96,128]{4,3,2,1,0:T(8,128)(2,1)S(1)}, u32[]{:S(2)}, u32[]{:S(2)}) %collective-permute-start.3) | collective-permute-done | bytes 294944 | tf_op jit(solution)/shard_map/ppermute | solution.py:265
  90.9 1.9 collective-permute-start.4
  92.8 0.0 collective-permute-done.5.nxt
  92.8 2.4 %collective-permute-start.6 = (bf16[3,2,2,96,128]{4,3,2,1,0:T(8,128)(2,1)}, bf16[3,2,2,96,128]{4,3,2,1,0:T(8,128)(2,1)}, u32[]{:S(2)}, u32[]{:S(2)}) collective-permute-start(bf16[3,2,2,96,128]{4,3,2,1,0:T(8,128)(2,1)} %collective-permute-done.5.nxt), channel_id=1, source_target_pairs={{0,1},{1,0},{2,3},{3,2},{4,5},{5,4},{6,7},{7,6},{8,9},{9,8},{10,11... | collective-permute-start | bytes 884744 | tf_op jit(solution)/shard_map/ppermute | solution.py:245
  95.4 0.0 copy-done
  95.4 0.1 constant_dynamic-slice_fusion
  95.5 0.5 fusion.10
  96.0 1.4 stack.12.info
  97.3 0.0 all-to-all-done.1
  97.3 0.0 collective-permute-done.2.side_s
  97.4 0.0 collective-permute-done.own_s
  97.4 0.0 collective-permute-done.4.prev_s
  97.4 0.0 collective-permute-done.6.nxt_s
  97.4 21.3 %shard_map.78 = (bf16[4,2,2,96,128]{4,3,2,1,0:T(8,128)(2,1)}, bf16[72,96,128]{2,1,0:T(8,128)(2,1)}, bf16[72,96,128]{2,1,0:T(8,128)(2,1)}) custom-call(s32[5]{0:T(128)S(1)} %stack.12.info, bf16[4,2,2,2,96,128]{5,4,3,2,1,0:T(8,128)(2,1)S(1)} %bitcast.31, bf16[4,2,2,2,96,128]{5,4,3,2,1,0:T(8,128)(2,1)S(1)} %collective-permute-done.own_s, ...), custom_call_target="tpu_custom_call" | custom-call | flops 6000000000 | bytes 9000000 | tf_op jit(solution)/shard_map/pallas_call | solution.py:213
  118.7 1.9 collective-permute-start.7
  120.6 3.9 %collective-permute-done.7 = bf16[72,96,128]{2,1,0:T(8,128)(2,1)S(1)} collective-permute-done((bf16[72,96,128]{2,1,0:T(8,128)(2,1)}, bf16[72,96,128]{2,1,0:T(8,128)(2,1)S(1)}, u32[]{:S(2)}, u32[]{:S(2)}) %collective-permute-start.7) | collective-permute-done | bytes 1769504 | tf_op jit(solution)/shard_map/ppermute | solution.py:245
  124.5 2.2 %fusion.6 = (bf16[72,96,128]{2,1,0:T(8,128)(2,1)S(1)}, f32[72,96,128]{2,1,0:T(8,128)S(1)}) fusion(bf16[72,96,128]{2,1,0:T(8,128)(2,1)S(1)} %collective-permute-done.7, bf16[72,96,128]{2,1,0:T(8,128)(2,1)} %get-tuple-element.57), kind=kLoop, calls=%fused_computation.17 | loop fusion | flops 3538944 | bytes 8847360 | tf_op jit(solution)/shard_map/convert.1
  126.6 0.8 fusion.7
  127.5 1.9 collective-permute-start.8
  129.4 6.0 %collective-permute-start.9 = (bf16[3,2,2,96,128]{4,3,2,1,0:T(8,128)(2,1)}, bf16[3,2,2,96,128]{4,3,2,1,0:T(8,128)(2,1)}, u32[]{:S(2)}, u32[]{:S(2)}) collective-permute-start(bf16[3,2,2,96,128]{4,3,2,1,0:T(8,128)(2,1)} %bitcast.15), channel_id=1, source_target_pairs={{64,0},{128,64},{192,128},{256,192},{320,256},{384,320},{448,384},... | collective-permute-start | bytes 884744 | tf_op jit(solution)/shard_map/ppermute | solution.py:275
  135.5 9.9 %all-to-all-start.2 = ((bf16[16,1,96,128]{3,2,1,0:T(8,128)(2,1)}), bf16[16,1,96,128]{3,2,1,0:T(8,128)(2,1)}, u32[]{:S(2)}, u32[]{:S(2)}) async-start(bf16[16,1,96,128]{3,2,1,0:T(8,128)(2,1)} %bitcast.10), calls=%async_computation.2 | async-start | bytes 786432 | tf_op jit(solution)/shard_map/all_to_all | solution.py:241
  145.4 0.1 slice.225
  145.4 0.1 slice.218
  145.5 0.0 collective-permute-done.8
  145.6 1.0 convert_element_type.32
  146.6 0.0 collective-permute-done.9
  146.6 1.0 convert_element_type.34
  147.7 0.1 convert_element_type.35
  147.8 3.4 %collective-permute-start.10 = (bf16[4,2,2,96,128]{4,3,2,1,0:T(8,128)(2,1)S(1)}, bf16[4,2,2,96,128]{4,3,2,1,0:T(8,128)(2,1)S(1)}, u32[]{:S(2)}, u32[]{:S(2)}) collective-permute-start(bf16[4,2,2,96,128]{4,3,2,1,0:T(8,128)(2,1)S(1)} %convert_element_type.35), channel_id=1, source_target_pairs={{8,16},{16,8},{40,48},{48,40},{0,56},{56,0},{32,24},{24,32},{9,17}... | collective-permute-start | bytes 1179656 | tf_op jit(solution)/shard_map/ppermute | solution.py:278
  151.3 0.1 fusion.1
  151.4 15.2 %collective-permute-done.10 = bf16[4,2,2,96,128]{4,3,2,1,0:T(8,128)(2,1)S(1)} collective-permute-done((bf16[4,2,2,96,128]{4,3,2,1,0:T(8,128)(2,1)S(1)}, bf16[4,2,2,96,128]{4,3,2,1,0:T(8,128)(2,1)S(1)}, u32[]{:S(2)}, u32[]{:S(2)}) %collective-permute-start.10) | collective-permute-done | bytes 393248 | tf_op jit(solution)/shard_map/ppermute | solution.py:278
  166.5 0.1 convert_element_type.36
  166.6 1.2 add_convert_fusion
  167.8 0.0 all-to-all-done.2.in_ref
  167.8 8.9 %all-to-all-start.3 = ((bf16[16,2,96,128]{3,2,1,0:T(8,128)(2,1)}), bf16[16,2,96,128]{3,2,1,0:T(8,128)(2,1)S(1)}, u32[]{:S(2)}, u32[]{:S(2)}) async-start(bf16[16,2,96,128]{3,2,1,0:T(8,128)(2,1)} %bitcast.19), calls=%async_computation.3 | async-start | bytes 1572864 | tf_op jit(solution)/shard_map/all_to_all | solution.py:241
  176.6 1.8 shard_map.79
  178.5 29.5 %all-to-all-done.3.in_ref = bf16[16,2,96,128]{3,2,1,0:T(8,128)(2,1)S(1)} async-done(((bf16[16,2,96,128]{3,2,1,0:T(8,128)(2,1)}), bf16[16,2,96,128]{3,2,1,0:T(8,128)(2,1)S(1)}, u32[]{:S(2)}, u32[]{:S(2)}) %all-to-all-start.3) | async-done | bytes 786464 | tf_op jit(solution)/shard_map/all_to_all | solution.py:241
  208.0 0.0 copy-start.1
  208.0 0.9 copy-done.1
  208.8 2.2 %shard_map.80 = (bf16[96,2048]{1,0:T(8,128)(2,1)}, bf16[96,2048]{1,0:T(8,128)(2,1)}) custom-call(s32[1]{0:T(128)} %bitcast.zm_ref, bf16[16,2,96,128]{3,2,1,0:T(8,128)(2,1)} %copy-done.1), custom_call_target="tpu_custom_call" | custom-call | bytes 1572864 | tf_op jit(solution)/shard_map/pallas_call | solution.py:62
  (11 shorter events, 0.3 us)
Async XLA Ops:
  0.6 94.7 %copy-start = (s32[16,2]{0,1:T(2,128)S(1)}, s32[16,2]{0,1:T(2,128)}, u32[]{:S(2)}) copy-start(s32[16,2]{0,1:T(2,128)} %param.17) | copy-start | bytes 388
  2.9 36.1 %all-to-all-start = ((bf16[16,2,96,128]{3,2,1,0:T(8,128)(2,1)}), bf16[16,2,96,128]{3,2,1,0:T(8,128)(2,1)S(1)}, u32[]{:S(2)}, u32[]{:S(2)}) async-start(bf16[16,2,96,128]{3,2,1,0:T(8,128)(2,1)} %shard_map.76), calls=%async_computation | async-start | bytes 1572864 | tf_op jit(solution)/shard_map/all_to_all | solution.py:241
  39.0 58.4 %all-to-all-start.1 = ((bf16[16,2,96,128]{3,2,1,0:T(8,128)(2,1)}), bf16[16,2,96,128]{3,2,1,0:T(8,128)(2,1)S(1)}, u32[]{:S(2)}, u32[]{:S(2)}) async-start(bf16[16,2,96,128]{3,2,1,0:T(8,128)(2,1)} %shard_map.77), calls=%async_computation.1 | async-start | bytes 1572864 | tf_op jit(solution)/shard_map/all_to_all | solution.py:241
  49.4 27.9 %collective-permute-start.1 = (bf16[4,2,2,96,128]{4,3,2,1,0:T(8,128)(2,1)S(1)}, bf16[4,2,2,96,128]{4,3,2,1,0:T(8,128)(2,1)S(1)}, u32[]{:S(2)}, u32[]{:S(2)}) collective-permute-start(bf16[4,2,2,96,128]{4,3,2,1,0:T(8,128)(2,1)S(1)} %dynamic-slice_bitcast_fusion), channel_id=1, source_target_pairs={{8,16},{16,8},{40,48},{48,40},{0,56},{56,0},{32,24},{24,32},{9,17}... | collective-permute-start | bytes 1179656 | tf_op jit(solution)/shard_map/ppermute | solution.py:263
  52.9 44.4 %collective-permute-start = (bf16[4,2,2,2,96,128]{5,4,3,2,1,0:T(8,128)(2,1)S(1)}, bf16[4,2,2,2,96,128]{5,4,3,2,1,0:T(8,128)(2,1)S(1)}, u32[]{:S(2)}, u32[]{:S(2)}) collective-permute-start(bf16[4,2,2,2,96,128]{5,4,3,2,1,0:T(8,128)(2,1)S(1)} %bitcast.30), channel_id=1, source_target_pairs={{0,1},{1,0},{2,3},{3,2},{4,5},{5,4},{6,7},{7,6},{8,9},{9,8},{10,11... | collective-permute-start | bytes 2359304 | tf_op jit(solution)/shard_map/ppermute | solution.py:245
  77.3 13.6 %collective-permute-start.3 = (bf16[3,2,2,96,128]{4,3,2,1,0:T(8,128)(2,1)S(1)}, bf16[3,2,2,96,128]{4,3,2,1,0:T(8,128)(2,1)S(1)}, u32[]{:S(2)}, u32[]{:S(2)}) collective-permute-start(bf16[3,2,2,96,128]{4,3,2,1,0:T(8,128)(2,1)S(1)} %pad_maximum_fusion), channel_id=1, source_target_pairs={{0,64},{64,128},{128,192},{192,256},{256,320},{320,384},{384,448},... | collective-permute-start | bytes 884744 | tf_op jit(solution)/shard_map/ppermute | solution.py:265
  80.8 12.0 %collective-permute-start.5 = (bf16[3,2,2,96,128]{4,3,2,1,0:T(8,128)(2,1)S(1)}, bf16[3,2,2,96,128]{4,3,2,1,0:T(8,128)(2,1)}, u32[]{:S(2)}, u32[]{:S(2)}) collective-permute-start(bf16[3,2,2,96,128]{4,3,2,1,0:T(8,128)(2,1)S(1)} %pad_maximum_fusion.1), channel_id=1, source_target_pairs={{64,0},{128,64},{192,128},{256,192},{320,256},{384,320},{448,384},... | collective-permute-start | bytes 884744 | tf_op jit(solution)/shard_map/ppermute | solution.py:264
  86.2 11.2 %collective-permute-start.2 = (bf16[4,2,2,96,128]{4,3,2,1,0:T(8,128)(2,1)S(1)}, bf16[4,2,2,96,128]{4,3,2,1,0:T(8,128)(2,1)S(1)}, u32[]{:S(2)}, u32[]{:S(2)}) collective-permute-start(bf16[4,2,2,96,128]{4,3,2,1,0:T(8,128)(2,1)S(1)} %collective-permute-done.1.side), channel_id=1, source_target_pairs={{0,1},{1,0},{2,3},{3,2},{4,5},{5,4},{6,7},{7,6},{8,9},{9,8},{10,11... | collective-permute-start | bytes 1179656 | tf_op jit(solution)/shard_map/ppermute | solution.py:245
  90.9 6.5 %collective-permute-start.4 = (bf16[3,2,2,96,128]{4,3,2,1,0:T(8,128)(2,1)S(1)}, bf16[3,2,2,96,128]{4,3,2,1,0:T(8,128)(2,1)}, u32[]{:S(2)}, u32[]{:S(2)}) collective-permute-start(bf16[3,2,2,96,128]{4,3,2,1,0:T(8,128)(2,1)S(1)} %collective-permute-done.3.prev), channel_id=1, source_target_pairs={{0,1},{1,0},{2,3},{3,2},{4,5},{5,4},{6,7},{7,6},{8,9},{9,8},{10,11... | collective-permute-start | bytes 884744 | tf_op jit(solution)/shard_map/ppermute | solution.py:245
  92.8 4.5 %collective-permute-start.6 = (bf16[3,2,2,96,128]{4,3,2,1,0:T(8,128)(2,1)}, bf16[3,2,2,96,128]{4,3,2,1,0:T(8,128)(2,1)}, u32[]{:S(2)}, u32[]{:S(2)}) collective-permute-start(bf16[3,2,2,96,128]{4,3,2,1,0:T(8,128)(2,1)} %collective-permute-done.5.nxt), channel_id=1, source_target_pairs={{0,1},{1,0},{2,3},{3,2},{4,5},{5,4},{6,7},{7,6},{8,9},{9,8},{10,11... | collective-permute-start | bytes 884744 | tf_op jit(solution)/shard_map/ppermute | solution.py:245
  118.7 5.8 %collective-permute-start.7 = (bf16[72,96,128]{2,1,0:T(8,128)(2,1)}, bf16[72,96,128]{2,1,0:T(8,128)(2,1)S(1)}, u32[]{:S(2)}, u32[]{:S(2)}) collective-permute-start(bf16[72,96,128]{2,1,0:T(8,128)(2,1)} %get-tuple-element.58), channel_id=1, source_target_pairs={{0,1},{1,0},{2,3},{3,2},{4,5},{5,4},{6,7},{7,6},{8,9},{9,8},{10,11... | collective-permute-start | bytes 5308424 | tf_op jit(solution)/shard_map/ppermute | solution.py:245
  127.5 18.1 %collective-permute-start.8 = (bf16[3,2,2,96,128]{4,3,2,1,0:T(8,128)(2,1)}, bf16[3,2,2,96,128]{4,3,2,1,0:T(8,128)(2,1)}, u32[]{:S(2)}, u32[]{:S(2)}) collective-permute-start(bf16[3,2,2,96,128]{4,3,2,1,0:T(8,128)(2,1)} %bitcast.13), channel_id=1, source_target_pairs={{0,64},{64,128},{128,192},{192,256},{256,320},{320,384},{384,448},... | collective-permute-start | bytes 884744 | tf_op jit(solution)/shard_map/ppermute | solution.py:276
  129.4 17.2 %collective-permute-start.9 = (bf16[3,2,2,96,128]{4,3,2,1,0:T(8,128)(2,1)}, bf16[3,2,2,96,128]{4,3,2,1,0:T(8,128)(2,1)}, u32[]{:S(2)}, u32[]{:S(2)}) collective-permute-start(bf16[3,2,2,96,128]{4,3,2,1,0:T(8,128)(2,1)} %bitcast.15), channel_id=1, source_target_pairs={{64,0},{128,64},{192,128},{256,192},{320,256},{384,320},{448,384},... | collective-permute-start | bytes 884744 | tf_op jit(solution)/shard_map/ppermute | solution.py:275
  135.5 32.3 %all-to-all-start.2 = ((bf16[16,1,96,128]{3,2,1,0:T(8,128)(2,1)}), bf16[16,1,96,128]{3,2,1,0:T(8,128)(2,1)}, u32[]{:S(2)}, u32[]{:S(2)}) async-start(bf16[16,1,96,128]{3,2,1,0:T(8,128)(2,1)} %bitcast.10), calls=%async_computation.2 | async-start | bytes 786432 | tf_op jit(solution)/shard_map/all_to_all | solution.py:241
  147.8 18.8 %collective-permute-start.10 = (bf16[4,2,2,96,128]{4,3,2,1,0:T(8,128)(2,1)S(1)}, bf16[4,2,2,96,128]{4,3,2,1,0:T(8,128)(2,1)S(1)}, u32[]{:S(2)}, u32[]{:S(2)}) collective-permute-start(bf16[4,2,2,96,128]{4,3,2,1,0:T(8,128)(2,1)S(1)} %convert_element_type.35), channel_id=1, source_target_pairs={{8,16},{16,8},{40,48},{48,40},{0,56},{56,0},{32,24},{24,32},{9,17}... | collective-permute-start | bytes 1179656 | tf_op jit(solution)/shard_map/ppermute | solution.py:278
  167.8 40.2 %all-to-all-start.3 = ((bf16[16,2,96,128]{3,2,1,0:T(8,128)(2,1)}), bf16[16,2,96,128]{3,2,1,0:T(8,128)(2,1)S(1)}, u32[]{:S(2)}, u32[]{:S(2)}) async-start(bf16[16,2,96,128]{3,2,1,0:T(8,128)(2,1)} %bitcast.19), calls=%async_computation.3 | async-start | bytes 1572864 | tf_op jit(solution)/shard_map/all_to_all | solution.py:241
  208.0 0.9 copy-start.1

commit v2 on v1

v2 whole, which is shorter than its diff:
```python
import functools

import jax
import jax.numpy as jnp
from jax import lax
from jax.experimental import pallas as pl
from jax.experimental.pallas import tpu as pltpu
from jax.sharding import Mesh, PartitionSpec as P

HD = 128
HEADS = 16
PIECE = 96
HALF = 192
TILE = 384
BF = jnp.bfloat16
F32 = jnp.float32
AXES = ("yl", "x", "zh", "zm", "zl", "yhh", "yhl", "c")
SIZES = (2, 4, 2, 2, 2, 2, 2, 2)
GROUP = ("zh", "yhh", "zl", "yhl")
Z = ("zh", "zm", "zl")
Z_PAIRS = [(1, 2), (2, 1), (5, 6), (6, 5), (0, 7), (7, 0), (4, 3), (3, 4)]
LINE = ("yl", "x")
FORTH = [(i, i + 1) for i in range(7)]
BACK = [(i + 1, i) for i in range(7)]
SWAP = [(0, 1), (1, 0)]
NEG = float("-inf")


def head_of(chip, zm):
    zh, yhh, zl, yhl = (chip // 8) % 2, (chip // 4) % 2, (chip // 2) % 2, chip % 2
    return ((zh * 2 + zl + zm) % 4) * 4 + yhh * 2 + yhl


def spread_kernel(zm_ref, a_ref, b_ref, out_ref):
    zm = zm_ref[0]
    for chip in range(HEADS):
        columns = pl.ds(pl.multiple_of(head_of(chip, zm) * HD, HD), HD)
        out_ref[chip, 0] = a_ref[:, columns]
        out_ref[chip, 1] = b_ref[:, columns]


def spread(zm, a, b):
    return pl.pallas_call(
        spread_kernel,
        out_shape=jax.ShapeDtypeStruct((HEADS, 2, PIECE, HD), BF),
        in_specs=[pl.BlockSpec(memory_space=pltpu.SMEM)] + [pl.BlockSpec(memory_space=pltpu.VMEM)] * 2,
        out_specs=pl.BlockSpec(memory_space=pltpu.VMEM),
        cost_estimate=pl.CostEstimate(flops=0, bytes_accessed=4 * 393216, transcendentals=0),
    )(zm, a, b)


def gather_kernel(count, zm_ref, in_ref, *out_refs):
    zm = zm_ref[0]
    for chip in range(HEADS):
        columns = pl.ds(pl.multiple_of(head_of(chip, zm) * HD, HD), HD)
        for n in range(count):
            out_refs[n][:, columns] = in_ref[chip, n]


def gather(zm, blocks):
    count = blocks.shape[1]
    return pl.pallas_call(
        functools.partial(gather_kernel, count),
        out_shape=[jax.ShapeDtypeStruct((PIECE, HEADS * HD), BF)] * count,
        in_specs=[pl.BlockSpec(memory_space=pltpu.SMEM), pl.BlockSpec(memory_space=pltpu.VMEM)],
        out_specs=[pl.BlockSpec(memory_space=pltpu.VMEM)] * count,
        cost_estimate=pl.CostEstimate(flops=0, bytes_accessed=2 * count * 393216, transcendentals=0),
    )(zm, blocks)


def dot(a, b, dims):
    return lax.dot_general(a, b, (dims, ((), ())), preferred_element_type=F32)


def attention_kernel(
    zm_ref, chip_ref, line_ref, window_ref, own, own_s, side, side_s, prev, prev_s, nxt, nxt_s, qg,
    dq_out, mine_out, sib_out,
    k_buf, v_buf, q_buf, g_buf, dk_acc, dv_acc, s_main, s_side, p_main, p_side, sems,
):
    zm, line = zm_ref[0], line_ref[0]
    head = head_of(chip_ref[0], zm)
    reach_t, reach_h = window_ref[head, 0], window_ref[head, 1]
    first_col = jnp.where(line == 0, 1, 0)
    last_col = jnp.where(line == 7, 4, 5)
    zls = (zm, 1 - zm)
    copies = []

    def copy(src, dst):
        c = pltpu.make_async_copy(src, dst, sems.at[len(copies)])
        c.start()
        copies.append(c)

    for kv, buf, part in ((0, k_buf, q_buf), (1, v_buf, g_buf)):
        for row in (0, 1):
            copy(qg.at[:, zls[row], :, kv], part.at[:, row])
        for core, (o, h, p, n) in enumerate(((own, side, prev, nxt), (own_s, side_s, prev_s, nxt_s))):
            for row in (0, 1):
                copy(o.at[:, zls[row], :, kv], buf.at[pl.ds(1, 4), row, core])
                copy(p.at[zls[row], :, kv], buf.at[0, row, core])
                copy(n.at[zls[row], :, kv], buf.at[5, row, core])
            copy(h.at[:, :, kv], buf.at[pl.ds(1, 4), 2, core])
            copy(p.at[2, :, kv], buf.at[0, 2, core])
            copy(n.at[2, :, kv], buf.at[5, 2, core])
    dk_acc[0:2] = jnp.zeros((2,) + dk_acc.shape[1:], F32)
    dv_acc[0:2] = jnp.zeros((2,) + dv_acc.shape[1:], F32)
    for c in copies:
        c.wait()

    scale2 = HD ** (-0.5) * 1.4426950408889634
    row_bias = jnp.where(reach_h >= 1, 0.0, NEG).astype(F32)

    def keys(buf, col):
        return buf[col, 0:2].reshape(2 * TILE, HD), buf[col, 2].reshape(TILE, HD)

    def lanes(j):
        return slice(j * 128, (j + 1) * 128)

    def finish(col, kv, block):
        block = (block * (1.0 if kv else HD ** (-0.5))).astype(BF).T
        for row in range(3):
            place = 2 if row == 2 else zls[row]
            for core, out in ((0, mine_out), (1, sib_out)):
                for yhl in (0, 1):
                    start = row * TILE + core * HALF + yhl * PIECE
                    out[col, place, yhl, kv] = block[start : start + PIECE]

    def one_time(time, carry):
        q = q_buf[time].reshape(TILE, HD)
        g = g_buf[time].reshape(TILE, HD)
        q1, g1 = q[HALF:], g[HALF:]
        tops = [jnp.full((HALF, 128), NEG, F32)] * 2
        for d in range(3):
            col = time + d
            allowed = (col >= first_col) & (col <= last_col) & ((reach_t >= 1) | (d == 1))
            time_bias = jnp.where(allowed, 0.0, NEG).astype(F32)
            far_bias = time_bias + row_bias
            k01, k2 = keys(k_buf, col)
            s = dot(q, k01, ((1,), (1,))) * scale2
            for half in (0, 1):
                for j in range(6):
                    part = s[half * HALF : (half + 1) * HALF, lanes(j)]
                    if j // 3 != half:
                        part = part + far_bias
                    elif d != 1:
                        part = part + time_bias
                    s_main[d, half * HALF : (half + 1) * HALF, lanes(j)] = part
                    tops[half] = jnp.maximum(tops[half], part)
            s = dot(q1, k2, ((1,), (1,))) * scale2 + far_bias
            s_side[d] = s
            for j in range(3):
                tops[1] = jnp.maximum(tops[1], s[:, lanes(j)])
        tops = [jnp.max(t, axis=1, keepdims=True) for t in tops]
        top = jnp.concatenate(tops, axis=0)
        total = jnp.zeros((TILE, 128), F32)
        delta = jnp.zeros((TILE, 128), F32)
        total1 = jnp.zeros((HALF, 128), F32)
        delta1 = jnp.zeros((HALF, 128), F32)
        for d in range(3):
            v01, v2 = keys(v_buf, time + d)
            p = dot(g, v01, ((1,), (1,)))
            p_main[d] = p
            for j in range(6):
                e = jnp.exp2(s_main[d, :, lanes(j)] - top)
                s_main[d, :, lanes(j)] = e
                total += e
                delta += e * p[:, lanes(j)]
            p = dot(g1, v2, ((1,), (1,)))
            p_side[d] = p
            for j in range(3):
                e = jnp.exp2(s_side[d, :, lanes(j)] - tops[1])
                s_side[d, :, lanes(j)] = e
                total1 += e
                delta1 += e * p[:, lanes(j)]
        total = jnp.concatenate([total[:HALF], total[HALF:] + total1], axis=0)
        delta = jnp.concatenate([delta[:HALF], delta[HALF:] + delta1], axis=0)
        inverse = 1.0 / jnp.sum(total, axis=1, keepdims=True)
        delta = jnp.sum(delta, axis=1, keepdims=True) * inverse
        qt, gt = q.T, g.T
        qt1, gt1 = qt[:, HALF:], gt[:, HALF:]
        dq = jnp.zeros((TILE, HD), F32)
        dq1 = jnp.zeros((HALF, HD), F32)
        for d in range(3):
            col = time + d
            k01, k2 = keys(k_buf, col)
            w = s_main[d] * inverse
            ds = (w * (p_main[d] - delta)).astype(BF)
            w1 = s_side[d] * inverse[HALF:]
            ds1 = (w1 * (p_side[d] - delta[HALF:])).astype(BF)
            dq += dot(ds, k01, ((1,), (0,)))
            dq1 += dot(ds1, k2, ((1,), (0,)))
            for kv, acc, main, last in ((0, dk_acc, dot(qt, ds, ((1,), (0,))), dot(qt1, ds1, ((1,), (0,)))),
                                  (1, dv_acc, dot(gt, w.astype(BF), ((1,), (0,))), dot(gt1, w1.astype(BF), ((1,), (0,))))):
                if d == 2:
                    acc[col, :, 0 : 2 * TILE] = main
                    acc[col, :, 2 * TILE :] = last
                elif d == 1:
                    acc[col, :, 0 : 2 * TILE] += main
                    acc[col, :, 2 * TILE :] += last
                else:
                    finish(col, kv, acc[col] + jnp.concatenate([main, last], axis=1))
        dq = jnp.concatenate([dq[:HALF], dq[HALF:] + dq1], axis=0) * (HD ** (-0.5))
        for row in (0, 1):
            dq_out[time, zls[row]] = dq[row * HALF : (row + 1) * HALF].astype(BF).reshape(2, PIECE, HD)
        return carry

    lax.fori_loop(0, 4, one_time, 0, unroll=1)
    for col in (4, 5):
        finish(col, 0, dk_acc[col])
        finish(col, 1, dv_acc[col])


def attention(*arrays):
    return pl.pallas_call(
        attention_kernel,
        out_shape=[
            jax.ShapeDtypeStruct((4, 2, 2, PIECE, HD), BF),
            jax.ShapeDtypeStruct((6, 3, 2, 2, PIECE, HD), BF),
            jax.ShapeDtypeStruct((6, 3, 2, 2, PIECE, HD), BF),
        ],
        in_specs=[pl.BlockSpec(memory_space=pltpu.SMEM)] * 4 + [pl.BlockSpec(memory_space=pl.ANY)] * 9,
        out_specs=[pl.BlockSpec(memory_space=pltpu.VMEM)] * 3,
        scratch_shapes=[
            pltpu.VMEM((6, 3, 2, 2, PIECE, HD), BF),
            pltpu.VMEM((6, 3, 2, 2, PIECE, HD), BF),
            pltpu.VMEM((4, 2, 2, PIECE, HD), BF),
            pltpu.VMEM((4, 2, 2, PIECE, HD), BF),
            pltpu.VMEM((6, HD, 3 * TILE), F32),
            pltpu.VMEM((6, HD, 3 * TILE), F32),
            pltpu.VMEM((3, TILE, 2 * TILE), F32),
            pltpu.VMEM((3, HALF, TILE), F32),
            pltpu.VMEM((3, TILE, 2 * TILE), F32),
            pltpu.VMEM((3, HALF, TILE), F32),
            pltpu.SemaphoreType.DMA((40,)),
        ],
        compiler_params=pltpu.CompilerParams(vmem_limit_bytes=48 * 1024 * 1024),
        cost_estimate=pl.CostEstimate(flops=6 * 10**9, bytes_accessed=9 * 10**6, transcendentals=5 * 10**6),
    )(*arrays)


def to_heads(blocks):
    return lax.all_to_all(blocks, GROUP, split_axis=0, concat_axis=0, tiled=True)


def swapped(block):
    return lax.ppermute(block, "c", SWAP)


def scalar(value):
    return jnp.full((1,), value, jnp.int32)


def per_device(queries, keys, values, out_grad, window):
    at = {name: lax.axis_index(name) for name in AXES}
    zm = at["zm"]
    zm_arg = scalar(zm)
    line = scalar(at["yl"] * 4 + at["x"])
    chip = scalar(((at["zh"] * 2 + at["yhh"]) * 2 + at["zl"]) * 2 + at["yhl"])

    own = to_heads(spread(zm_arg, keys, values)).reshape(4, 2, 2, 2, PIECE, HD)
    inner = lax.dynamic_slice_in_dim(own, 1 - zm, 1, 1)[:, 0]
    qg = spread(zm_arg, queries, out_grad)
    side = lax.ppermute(inner, Z, Z_PAIRS)
    qg, side = lax.optimization_barrier((qg, side))
    qg = to_heads(qg).reshape(4, 2, 2, 2, PIECE, HD)
    own_s = swapped(own)
    nxt = lax.ppermute(jnp.concatenate([own[0], side[:1]], axis=0), LINE, BACK)
    prev = lax.ppermute(jnp.concatenate([own[3], side[3:]], axis=0), LINE, FORTH)
    dq, mine, sib = attention(
        zm_arg, chip, line, window, own, own_s, side, swapped(side), prev, swapped(prev), nxt, swapped(nxt), qg
    )
    sib = swapped(sib)

    def terms(*at):
        return mine[at].astype(F32) + sib[at].astype(F32)

    to_last = lax.ppermute(terms(0).astype(BF), LINE, BACK)
    to_first = lax.ppermute(terms(5).astype(BF), LINE, FORTH)
    d_side = [terms(time + 1, 2) for time in range(4)]
    d_side[0] += to_first[2].astype(F32)
    d_side[3] += to_last[2].astype(F32)
    to_inner = lax.ppermute(jnp.stack(d_side).astype(BF), Z, Z_PAIRS)
    is_inner = (jnp.arange(2) == 1 - zm)[:, None, None, None, None]
    d_own = []
    for time in range(4):
        total = terms(time + 1, slice(0, 2)) + jnp.where(is_inner, to_inner[time][None].astype(F32), 0.0)
        if time == 0:
            total = total + to_first[:2].astype(F32)
        if time == 3:
            total = total + to_last[:2].astype(F32)
        d_own.append(total.astype(BF))
    grads = jnp.concatenate([jnp.stack(d_own), dq[:, :, :, None]], axis=3).reshape(HEADS, 3, PIECE, HD)
    grad_keys, grad_values, grad_queries = gather(zm_arg, to_heads(grads))
    return grad_queries, grad_keys, grad_values


def solution(mesh):
    fine = Mesh(mesh.devices.reshape(SIZES), AXES)
    rows = P(AXES, None)
    return jax.shard_map(
        per_device,
        mesh=fine,
        in_specs=(rows, rows, rows, rows, P()),
        out_specs=(rows, rows, rows),
        check_vma=False,
    )
```

time: 212 us -> 200 us (0.943)
  the two profiles are of different devices: /device:TPU:120 before, /device:TPU:6 now
where the time goes in v2:
time: 200 us; the launch traced here: 199 us
  waiting for transfers between devices  70.8 us (35%)
  starting transfers between devices  57 us (28%)
  blocking collectives  40.8 us (20%)
  Pallas kernels  27.2 us (14%)
  other arithmetic  2.16 us (1%)
    all_to_all x1, blocking collectives, to_heads(): lax.all_to_all(blocks, GROUP, split_axis=0, concat_axis=0, tiled=True)  40.8 us
    all_to_all x2, waiting for transfers between devices, to_heads(): lax.all_to_all(blocks, GROUP, split_axis=0, concat_axis=0, tiled=True)  26.6 us
    all_to_all x2, starting transfers between devices, to_heads(): lax.all_to_all(blocks, GROUP, split_axis=0, concat_axis=0, tiled=True)  24.8 us
    pallas_call x1, Pallas kernels, attention(): pl.pallas_call(attention_kernel, out_shape=[jax.ShapeDtypeStruct((4, 2, 2...  20.2 us
    ppermute x1, waiting for transfers between devices, per_device(): lax.ppermute(jnp.concatenate([own[3], side[3:]], axis=0), LINE, FORTH)  12 us
    ppermute x5, starting transfers between devices, swapped(): return lax.ppermute(block, 'c', SWAP)  10.6 us
    ppermute x1, waiting for transfers between devices, per_device(): to_inner = lax.ppermute(jnp.stack(d_side).astype(BF), Z, Z_PAIRS)  8.49 us
    ppermute x1, waiting for transfers between devices, per_device(): side = lax.ppermute(inner, Z, Z_PAIRS)  7.79 us
  transfers between devices with their start and end apart: 13, of which 8 were waited for; matrix products, arithmetic and copies ran while one was open for 0% of the time, Pallas kernels for 1%

profile of v2, /device:TPU:6, one launch (start us, length us, event | category | flops | bytes accessed | tf_op | source)
XLA Modules:
  0.0 199.0 jit_solution(2532031931534211142)
XLA Ops:
  0.6 2.2 %shard_map.76 = bf16[16,2,96,128]{3,2,1,0:T(8,128)(2,1)} custom-call(s32[1]{0:T(128)} %bitcast.zm_ref, bf16[96,2048]{1,0:T(8,128)(2,1)} %a_ref.2, bf16[96,2048]{1,0:T(8,128)(2,1)} %b_ref.2), custom_call_target="tpu_custom_call" | custom-call | bytes 1572864 | tf_op jit(solution)/shard_map/pallas_call | solution.py:43
  2.8 15.7 %all-to-all-start = ((bf16[16,2,96,128]{3,2,1,0:T(8,128)(2,1)}), bf16[16,2,96,128]{3,2,1,0:T(8,128)(2,1)S(1)}, u32[]{:S(2)}, u32[]{:S(2)}) async-start(bf16[16,2,96,128]{3,2,1,0:T(8,128)(2,1)} %shard_map.76), calls=%async_computation | async-start | bytes 1572864 | tf_op jit(solution)/shard_map/all_to_all | solution.py:241
  18.5 26.6 %all-to-all-done = bf16[16,2,96,128]{3,2,1,0:T(8,128)(2,1)S(1)} async-done(((bf16[16,2,96,128]{3,2,1,0:T(8,128)(2,1)}), bf16[16,2,96,128]{3,2,1,0:T(8,128)(2,1)S(1)}, u32[]{:S(2)}, u32[]{:S(2)}) %all-to-all-start) | async-done | bytes 786464 | tf_op jit(solution)/shard_map/all_to_all | solution.py:241
  45.1 2.3 %collective-permute-start.1 = (bf16[4,2,2,96,128]{4,3,2,1,0:T(8,128)(2,1)S(1)}, bf16[4,2,2,96,128]{4,3,2,1,0:T(8,128)(2,1)S(1)}, u32[]{:S(2)}, u32[]{:S(2)}) collective-permute-start(bf16[4,2,2,96,128]{4,3,2,1,0:T(8,128)(2,1)S(1)} %dynamic-slice_bitcast_fusion), channel_id=1, source_target_pairs={{8,16},{16,8},{40,48},{48,40},{0,56},{56,0},{32,24},{24,32},{9,17}... | collective-permute-start | bytes 1179656 | tf_op jit(solution)/shard_map/ppermute | solution.py:262
  47.4 2.2 %shard_map.77 = bf16[16,2,96,128]{3,2,1,0:T(8,128)(2,1)} custom-call(s32[1]{0:T(128)} %bitcast.zm_ref, bf16[96,2048]{1,0:T(8,128)(2,1)} %a_ref.3, bf16[96,2048]{1,0:T(8,128)(2,1)} %b_ref.3), custom_call_target="tpu_custom_call" | custom-call | bytes 1572864 | tf_op jit(solution)/shard_map/pallas_call | solution.py:43
  49.6 0.0 copy-start.1
  49.6 7.8 %collective-permute-done.1.side = bf16[4,2,2,96,128]{4,3,2,1,0:T(8,128)(2,1)S(1)} collective-permute-done((bf16[4,2,2,96,128]{4,3,2,1,0:T(8,128)(2,1)S(1)}, bf16[4,2,2,96,128]{4,3,2,1,0:T(8,128)(2,1)S(1)}, u32[]{:S(2)}, u32[]{:S(2)}) %collective-permute-start.1) | collective-permute-done | bytes 393248 | tf_op jit(solution)/shard_map/ppermute | solution.py:262
  57.4 9.1 %all-to-all-start.1 = ((bf16[16,2,96,128]{3,2,1,0:T(8,128)(2,1)}), bf16[16,2,96,128]{3,2,1,0:T(8,128)(2,1)S(1)}, u32[]{:S(2)}, u32[]{:S(2)}) async-start(bf16[16,2,96,128]{3,2,1,0:T(8,128)(2,1)} %shard_map.77), calls=%async_computation.1 | async-start | bytes 1572864 | tf_op jit(solution)/shard_map/all_to_all | solution.py:241
  66.5 1.9 collective-permute-start
  68.6 1.9 collective-permute-start.3
  70.5 3.9 %collective-permute-start.5 = (bf16[3,2,2,96,128]{4,3,2,1,0:T(8,128)(2,1)S(1)}, bf16[3,2,2,96,128]{4,3,2,1,0:T(8,128)(2,1)}, u32[]{:S(2)}, u32[]{:S(2)}) collective-permute-start(bf16[3,2,2,96,128]{4,3,2,1,0:T(8,128)(2,1)S(1)} %pad_maximum_fusion.4), channel_id=1, source_target_pairs={{64,0},{128,64},{192,128},{256,192},{320,256},{384,320},{448,384},... | collective-permute-start | bytes 884744 | tf_op jit(solution)/shard_map/ppermute | solution.py:266
  74.5 1.9 collective-permute-start.2
  76.4 12.0 %collective-permute-done.3.prev = bf16[3,2,2,96,128]{4,3,2,1,0:T(8,128)(2,1)S(1)} collective-permute-done((bf16[3,2,2,96,128]{4,3,2,1,0:T(8,128)(2,1)S(1)}, bf16[3,2,2,96,128]{4,3,2,1,0:T(8,128)(2,1)S(1)}, u32[]{:S(2)}, u32[]{:S(2)}) %collective-permute-start.3) | collective-permute-done | bytes 294944 | tf_op jit(solution)/shard_map/ppermute | solution.py:267
  88.4 1.9 collective-permute-start.4
  90.3 0.0 collective-permute-done.5.nxt
  90.3 2.4 %collective-permute-start.6 = (bf16[3,2,2,96,128]{4,3,2,1,0:T(8,128)(2,1)}, bf16[3,2,2,96,128]{4,3,2,1,0:T(8,128)(2,1)}, u32[]{:S(2)}, u32[]{:S(2)}) collective-permute-start(bf16[3,2,2,96,128]{4,3,2,1,0:T(8,128)(2,1)} %collective-permute-done.5.nxt), channel_id=1, source_target_pairs={{0,1},{1,0},{2,3},{3,2},{4,5},{5,4},{6,7},{7,6},{8,9},{9,8},{10,11... | collective-permute-start | bytes 884744 | tf_op jit(solution)/shard_map/ppermute | solution.py:245
  92.8 0.0 copy-done.1
  92.8 0.1 copy.8.window_ref
  92.9 0.0 collective-permute-done.2.side_s
  92.9 0.0 collective-permute-done.own_s
  92.9 0.0 collective-permute-done.4.prev_s
  92.9 1.4 collective-permute-done.6.nxt_s
  94.3 0.0 all-to-all-done.1
  94.3 20.2 %shard_map.78 = (bf16[4,2,2,96,128]{4,3,2,1,0:T(8,128)(2,1)S(1)}, bf16[6,3,2,2,96,128]{5,4,3,2,1,0:T(8,128)(2,1)}, bf16[6,3,2,2,96,128]{5,4,3,2,1,0:T(8,128)(2,1)}) custom-call(s32[1]{0:T(128)} %bitcast.zm_ref, s32[1]{0:T(128)} %bitcast.1.chip_ref, s32[1]{0:T(128)} %bitcast.2.line_ref, s32[16,2]{1,0:T(8,128)S(1)} %copy.8.window_ref, ...), custom_call_target="tpu_custom_call" | custom-call | flops 6000000000 | bytes 9000000 | tf_op jit(solution)/shard_map/pallas_call | solution.py:213
  114.5 0.0 copy-start
  114.5 2.4 %collective-permute-start.7 = (bf16[6,3,2,2,96,128]{5,4,3,2,1,0:T(8,128)(2,1)}, bf16[6,3,2,2,96,128]{5,4,3,2,1,0:T(8,128)(2,1)S(1)}, u32[]{:S(2)}, u32[]{:S(2)}) collective-permute-start(bf16[6,3,2,2,96,128]{5,4,3,2,1,0:T(8,128)(2,1)} %get-tuple-element.14), channel_id=1, source_target_pairs={{0,1},{1,0},{2,3},{3,2},{4,5},{5,4},{6,7},{7,6},{8,9},{9,8},{10,11... | collective-permute-start | bytes 5308424 | tf_op jit(solution)/shard_map/ppermute | solution.py:245
  116.9 3.5 %collective-permute-done.7 = bf16[6,3,2,2,96,128]{5,4,3,2,1,0:T(8,128)(2,1)S(1)} collective-permute-done((bf16[6,3,2,2,96,128]{5,4,3,2,1,0:T(8,128)(2,1)}, bf16[6,3,2,2,96,128]{5,4,3,2,1,0:T(8,128)(2,1)S(1)}, u32[]{:S(2)}, u32[]{:S(2)}) %collective-permute-start.7) | collective-permute-done | bytes 1769504 | tf_op jit(solution)/shard_map/ppermute | solution.py:245
  120.4 1.2 fusion.4
  121.7 6.5 %collective-permute-start.8 = (bf16[3,2,2,96,128]{4,3,2,1,0:T(8,128)(2,1)S(1)}, bf16[3,2,2,96,128]{4,3,2,1,0:T(8,128)(2,1)S(1)}, u32[]{:S(2)}, u32[]{:S(2)}) collective-permute-start(bf16[3,2,2,96,128]{4,3,2,1,0:T(8,128)(2,1)S(1)} %get-tuple-element.25), channel_id=1, source_target_pairs={{0,64},{64,128},{128,192},{192,256},{256,320},{320,384},{384,448},... | collective-permute-start | bytes 884744 | tf_op jit(solution)/shard_map/ppermute | solution.py:277
  128.2 1.9 collective-permute-start.9
  130.1 0.0 copy-done
  130.1 0.1 fusion.10
  130.2 4.8 %collective-permute-done.8 = bf16[3,2,2,96,128]{4,3,2,1,0:T(8,128)(2,1)S(1)} collective-permute-done((bf16[3,2,2,96,128]{4,3,2,1,0:T(8,128)(2,1)S(1)}, bf16[3,2,2,96,128]{4,3,2,1,0:T(8,128)(2,1)S(1)}, u32[]{:S(2)}, u32[]{:S(2)}) %collective-permute-start.8) | collective-permute-done | bytes 294944 | tf_op jit(solution)/shard_map/ppermute | solution.py:277
  134.9 6.2 %collective-permute-done.9 = bf16[3,2,2,96,128]{4,3,2,1,0:T(8,128)(2,1)S(1)} collective-permute-done((bf16[3,2,2,96,128]{4,3,2,1,0:T(8,128)(2,1)S(1)}, bf16[3,2,2,96,128]{4,3,2,1,0:T(8,128)(2,1)S(1)}, u32[]{:S(2)}, u32[]{:S(2)}) %collective-permute-start.9) | collective-permute-done | bytes 294944 | tf_op jit(solution)/shard_map/ppermute | solution.py:276
  141.2 0.1 fusion.9
  141.3 0.1 pad_maximum_fusion.2
  141.3 5.1 %collective-permute-start.10 = (bf16[4,2,2,96,128]{4,3,2,1,0:T(8,128)(2,1)S(1)}, bf16[4,2,2,96,128]{4,3,2,1,0:T(8,128)(2,1)S(1)}, u32[]{:S(2)}, u32[]{:S(2)}) collective-permute-start(bf16[4,2,2,96,128]{4,3,2,1,0:T(8,128)(2,1)S(1)} %pad_maximum_fusion.2), channel_id=1, source_target_pairs={{8,16},{16,8},{40,48},{48,40},{0,56},{56,0},{32,24},{24,32},{9,17}... | collective-permute-start | bytes 1179656 | tf_op jit(solution)/shard_map/ppermute | solution.py:281
  146.4 8.5 %collective-permute-done.10 = bf16[4,2,2,96,128]{4,3,2,1,0:T(8,128)(2,1)S(1)} collective-permute-done((bf16[4,2,2,96,128]{4,3,2,1,0:T(8,128)(2,1)S(1)}, bf16[4,2,2,96,128]{4,3,2,1,0:T(8,128)(2,1)S(1)}, u32[]{:S(2)}, u32[]{:S(2)}) %collective-permute-start.10) | collective-permute-done | bytes 393248 | tf_op jit(solution)/shard_map/ppermute | solution.py:281
  154.9 0.1 fusion.15
  155.0 0.2 fusion.6
  155.2 0.2 add_convert_fusion.3
  155.4 0.1 pad_maximum_fusion.1
  155.5 0.1 pad_maximum_fusion
  155.6 40.8 %all_to_all.15.in_ref = bf16[16,3,96,128]{3,2,1,0:T(8,128)(2,1)} all-to-all(bf16[16,3,96,128]{3,2,1,0:T(8,128)(2,1)S(1)} %pad_maximum_fusion), channel_id=1, replica_groups=mesh['yl'=2,'x'=4,'zh'=2,'zm'=2,'zl'=2,'yhh'=2,'yhl'=2,'c'=2] {'zh','yhh..., dimensions={0} | all-to-all | bytes 2359296 | tf_op jit(solution)/shard_map/all_to_all | solution.py:241
  196.4 2.6 %shard_map.79 = (bf16[96,2048]{1,0:T(8,128)(2,1)}, bf16[96,2048]{1,0:T(8,128)(2,1)}, bf16[96,2048]{1,0:T(8,128)(2,1)}) custom-call(s32[1]{0:T(128)} %bitcast.zm_ref, bf16[16,3,96,128]{3,2,1,0:T(8,128)(2,1)} %all_to_all.15.in_ref), custom_call_target="tpu_custom_call" | custom-call | bytes 2359296 | tf_op jit(solution)/shard_map/pallas_call | solution.py:62
  (6 shorter events, 0.1 us)
Async XLA Ops:
  2.8 42.2 %all-to-all-start = ((bf16[16,2,96,128]{3,2,1,0:T(8,128)(2,1)}), bf16[16,2,96,128]{3,2,1,0:T(8,128)(2,1)S(1)}, u32[]{:S(2)}, u32[]{:S(2)}) async-start(bf16[16,2,96,128]{3,2,1,0:T(8,128)(2,1)} %shard_map.76), calls=%async_computation | async-start | bytes 1572864 | tf_op jit(solution)/shard_map/all_to_all | solution.py:241
  45.1 12.3 %collective-permute-start.1 = (bf16[4,2,2,96,128]{4,3,2,1,0:T(8,128)(2,1)S(1)}, bf16[4,2,2,96,128]{4,3,2,1,0:T(8,128)(2,1)S(1)}, u32[]{:S(2)}, u32[]{:S(2)}) collective-permute-start(bf16[4,2,2,96,128]{4,3,2,1,0:T(8,128)(2,1)S(1)} %dynamic-slice_bitcast_fusion), channel_id=1, source_target_pairs={{8,16},{16,8},{40,48},{48,40},{0,56},{56,0},{32,24},{24,32},{9,17}... | collective-permute-start | bytes 1179656 | tf_op jit(solution)/shard_map/ppermute | solution.py:262
  49.6 43.1 %copy-start.1 = (s32[16,2]{0,1:T(2,128)S(1)}, s32[16,2]{0,1:T(2,128)}, u32[]{:S(2)}) copy-start(s32[16,2]{0,1:T(2,128)} %param.9) | copy-start | bytes 388
  57.4 36.9 %all-to-all-start.1 = ((bf16[16,2,96,128]{3,2,1,0:T(8,128)(2,1)}), bf16[16,2,96,128]{3,2,1,0:T(8,128)(2,1)S(1)}, u32[]{:S(2)}, u32[]{:S(2)}) async-start(bf16[16,2,96,128]{3,2,1,0:T(8,128)(2,1)} %shard_map.77), calls=%async_computation.1 | async-start | bytes 1572864 | tf_op jit(solution)/shard_map/all_to_all | solution.py:241
  66.5 26.3 %collective-permute-start = (bf16[4,2,2,2,96,128]{5,4,3,2,1,0:T(8,128)(2,1)S(1)}, bf16[4,2,2,2,96,128]{5,4,3,2,1,0:T(8,128)(2,1)S(1)}, u32[]{:S(2)}, u32[]{:S(2)}) collective-permute-start(bf16[4,2,2,2,96,128]{5,4,3,2,1,0:T(8,128)(2,1)S(1)} %bitcast.68), channel_id=1, source_target_pairs={{0,1},{1,0},{2,3},{3,2},{4,5},{5,4},{6,7},{7,6},{8,9},{9,8},{10,11... | collective-permute-start | bytes 2359304 | tf_op jit(solution)/shard_map/ppermute | solution.py:245
  68.6 19.9 %collective-permute-start.3 = (bf16[3,2,2,96,128]{4,3,2,1,0:T(8,128)(2,1)S(1)}, bf16[3,2,2,96,128]{4,3,2,1,0:T(8,128)(2,1)S(1)}, u32[]{:S(2)}, u32[]{:S(2)}) collective-permute-start(bf16[3,2,2,96,128]{4,3,2,1,0:T(8,128)(2,1)S(1)} %pad_maximum_fusion.3), channel_id=1, source_target_pairs={{0,64},{64,128},{128,192},{192,256},{256,320},{320,384},{384,448},... | collective-permute-start | bytes 884744 | tf_op jit(solution)/shard_map/ppermute | solution.py:267
  70.5 19.8 %collective-permute-start.5 = (bf16[3,2,2,96,128]{4,3,2,1,0:T(8,128)(2,1)S(1)}, bf16[3,2,2,96,128]{4,3,2,1,0:T(8,128)(2,1)}, u32[]{:S(2)}, u32[]{:S(2)}) collective-permute-start(bf16[3,2,2,96,128]{4,3,2,1,0:T(8,128)(2,1)S(1)} %pad_maximum_fusion.4), channel_id=1, source_target_pairs={{64,0},{128,64},{192,128},{256,192},{320,256},{384,320},{448,384},... | collective-permute-start | bytes 884744 | tf_op jit(solution)/shard_map/ppermute | solution.py:266
  74.5 18.4 %collective-permute-start.2 = (bf16[4,2,2,96,128]{4,3,2,1,0:T(8,128)(2,1)S(1)}, bf16[4,2,2,96,128]{4,3,2,1,0:T(8,128)(2,1)S(1)}, u32[]{:S(2)}, u32[]{:S(2)}) collective-permute-start(bf16[4,2,2,96,128]{4,3,2,1,0:T(8,128)(2,1)S(1)} %collective-permute-done.1.side), channel_id=1, source_target_pairs={{0,1},{1,0},{2,3},{3,2},{4,5},{5,4},{6,7},{7,6},{8,9},{9,8},{10,11... | collective-permute-start | bytes 1179656 | tf_op jit(solution)/shard_map/ppermute | solution.py:245
  88.4 4.5 %collective-permute-start.4 = (bf16[3,2,2,96,128]{4,3,2,1,0:T(8,128)(2,1)S(1)}, bf16[3,2,2,96,128]{4,3,2,1,0:T(8,128)(2,1)}, u32[]{:S(2)}, u32[]{:S(2)}) collective-permute-start(bf16[3,2,2,96,128]{4,3,2,1,0:T(8,128)(2,1)S(1)} %collective-permute-done.3.prev), channel_id=1, source_target_pairs={{0,1},{1,0},{2,3},{3,2},{4,5},{5,4},{6,7},{7,6},{8,9},{9,8},{10,11... | collective-permute-start | bytes 884744 | tf_op jit(solution)/shard_map/ppermute | solution.py:245
  90.3 3.9 %collective-permute-start.6 = (bf16[3,2,2,96,128]{4,3,2,1,0:T(8,128)(2,1)}, bf16[3,2,2,96,128]{4,3,2,1,0:T(8,128)(2,1)}, u32[]{:S(2)}, u32[]{:S(2)}) collective-permute-start(bf16[3,2,2,96,128]{4,3,2,1,0:T(8,128)(2,1)} %collective-permute-done.5.nxt), channel_id=1, source_target_pairs={{0,1},{1,0},{2,3},{3,2},{4,5},{5,4},{6,7},{7,6},{8,9},{9,8},{10,11... | collective-permute-start | bytes 884744 | tf_op jit(solution)/shard_map/ppermute | solution.py:245
  114.5 15.6 %copy-start = (bf16[6,3,2,2,96,128]{5,4,3,2,1,0:T(8,128)(2,1)S(1)}, bf16[6,3,2,2,96,128]{5,4,3,2,1,0:T(8,128)(2,1)}, u32[]{:S(2)}) copy-start(bf16[6,3,2,2,96,128]{5,4,3,2,1,0:T(8,128)(2,1)} %get-tuple-element.13) | copy-start | bytes 5308420
  114.5 5.9 %collective-permute-start.7 = (bf16[6,3,2,2,96,128]{5,4,3,2,1,0:T(8,128)(2,1)}, bf16[6,3,2,2,96,128]{5,4,3,2,1,0:T(8,128)(2,1)S(1)}, u32[]{:S(2)}, u32[]{:S(2)}) collective-permute-start(bf16[6,3,2,2,96,128]{5,4,3,2,1,0:T(8,128)(2,1)} %get-tuple-element.14), channel_id=1, source_target_pairs={{0,1},{1,0},{2,3},{3,2},{4,5},{5,4},{6,7},{7,6},{8,9},{9,8},{10,11... | collective-permute-start | bytes 5308424 | tf_op jit(solution)/shard_map/ppermute | solution.py:245
  121.7 13.3 %collective-permute-start.8 = (bf16[3,2,2,96,128]{4,3,2,1,0:T(8,128)(2,1)S(1)}, bf16[3,2,2,96,128]{4,3,2,1,0:T(8,128)(2,1)S(1)}, u32[]{:S(2)}, u32[]{:S(2)}) collective-permute-start(bf16[3,2,2,96,128]{4,3,2,1,0:T(8,128)(2,1)S(1)} %get-tuple-element.25), channel_id=1, source_target_pairs={{0,64},{64,128},{128,192},{192,256},{256,320},{320,384},{384,448},... | collective-permute-start | bytes 884744 | tf_op jit(solution)/shard_map/ppermute | solution.py:277
  128.2 13.0 %collective-permute-start.9 = (bf16[3,2,2,96,128]{4,3,2,1,0:T(8,128)(2,1)S(1)}, bf16[3,2,2,96,128]{4,3,2,1,0:T(8,128)(2,1)S(1)}, u32[]{:S(2)}, u32[]{:S(2)}) collective-permute-start(bf16[3,2,2,96,128]{4,3,2,1,0:T(8,128)(2,1)S(1)} %get-tuple-element.26), channel_id=1, source_target_pairs={{64,0},{128,64},{192,128},{256,192},{320,256},{384,320},{448,384},... | collective-permute-start | bytes 884744 | tf_op jit(solution)/shard_map/ppermute | solution.py:276
  141.3 13.6 %collective-permute-start.10 = (bf16[4,2,2,96,128]{4,3,2,1,0:T(8,128)(2,1)S(1)}, bf16[4,2,2,96,128]{4,3,2,1,0:T(8,128)(2,1)S(1)}, u32[]{:S(2)}, u32[]{:S(2)}) collective-permute-start(bf16[4,2,2,96,128]{4,3,2,1,0:T(8,128)(2,1)S(1)} %pad_maximum_fusion.2), channel_id=1, source_target_pairs={{8,16},{16,8},{40,48},{48,40},{0,56},{56,0},{32,24},{24,32},{9,17}... | collective-permute-start | bytes 1179656 | tf_op jit(solution)/shard_map/ppermute | solution.py:281

commit v3 on v2

--- a/solution.py
+++ b/solution.py
@@ -74,7 +74,7 @@
 
 def attention_kernel(
     zm_ref, chip_ref, line_ref, window_ref, own, own_s, side, side_s, prev, prev_s, nxt, nxt_s, qg,
-    dq_out, mine_out, sib_out,
+    dq_out, mine_out, sib_edge, sib_mid,
     k_buf, v_buf, q_buf, g_buf, dk_acc, dv_acc, s_main, s_side, p_main, p_side, sems,
 ):
     zm, line = zm_ref[0], line_ref[0]
@@ -91,26 +91,24 @@
         copies.append(c)
 
     for kv, buf, part in ((0, k_buf, q_buf), (1, v_buf, g_buf)):
-        for row in (0, 1):
-            copy(qg.at[:, zls[row], :, kv], part.at[:, row])
+        copy(qg.at[:, :, :, kv], part)
         for core, (o, h, p, n) in enumerate(((own, side, prev, nxt), (own_s, side_s, prev_s, nxt_s))):
-            for row in (0, 1):
-                copy(o.at[:, zls[row], :, kv], buf.at[pl.ds(1, 4), row, core])
-                copy(p.at[zls[row], :, kv], buf.at[0, row, core])
-                copy(n.at[zls[row], :, kv], buf.at[5, row, core])
+            copy(o.at[:, :, :, kv], buf.at[pl.ds(1, 4), pl.ds(0, 2), core])
             copy(h.at[:, :, kv], buf.at[pl.ds(1, 4), 2, core])
-            copy(p.at[2, :, kv], buf.at[0, 2, core])
-            copy(n.at[2, :, kv], buf.at[5, 2, core])
-    dk_acc[0:2] = jnp.zeros((2,) + dk_acc.shape[1:], F32)
-    dv_acc[0:2] = jnp.zeros((2,) + dv_acc.shape[1:], F32)
-    for c in copies:
+            copy(p.at[:, :, kv], buf.at[0, :, core])
+            copy(n.at[:, :, kv], buf.at[5, :, core])
+    for c in copies[: len(copies) // 2]:
         c.wait()
 
     scale2 = HD ** (-0.5) * 1.4426950408889634
     row_bias = jnp.where(reach_h >= 1, 0.0, NEG).astype(F32)
 
     def keys(buf, col):
-        return buf[col, 0:2].reshape(2 * TILE, HD), buf[col, 2].reshape(TILE, HD)
+        edge, inner, side = (buf[col, row].reshape(TILE, HD) for row in (*zls, 2))
+        return jnp.concatenate([edge, inner], axis=0), side
+
+    def queries(buf, time):
+        return jnp.concatenate([buf[time, zl].reshape(HALF, HD) for zl in zls], axis=0)
 
     def lanes(j):
         return slice(j * 128, (j + 1) * 128)
@@ -119,36 +117,42 @@
         block = (block * (1.0 if kv else HD ** (-0.5))).astype(BF).T
         for row in range(3):
             place = 2 if row == 2 else zls[row]
-            for core, out in ((0, mine_out), (1, sib_out)):
+            sib, at = (sib_edge, col // 5) if col in (0, 5) else (sib_mid, col - 1)
+            for core, out, at in ((0, mine_out, col), (1, sib, at)):
                 for yhl in (0, 1):
                     start = row * TILE + core * HALF + yhl * PIECE
-                    out[col, place, yhl, kv] = block[start : start + PIECE]
-
-    def one_time(time, carry):
-        q = q_buf[time].reshape(TILE, HD)
-        g = g_buf[time].reshape(TILE, HD)
-        q1, g1 = q[HALF:], g[HALF:]
-        tops = [jnp.full((HALF, 128), NEG, F32)] * 2
-        for d in range(3):
-            col = time + d
-            allowed = (col >= first_col) & (col <= last_col) & ((reach_t >= 1) | (d == 1))
-            time_bias = jnp.where(allowed, 0.0, NEG).astype(F32)
-            far_bias = time_bias + row_bias
-            k01, k2 = keys(k_buf, col)
-            s = dot(q, k01, ((1,), (1,))) * scale2
-            for half in (0, 1):
-                for j in range(6):
-                    part = s[half * HALF : (half + 1) * HALF, lanes(j)]
-                    if j // 3 != half:
-                        part = part + far_bias
-                    elif d != 1:
-                        part = part + time_bias
-                    s_main[d, half * HALF : (half + 1) * HALF, lanes(j)] = part
-                    tops[half] = jnp.maximum(tops[half], part)
-            s = dot(q1, k2, ((1,), (1,))) * scale2 + far_bias
-            s_side[d] = s
-            for j in range(3):
-                tops[1] = jnp.maximum(tops[1], s[:, lanes(j)])
+                    out[at, place, yhl, kv] = block[start : start + PIECE]
+
+    def scores(time, d, slot, tops):
+        col = time + d
+        allowed = (col >= first_col) & (col <= last_col) & ((reach_t >= 1) | (d == 1))
+        time_bias = jnp.where(allowed, 0.0, NEG).astype(F32)
+        far_bias = time_bias + row_bias
+        tops = list(tops)
+        q = queries(q_buf, time)
+        k01, k2 = keys(k_buf, col)
+        s = dot(q, k01, ((1,), (1,))) * scale2
+        for half in (0, 1):
+            for j in range(6):
+                part = s[half * HALF : (half + 1) * HALF, lanes(j)]
+                if j // 3 != half:
+                    part = part + far_bias
+                elif d != 1:
+                    part = part + time_bias
+                s_main[slot, d, half * HALF : (half + 1) * HALF, lanes(j)] = part
+                tops[half] = jnp.maximum(tops[half], part)
+        s = dot(q[HALF:], k2, ((1,), (1,))) * scale2 + far_bias
+        s_side[slot, d] = s
+        for j in range(3):
+            tops[1] = jnp.maximum(tops[1], s[:, lanes(j)])
+        return tuple(tops)
+
+    no_tops = (jnp.full((HALF, 128), NEG, F32),) * 2
+
+    def one_time(time, slot, tops, after):
+        q = queries(q_buf, time)
+        g = queries(g_buf, time)
+        g1 = g[HALF:]
         tops = [jnp.max(t, axis=1, keepdims=True) for t in tops]
         top = jnp.concatenate(tops, axis=0)
         total = jnp.zeros((TILE, 128), F32)
@@ -160,15 +164,15 @@
             p = dot(g, v01, ((1,), (1,)))
             p_main[d] = p
             for j in range(6):
-                e = jnp.exp2(s_main[d, :, lanes(j)] - top)
-                s_main[d, :, lanes(j)] = e
+                e = jnp.exp2(s_main[slot, d, :, lanes(j)] - top)
+                s_main[slot, d, :, lanes(j)] = e
                 total += e
                 delta += e * p[:, lanes(j)]
             p = dot(g1, v2, ((1,), (1,)))
             p_side[d] = p
             for j in range(3):
-                e = jnp.exp2(s_side[d, :, lanes(j)] - tops[1])
-                s_side[d, :, lanes(j)] = e
+                e = jnp.exp2(s_side[slot, d, :, lanes(j)] - tops[1])
+                s_side[slot, d, :, lanes(j)] = e
                 total1 += e
                 delta1 += e * p[:, lanes(j)]
         total = jnp.concatenate([total[:HALF], total[HALF:] + total1], axis=0)
@@ -179,31 +183,43 @@
         qt1, gt1 = qt[:, HALF:], gt[:, HALF:]
         dq = jnp.zeros((TILE, HD), F32)
         dq1 = jnp.zeros((HALF, HD), F32)
+        next_tops = no_tops
         for d in range(3):
             col = time + d
+            if after is not None:
+                next_tops = scores(after, d, 1 - slot, next_tops)
             k01, k2 = keys(k_buf, col)
-            w = s_main[d] * inverse
+            w = s_main[slot, d] * inverse
             ds = (w * (p_main[d] - delta)).astype(BF)
-            w1 = s_side[d] * inverse[HALF:]
+            w1 = s_side[slot, d] * inverse[HALF:]
             ds1 = (w1 * (p_side[d] - delta[HALF:])).astype(BF)
             dq += dot(ds, k01, ((1,), (0,)))
             dq1 += dot(ds1, k2, ((1,), (0,)))
-            for kv, acc, main, last in ((0, dk_acc, dot(qt, ds, ((1,), (0,))), dot(qt1, ds1, ((1,), (0,)))),
-                                  (1, dv_acc, dot(gt, w.astype(BF), ((1,), (0,))), dot(gt1, w1.astype(BF), ((1,), (0,))))):
-                if d == 2:
+            main_k, last_k = dot(qt, ds, ((1,), (0,))), dot(qt1, ds1, ((1,), (0,)))
+            main_v, last_v = dot(gt, w.astype(BF), ((1,), (0,))), dot(gt1, w1.astype(BF), ((1,), (0,)))
+            for kv, acc, main, last in ((0, dk_acc, main_k, last_k), (1, dv_acc, main_v, last_v)):
+                if d == 2 or (time == 0 and d == 1):
                     acc[col, :, 0 : 2 * TILE] = main
                     acc[col, :, 2 * TILE :] = last
                 elif d == 1:
                     acc[col, :, 0 : 2 * TILE] += main
                     acc[col, :, 2 * TILE :] += last
                 else:
-                    finish(col, kv, acc[col] + jnp.concatenate([main, last], axis=1))
-        dq = jnp.concatenate([dq[:HALF], dq[HALF:] + dq1], axis=0) * (HD ** (-0.5))
+                    block = jnp.concatenate([main, last], axis=1)
+                    finish(col, kv, block if time == 0 else block + acc[col])
+        dq = jnp.concatenate([dq[:HALF], dq[HALF:] + dq1], axis=0) * HD ** (-0.5)
         for row in (0, 1):
             dq_out[time, zls[row]] = dq[row * HALF : (row + 1) * HALF].astype(BF).reshape(2, PIECE, HD)
-        return carry
-
-    lax.fori_loop(0, 4, one_time, 0, unroll=1)
+        return next_tops
+
+    tops = no_tops
+    for d in range(3):
+        tops = scores(0, d, 0, tops)
+    for c in copies[len(copies) // 2 :]:
+        c.wait()
+
+    for time in range(4):
+        tops = one_time(time, time % 2, tops, time + 1 if time < 3 else None)
     for col in (4, 5):
         finish(col, 0, dk_acc[col])
         finish(col, 1, dv_acc[col])
@@ -215,10 +231,11 @@
         out_shape=[
             jax.ShapeDtypeStruct((4, 2, 2, PIECE, HD), BF),
             jax.ShapeDtypeStruct((6, 3, 2, 2, PIECE, HD), BF),
-            jax.ShapeDtypeStruct((6, 3, 2, 2, PIECE, HD), BF),
+            jax.ShapeDtypeStruct((2, 3, 2, 2, PIECE, HD), BF),
+            jax.ShapeDtypeStruct((4, 3, 2, 2, PIECE, HD), BF),
         ],
         in_specs=[pl.BlockSpec(memory_space=pltpu.SMEM)] * 4 + [pl.BlockSpec(memory_space=pl.ANY)] * 9,
-        out_specs=[pl.BlockSpec(memory_space=pltpu.VMEM)] * 3,
+        out_specs=[pl.BlockSpec(memory_space=pltpu.VMEM)] * 4,
         scratch_shapes=[
             pltpu.VMEM((6, 3, 2, 2, PIECE, HD), BF),
             pltpu.VMEM((6, 3, 2, 2, PIECE, HD), BF),
@@ -226,11 +243,11 @@
             pltpu.VMEM((4, 2, 2, PIECE, HD), BF),
             pltpu.VMEM((6, HD, 3 * TILE), F32),
             pltpu.VMEM((6, HD, 3 * TILE), F32),
+            pltpu.VMEM((2, 3, TILE, 2 * TILE), F32),
+            pltpu.VMEM((2, 3, HALF, TILE), F32),
             pltpu.VMEM((3, TILE, 2 * TILE), F32),
             pltpu.VMEM((3, HALF, TILE), F32),
-            pltpu.VMEM((3, TILE, 2 * TILE), F32),
-            pltpu.VMEM((3, HALF, TILE), F32),
-            pltpu.SemaphoreType.DMA((40,)),
+            pltpu.SemaphoreType.DMA((18,)),
         ],
         compiler_params=pltpu.CompilerParams(vmem_limit_bytes=48 * 1024 * 1024),
         cost_estimate=pl.CostEstimate(flops=6 * 10**9, bytes_accessed=9 * 10**6, transcendentals=5 * 10**6),
@@ -265,16 +282,20 @@
     own_s = swapped(own)
     nxt = lax.ppermute(jnp.concatenate([own[0], side[:1]], axis=0), LINE, BACK)
     prev = lax.ppermute(jnp.concatenate([own[3], side[3:]], axis=0), LINE, FORTH)
-    dq, mine, sib = attention(
+    dq, mine, sib_edge, sib_mid = attention(
         zm_arg, chip, line, window, own, own_s, side, swapped(side), prev, swapped(prev), nxt, swapped(nxt), qg
     )
-    sib = swapped(sib)
-
-    def terms(*at):
-        return mine[at].astype(F32) + sib[at].astype(F32)
-
-    to_last = lax.ppermute(terms(0).astype(BF), LINE, BACK)
-    to_first = lax.ppermute(terms(5).astype(BF), LINE, FORTH)
+    sib_edge = swapped(sib_edge)
+    d_prev = (mine[0].astype(F32) + sib_edge[0].astype(F32)).astype(BF)
+    d_nxt = (mine[5].astype(F32) + sib_edge[1].astype(F32)).astype(BF)
+    sib_mid, d_prev, d_nxt = lax.optimization_barrier((sib_mid, d_prev, d_nxt))
+    to_last = lax.ppermute(d_prev, LINE, BACK)
+    to_first = lax.ppermute(d_nxt, LINE, FORTH)
+    sib_mid = swapped(sib_mid)
+
+    def terms(col, *at):
+        return mine[col, *at].astype(F32) + sib_mid[col - 1, *at].astype(F32)
+
     d_side = [terms(time + 1, 2) for time in range(4)]
     d_side[0] += to_first[2].astype(F32)
     d_side[3] += to_last[2].astype(F32)

time: 200 us -> 197 us (0.985)
  Pallas kernels: 27.2 us -> 24.4 us
  waiting for transfers between devices: 70.8 us -> 68.4 us
  starting transfers between devices: 57 us -> 59.3 us
    pallas_call x1, Pallas kernels: 20.2 us -> 17.4 us  [attention(): pl.pallas_call(attention_kernel, out_shape=[jax.ShapeDtypeStruct((4, 2, 2...]
    ppermute x5 -> x6, starting transfers between devices: 10.6 us -> 12.9 us  [swapped(): return lax.ppermute(block, 'c', SWAP)]
    ppermute x5 -> x6, waiting for transfers between devices: 4.92 us -> 3.03 us  [swapped(): return lax.ppermute(block, 'c', SWAP)]
  transfers between devices with their start and end apart: 13 -> 14, of which waited for: 8 -> 8; matrix products, arithmetic and copies ran while one was open for 0% -> 0% of each run, Pallas kernels for 1% -> 1%
where the time goes in v3:
time: 197 us; the launch traced here: 196 us
  waiting for transfers between devices  68.4 us (35%)
  starting transfers between devices  59.3 us (30%)
  blocking collectives  40.9 us (21%)
  Pallas kernels  24.4 us (12%)
  other arithmetic  2.16 us (1%)
    all_to_all x1, blocking collectives, to_heads(): lax.all_to_all(blocks, GROUP, split_axis=0, concat_axis=0, tiled=True)  40.9 us
    all_to_all x2, waiting for transfers between devices, to_heads(): lax.all_to_all(blocks, GROUP, split_axis=0, concat_axis=0, tiled=True)  26.6 us
    all_to_all x2, starting transfers between devices, to_heads(): lax.all_to_all(blocks, GROUP, split_axis=0, concat_axis=0, tiled=True)  24.8 us
    pallas_call x1, Pallas kernels, attention(): pl.pallas_call(attention_kernel, out_shape=[jax.ShapeDtypeStruct((4, 2, 2...  17.4 us
    ppermute x6, starting transfers between devices, swapped(): return lax.ppermute(block, 'c', SWAP)  12.9 us
    ppermute x1, waiting for transfers between devices, per_device(): lax.ppermute(jnp.concatenate([own[3], side[3:]], axis=0), LINE, FORTH)  12 us
    ppermute x1, waiting for transfers between devices, per_device(): to_inner = lax.ppermute(jnp.stack(d_side).astype(BF), Z, Z_PAIRS)  8.23 us
    ppermute x1, waiting for transfers between devices, per_device(): side = lax.ppermute(inner, Z, Z_PAIRS)  7.8 us
  transfers between devices with their start and end apart: 14, of which 8 were waited for; matrix products, arithmetic and copies ran while one was open for 0% of the time, Pallas kernels for 1%

profile of v3, /device:TPU:6, one launch (start us, length us, event | category | flops | bytes accessed | tf_op | source)
XLA Modules:
  0.0 196.2 jit_solution(9133411704479935844)
XLA Ops:
  0.6 2.2 %shard_map.76 = bf16[16,2,96,128]{3,2,1,0:T(8,128)(2,1)} custom-call(s32[1]{0:T(128)} %bitcast.zm_ref, bf16[96,2048]{1,0:T(8,128)(2,1)} %a_ref.2, bf16[96,2048]{1,0:T(8,128)(2,1)} %b_ref.2), custom_call_target="tpu_custom_call" | custom-call | bytes 1572864 | tf_op jit(solution)/shard_map/pallas_call | solution.py:43
  2.8 15.7 %all-to-all-start = ((bf16[16,2,96,128]{3,2,1,0:T(8,128)(2,1)}), bf16[16,2,96,128]{3,2,1,0:T(8,128)(2,1)S(1)}, u32[]{:S(2)}, u32[]{:S(2)}) async-start(bf16[16,2,96,128]{3,2,1,0:T(8,128)(2,1)} %shard_map.76), calls=%async_computation | async-start | bytes 1572864 | tf_op jit(solution)/shard_map/all_to_all | solution.py:258
  18.5 26.6 %all-to-all-done = bf16[16,2,96,128]{3,2,1,0:T(8,128)(2,1)S(1)} async-done(((bf16[16,2,96,128]{3,2,1,0:T(8,128)(2,1)}), bf16[16,2,96,128]{3,2,1,0:T(8,128)(2,1)S(1)}, u32[]{:S(2)}, u32[]{:S(2)}) %all-to-all-start) | async-done | bytes 786464 | tf_op jit(solution)/shard_map/all_to_all | solution.py:258
  45.1 2.3 %collective-permute-start.1 = (bf16[4,2,2,96,128]{4,3,2,1,0:T(8,128)(2,1)S(1)}, bf16[4,2,2,96,128]{4,3,2,1,0:T(8,128)(2,1)S(1)}, u32[]{:S(2)}, u32[]{:S(2)}) collective-permute-start(bf16[4,2,2,96,128]{4,3,2,1,0:T(8,128)(2,1)S(1)} %dynamic-slice_bitcast_fusion), channel_id=1, source_target_pairs={{8,16},{16,8},{40,48},{48,40},{0,56},{56,0},{32,24},{24,32},{9,17}... | collective-permute-start | bytes 1179656 | tf_op jit(solution)/shard_map/ppermute | solution.py:279
  47.4 2.2 %shard_map.77 = bf16[16,2,96,128]{3,2,1,0:T(8,128)(2,1)} custom-call(s32[1]{0:T(128)} %bitcast.zm_ref, bf16[96,2048]{1,0:T(8,128)(2,1)} %a_ref.3, bf16[96,2048]{1,0:T(8,128)(2,1)} %b_ref.3), custom_call_target="tpu_custom_call" | custom-call | bytes 1572864 | tf_op jit(solution)/shard_map/pallas_call | solution.py:43
  49.6 7.8 %collective-permute-done.1.side = bf16[4,2,2,96,128]{4,3,2,1,0:T(8,128)(2,1)S(1)} collective-permute-done((bf16[4,2,2,96,128]{4,3,2,1,0:T(8,128)(2,1)S(1)}, bf16[4,2,2,96,128]{4,3,2,1,0:T(8,128)(2,1)S(1)}, u32[]{:S(2)}, u32[]{:S(2)}) %collective-permute-start.1) | collective-permute-done | bytes 393248 | tf_op jit(solution)/shard_map/ppermute | solution.py:279
  57.4 9.1 %all-to-all-start.1 = ((bf16[16,2,96,128]{3,2,1,0:T(8,128)(2,1)}), bf16[16,2,96,128]{3,2,1,0:T(8,128)(2,1)S(1)}, u32[]{:S(2)}, u32[]{:S(2)}) async-start(bf16[16,2,96,128]{3,2,1,0:T(8,128)(2,1)} %shard_map.77), calls=%async_computation.1 | async-start | bytes 1572864 | tf_op jit(solution)/shard_map/all_to_all | solution.py:258
  66.5 0.0 copy-start.1
  66.6 1.9 collective-permute-start
  68.6 1.9 collective-permute-start.3
  70.5 3.9 %collective-permute-start.5 = (bf16[3,2,2,96,128]{4,3,2,1,0:T(8,128)(2,1)S(1)}, bf16[3,2,2,96,128]{4,3,2,1,0:T(8,128)(2,1)}, u32[]{:S(2)}, u32[]{:S(2)}) collective-permute-start(bf16[3,2,2,96,128]{4,3,2,1,0:T(8,128)(2,1)S(1)} %pad_maximum_fusion.4), channel_id=1, source_target_pairs={{64,0},{128,64},{192,128},{256,192},{320,256},{384,320},{448,384},... | collective-permute-start | bytes 884744 | tf_op jit(solution)/shard_map/ppermute | solution.py:283
  74.5 1.9 collective-permute-start.2
  76.4 12.0 %collective-permute-done.3.prev = bf16[3,2,2,96,128]{4,3,2,1,0:T(8,128)(2,1)S(1)} collective-permute-done((bf16[3,2,2,96,128]{4,3,2,1,0:T(8,128)(2,1)S(1)}, bf16[3,2,2,96,128]{4,3,2,1,0:T(8,128)(2,1)S(1)}, u32[]{:S(2)}, u32[]{:S(2)}) %collective-permute-start.3) | collective-permute-done | bytes 294944 | tf_op jit(solution)/shard_map/ppermute | solution.py:284
  88.4 1.9 collective-permute-start.4
  90.3 0.0 collective-permute-done.5.nxt
  90.3 2.4 %collective-permute-start.6 = (bf16[3,2,2,96,128]{4,3,2,1,0:T(8,128)(2,1)}, bf16[3,2,2,96,128]{4,3,2,1,0:T(8,128)(2,1)}, u32[]{:S(2)}, u32[]{:S(2)}) collective-permute-start(bf16[3,2,2,96,128]{4,3,2,1,0:T(8,128)(2,1)} %collective-permute-done.5.nxt), channel_id=1, source_target_pairs={{0,1},{1,0},{2,3},{3,2},{4,5},{5,4},{6,7},{7,6},{8,9},{9,8},{10,11... | collective-permute-start | bytes 884744 | tf_op jit(solution)/shard_map/ppermute | solution.py:262
  92.8 0.0 copy-done.1
  92.8 0.1 copy.8.window_ref
  92.9 0.0 collective-permute-done.2.side_s
  92.9 0.0 collective-permute-done.own_s
  92.9 0.0 collective-permute-done.4.prev_s
  92.9 1.4 collective-permute-done.6.nxt_s
  94.3 0.0 all-to-all-done.1
  94.3 17.4 %shard_map.78 = (bf16[4,2,2,96,128]{4,3,2,1,0:T(8,128)(2,1)S(1)}, bf16[6,3,2,2,96,128]{5,4,3,2,1,0:T(8,128)(2,1)}, bf16[2,3,2,2,96,128]{5,4,3,2,1,0:T(8,128)(2,1)S(1)}, bf16[4,3,2,2,96,128]{5,4,3,2,1,0:T(8,128)(2,1)}) custom-call(s32[1]{0:T(128)} %bitcast.zm_ref, s32[1]{0:T(128)} %bitcast.1.chip_ref, s32[1]{0:T(128)} %bitcast.2.line_ref, ...), custom_call_target="tpu_custom_call" | custom-call | flops 6000000000 | bytes 9000000 | tf_op jit(solution)/shard_map/pallas_call | solution.py:229
  111.7 0.0 copy-start
  111.7 2.4 %collective-permute-start.7 = (bf16[2,3,2,2,96,128]{5,4,3,2,1,0:T(8,128)(2,1)S(1)}, bf16[2,3,2,2,96,128]{5,4,3,2,1,0:T(8,128)(2,1)S(1)}, u32[]{:S(2)}, u32[]{:S(2)}) collective-permute-start(bf16[2,3,2,2,96,128]{5,4,3,2,1,0:T(8,128)(2,1)S(1)} %get-tuple-element.19), channel_id=1, source_target_pairs={{0,1},{1,0},{2,3},{3,2},{4,5},{5,4},{6,7},{7,6},{8,9},{9,8},{10,11... | collective-permute-start | bytes 1769480 | tf_op jit(solution)/shard_map/ppermute | solution.py:262
  114.1 1.6 collective-permute-done.7
  115.7 1.2 fusion.5
  116.9 2.3 %collective-permute-start.8 = (bf16[4,3,2,2,96,128]{5,4,3,2,1,0:T(8,128)(2,1)}, bf16[4,3,2,2,96,128]{5,4,3,2,1,0:T(8,128)(2,1)S(1)}, u32[]{:S(2)}, u32[]{:S(2)}) collective-permute-start(bf16[4,3,2,2,96,128]{5,4,3,2,1,0:T(8,128)(2,1)} %get-tuple-element.20), channel_id=1, source_target_pairs={{0,1},{1,0},{2,3},{3,2},{4,5},{5,4},{6,7},{7,6},{8,9},{9,8},{10,11... | collective-permute-start | bytes 3538952 | tf_op jit(solution)/shard_map/ppermute | solution.py:262
  119.2 6.5 %collective-permute-start.9 = (bf16[3,2,2,96,128]{4,3,2,1,0:T(8,128)(2,1)S(1)}, bf16[3,2,2,96,128]{4,3,2,1,0:T(8,128)(2,1)S(1)}, u32[]{:S(2)}, u32[]{:S(2)}) collective-permute-start(bf16[3,2,2,96,128]{4,3,2,1,0:T(8,128)(2,1)S(1)} %get-tuple-element.21), channel_id=1, source_target_pairs={{0,64},{64,128},{128,192},{192,256},{256,320},{320,384},{384,448},... | collective-permute-start | bytes 884744 | tf_op jit(solution)/shard_map/ppermute | solution.py:293
  125.7 1.9 collective-permute-start.10
  127.7 0.0 collective-permute-done.8
  127.7 0.0 copy-done
  127.7 0.1 fusion.10
  127.7 4.5 %collective-permute-done.9 = bf16[3,2,2,96,128]{4,3,2,1,0:T(8,128)(2,1)S(1)} collective-permute-done((bf16[3,2,2,96,128]{4,3,2,1,0:T(8,128)(2,1)S(1)}, bf16[3,2,2,96,128]{4,3,2,1,0:T(8,128)(2,1)S(1)}, u32[]{:S(2)}, u32[]{:S(2)}) %collective-permute-start.9) | collective-permute-done | bytes 294944 | tf_op jit(solution)/shard_map/ppermute | solution.py:293
  132.3 6.2 %collective-permute-done.10 = bf16[3,2,2,96,128]{4,3,2,1,0:T(8,128)(2,1)S(1)} collective-permute-done((bf16[3,2,2,96,128]{4,3,2,1,0:T(8,128)(2,1)S(1)}, bf16[3,2,2,96,128]{4,3,2,1,0:T(8,128)(2,1)S(1)}, u32[]{:S(2)}, u32[]{:S(2)}) %collective-permute-start.10) | collective-permute-done | bytes 294944 | tf_op jit(solution)/shard_map/ppermute | solution.py:292
  138.5 0.1 fusion.9
  138.6 0.1 pad_maximum_fusion.2
  138.7 5.1 %collective-permute-start.11 = (bf16[4,2,2,96,128]{4,3,2,1,0:T(8,128)(2,1)S(1)}, bf16[4,2,2,96,128]{4,3,2,1,0:T(8,128)(2,1)S(1)}, u32[]{:S(2)}, u32[]{:S(2)}) collective-permute-start(bf16[4,2,2,96,128]{4,3,2,1,0:T(8,128)(2,1)S(1)} %pad_maximum_fusion.2), channel_id=1, source_target_pairs={{8,16},{16,8},{40,48},{48,40},{0,56},{56,0},{32,24},{24,32},{9,17}... | collective-permute-start | bytes 1179656 | tf_op jit(solution)/shard_map/ppermute | solution.py:302
  143.8 8.2 %collective-permute-done.11 = bf16[4,2,2,96,128]{4,3,2,1,0:T(8,128)(2,1)S(1)} collective-permute-done((bf16[4,2,2,96,128]{4,3,2,1,0:T(8,128)(2,1)S(1)}, bf16[4,2,2,96,128]{4,3,2,1,0:T(8,128)(2,1)S(1)}, u32[]{:S(2)}, u32[]{:S(2)}) %collective-permute-start.11) | collective-permute-done | bytes 393248 | tf_op jit(solution)/shard_map/ppermute | solution.py:302
  152.0 0.1 fusion.15
  152.1 0.2 fusion.6
  152.3 0.2 add_convert_fusion.3
  152.5 0.1 pad_maximum_fusion.1
  152.6 0.1 pad_maximum_fusion
  152.7 40.9 %all_to_all.15.in_ref = bf16[16,3,96,128]{3,2,1,0:T(8,128)(2,1)} all-to-all(bf16[16,3,96,128]{3,2,1,0:T(8,128)(2,1)S(1)} %pad_maximum_fusion), channel_id=1, replica_groups=mesh['yl'=2,'x'=4,'zh'=2,'zm'=2,'zl'=2,'yhh'=2,'yhl'=2,'c'=2] {'zh','yhh..., dimensions={0} | all-to-all | bytes 2359296 | tf_op jit(solution)/shard_map/all_to_all | solution.py:258
  193.6 2.6 %shard_map.79 = (bf16[96,2048]{1,0:T(8,128)(2,1)}, bf16[96,2048]{1,0:T(8,128)(2,1)}, bf16[96,2048]{1,0:T(8,128)(2,1)}) custom-call(s32[1]{0:T(128)} %bitcast.zm_ref, bf16[16,3,96,128]{3,2,1,0:T(8,128)(2,1)} %all_to_all.15.in_ref), custom_call_target="tpu_custom_call" | custom-call | bytes 2359296 | tf_op jit(solution)/shard_map/pallas_call | solution.py:62
  (6 shorter events, 0.1 us)
Async XLA Ops:
  2.8 42.2 %all-to-all-start = ((bf16[16,2,96,128]{3,2,1,0:T(8,128)(2,1)}), bf16[16,2,96,128]{3,2,1,0:T(8,128)(2,1)S(1)}, u32[]{:S(2)}, u32[]{:S(2)}) async-start(bf16[16,2,96,128]{3,2,1,0:T(8,128)(2,1)} %shard_map.76), calls=%async_computation | async-start | bytes 1572864 | tf_op jit(solution)/shard_map/all_to_all | solution.py:258
  45.1 12.3 %collective-permute-start.1 = (bf16[4,2,2,96,128]{4,3,2,1,0:T(8,128)(2,1)S(1)}, bf16[4,2,2,96,128]{4,3,2,1,0:T(8,128)(2,1)S(1)}, u32[]{:S(2)}, u32[]{:S(2)}) collective-permute-start(bf16[4,2,2,96,128]{4,3,2,1,0:T(8,128)(2,1)S(1)} %dynamic-slice_bitcast_fusion), channel_id=1, source_target_pairs={{8,16},{16,8},{40,48},{48,40},{0,56},{56,0},{32,24},{24,32},{9,17}... | collective-permute-start | bytes 1179656 | tf_op jit(solution)/shard_map/ppermute | solution.py:279
  57.4 36.9 %all-to-all-start.1 = ((bf16[16,2,96,128]{3,2,1,0:T(8,128)(2,1)}), bf16[16,2,96,128]{3,2,1,0:T(8,128)(2,1)S(1)}, u32[]{:S(2)}, u32[]{:S(2)}) async-start(bf16[16,2,96,128]{3,2,1,0:T(8,128)(2,1)} %shard_map.77), calls=%async_computation.1 | async-start | bytes 1572864 | tf_op jit(solution)/shard_map/all_to_all | solution.py:258
  66.5 26.2 %copy-start.1 = (s32[16,2]{0,1:T(2,128)S(1)}, s32[16,2]{0,1:T(2,128)}, u32[]{:S(2)}) copy-start(s32[16,2]{0,1:T(2,128)} %param.9) | copy-start | bytes 388
  66.6 26.3 %collective-permute-start = (bf16[4,2,2,2,96,128]{5,4,3,2,1,0:T(8,128)(2,1)S(1)}, bf16[4,2,2,2,96,128]{5,4,3,2,1,0:T(8,128)(2,1)S(1)}, u32[]{:S(2)}, u32[]{:S(2)}) collective-permute-start(bf16[4,2,2,2,96,128]{5,4,3,2,1,0:T(8,128)(2,1)S(1)} %bitcast.68), channel_id=1, source_target_pairs={{0,1},{1,0},{2,3},{3,2},{4,5},{5,4},{6,7},{7,6},{8,9},{9,8},{10,11... | collective-permute-start | bytes 2359304 | tf_op jit(solution)/shard_map/ppermute | solution.py:262
  68.6 19.8 %collective-permute-start.3 = (bf16[3,2,2,96,128]{4,3,2,1,0:T(8,128)(2,1)S(1)}, bf16[3,2,2,96,128]{4,3,2,1,0:T(8,128)(2,1)S(1)}, u32[]{:S(2)}, u32[]{:S(2)}) collective-permute-start(bf16[3,2,2,96,128]{4,3,2,1,0:T(8,128)(2,1)S(1)} %pad_maximum_fusion.3), channel_id=1, source_target_pairs={{0,64},{64,128},{128,192},{192,256},{256,320},{320,384},{384,448},... | collective-permute-start | bytes 884744 | tf_op jit(solution)/shard_map/ppermute | solution.py:284
  70.5 19.8 %collective-permute-start.5 = (bf16[3,2,2,96,128]{4,3,2,1,0:T(8,128)(2,1)S(1)}, bf16[3,2,2,96,128]{4,3,2,1,0:T(8,128)(2,1)}, u32[]{:S(2)}, u32[]{:S(2)}) collective-permute-start(bf16[3,2,2,96,128]{4,3,2,1,0:T(8,128)(2,1)S(1)} %pad_maximum_fusion.4), channel_id=1, source_target_pairs={{64,0},{128,64},{192,128},{256,192},{320,256},{384,320},{448,384},... | collective-permute-start | bytes 884744 | tf_op jit(solution)/shard_map/ppermute | solution.py:283
  74.5 18.4 %collective-permute-start.2 = (bf16[4,2,2,96,128]{4,3,2,1,0:T(8,128)(2,1)S(1)}, bf16[4,2,2,96,128]{4,3,2,1,0:T(8,128)(2,1)S(1)}, u32[]{:S(2)}, u32[]{:S(2)}) collective-permute-start(bf16[4,2,2,96,128]{4,3,2,1,0:T(8,128)(2,1)S(1)} %collective-permute-done.1.side), channel_id=1, source_target_pairs={{0,1},{1,0},{2,3},{3,2},{4,5},{5,4},{6,7},{7,6},{8,9},{9,8},{10,11... | collective-permute-start | bytes 1179656 | tf_op jit(solution)/shard_map/ppermute | solution.py:262
  88.4 4.5 %collective-permute-start.4 = (bf16[3,2,2,96,128]{4,3,2,1,0:T(8,128)(2,1)S(1)}, bf16[3,2,2,96,128]{4,3,2,1,0:T(8,128)(2,1)}, u32[]{:S(2)}, u32[]{:S(2)}) collective-permute-start(bf16[3,2,2,96,128]{4,3,2,1,0:T(8,128)(2,1)S(1)} %collective-permute-done.3.prev), channel_id=1, source_target_pairs={{0,1},{1,0},{2,3},{3,2},{4,5},{5,4},{6,7},{7,6},{8,9},{9,8},{10,11... | collective-permute-start | bytes 884744 | tf_op jit(solution)/shard_map/ppermute | solution.py:262
  90.3 3.9 %collective-permute-start.6 = (bf16[3,2,2,96,128]{4,3,2,1,0:T(8,128)(2,1)}, bf16[3,2,2,96,128]{4,3,2,1,0:T(8,128)(2,1)}, u32[]{:S(2)}, u32[]{:S(2)}) collective-permute-start(bf16[3,2,2,96,128]{4,3,2,1,0:T(8,128)(2,1)} %collective-permute-done.5.nxt), channel_id=1, source_target_pairs={{0,1},{1,0},{2,3},{3,2},{4,5},{5,4},{6,7},{7,6},{8,9},{9,8},{10,11... | collective-permute-start | bytes 884744 | tf_op jit(solution)/shard_map/ppermute | solution.py:262
  111.7 16.0 %copy-start = (bf16[6,3,2,2,96,128]{5,4,3,2,1,0:T(8,128)(2,1)S(1)}, bf16[6,3,2,2,96,128]{5,4,3,2,1,0:T(8,128)(2,1)}, u32[]{:S(2)}) copy-start(bf16[6,3,2,2,96,128]{5,4,3,2,1,0:T(8,128)(2,1)} %get-tuple-element.17) | copy-start | bytes 5308420
  111.7 4.0 %collective-permute-start.7 = (bf16[2,3,2,2,96,128]{5,4,3,2,1,0:T(8,128)(2,1)S(1)}, bf16[2,3,2,2,96,128]{5,4,3,2,1,0:T(8,128)(2,1)S(1)}, u32[]{:S(2)}, u32[]{:S(2)}) collective-permute-start(bf16[2,3,2,2,96,128]{5,4,3,2,1,0:T(8,128)(2,1)S(1)} %get-tuple-element.19), channel_id=1, source_target_pairs={{0,1},{1,0},{2,3},{3,2},{4,5},{5,4},{6,7},{7,6},{8,9},{9,8},{10,11... | collective-permute-start | bytes 1769480 | tf_op jit(solution)/shard_map/ppermute | solution.py:262
  116.9 10.7 %collective-permute-start.8 = (bf16[4,3,2,2,96,128]{5,4,3,2,1,0:T(8,128)(2,1)}, bf16[4,3,2,2,96,128]{5,4,3,2,1,0:T(8,128)(2,1)S(1)}, u32[]{:S(2)}, u32[]{:S(2)}) collective-permute-start(bf16[4,3,2,2,96,128]{5,4,3,2,1,0:T(8,128)(2,1)} %get-tuple-element.20), channel_id=1, source_target_pairs={{0,1},{1,0},{2,3},{3,2},{4,5},{5,4},{6,7},{7,6},{8,9},{9,8},{10,11... | collective-permute-start | bytes 3538952 | tf_op jit(solution)/shard_map/ppermute | solution.py:262
  119.2 13.1 %collective-permute-start.9 = (bf16[3,2,2,96,128]{4,3,2,1,0:T(8,128)(2,1)S(1)}, bf16[3,2,2,96,128]{4,3,2,1,0:T(8,128)(2,1)S(1)}, u32[]{:S(2)}, u32[]{:S(2)}) collective-permute-start(bf16[3,2,2,96,128]{4,3,2,1,0:T(8,128)(2,1)S(1)} %get-tuple-element.21), channel_id=1, source_target_pairs={{0,64},{64,128},{128,192},{192,256},{256,320},{320,384},{384,448},... | collective-permute-start | bytes 884744 | tf_op jit(solution)/shard_map/ppermute | solution.py:293
  125.7 12.8 %collective-permute-start.10 = (bf16[3,2,2,96,128]{4,3,2,1,0:T(8,128)(2,1)S(1)}, bf16[3,2,2,96,128]{4,3,2,1,0:T(8,128)(2,1)S(1)}, u32[]{:S(2)}, u32[]{:S(2)}) collective-permute-start(bf16[3,2,2,96,128]{4,3,2,1,0:T(8,128)(2,1)S(1)} %get-tuple-element.22), channel_id=1, source_target_pairs={{64,0},{128,64},{192,128},{256,192},{320,256},{384,320},{448,384},... | collective-permute-start | bytes 884744 | tf_op jit(solution)/shard_map/ppermute | solution.py:292
  138.7 13.3 %collective-permute-start.11 = (bf16[4,2,2,96,128]{4,3,2,1,0:T(8,128)(2,1)S(1)}, bf16[4,2,2,96,128]{4,3,2,1,0:T(8,128)(2,1)S(1)}, u32[]{:S(2)}, u32[]{:S(2)}) collective-permute-start(bf16[4,2,2,96,128]{4,3,2,1,0:T(8,128)(2,1)S(1)} %pad_maximum_fusion.2), channel_id=1, source_target_pairs={{8,16},{16,8},{40,48},{48,40},{0,56},{56,0},{32,24},{24,32},{9,17}... | collective-permute-start | bytes 1179656 | tf_op jit(solution)/shard_map/ppermute | solution.py:302

commit v4 on v3

--- a/solution.py
+++ b/solution.py
@@ -296,14 +296,15 @@
     def terms(col, *at):
         return mine[col, *at].astype(F32) + sib_mid[col - 1, *at].astype(F32)
 
-    d_side = [terms(time + 1, 2) for time in range(4)]
-    d_side[0] += to_first[2].astype(F32)
-    d_side[3] += to_last[2].astype(F32)
-    to_inner = lax.ppermute(jnp.stack(d_side).astype(BF), Z, Z_PAIRS)
+    to_mids = lax.ppermute(jnp.stack([terms(2, 2), terms(3, 2)]).astype(BF), Z, Z_PAIRS)
+    to_mids, to_first, to_last = lax.optimization_barrier((to_mids, to_first, to_last))
+    d_ends = [terms(1, 2) + to_first[2].astype(F32), terms(4, 2) + to_last[2].astype(F32)]
+    to_ends = lax.ppermute(jnp.stack(d_ends).astype(BF), Z, Z_PAIRS)
     is_inner = (jnp.arange(2) == 1 - zm)[:, None, None, None, None]
     d_own = []
     for time in range(4):
-        total = terms(time + 1, slice(0, 2)) + jnp.where(is_inner, to_inner[time][None].astype(F32), 0.0)
+        to_inner = to_mids[time - 1] if time in (1, 2) else to_ends[time // 3]
+        total = terms(time + 1, slice(0, 2)) + jnp.where(is_inner, to_inner[None].astype(F32), 0.0)
         if time == 0:
             total = total + to_first[:2].astype(F32)
         if time == 3:

time: 197 us -> 192 us (0.975)
  waiting for transfers between devices: 68.4 us -> 58.9 us
  starting transfers between devices: 59.3 us -> 64.4 us
    ppermute x1 -> x2, starting transfers between devices: 5.08 us -> 10.2 us  [the longest x1 5.08 us: per_device(): to_ends = lax.ppermute(jnp.stack(d_ends).astype(BF), Z, Z_PAIRS)]
    ppermute x1, waiting for transfers between devices: 4.53 us -> 0.01 us  [per_device(): to_first = lax.ppermute(d_nxt, LINE, FORTH)]
    ppermute x1 -> x2, waiting for transfers between devices: 8.23 us -> 3.87 us  [the longest x1 3.87 us: per_device(): to_ends = lax.ppermute(jnp.stack(d_ends).astype(BF), Z, Z_PAIRS)]
  transfers between devices with their start and end apart: 14 -> 15, of which waited for: 8 -> 7; matrix products, arithmetic and copies ran while one was open for 0% -> 0% of each run, Pallas kernels for 1% -> 1%
where the time goes in v4:
time: 192 us; the launch traced here: 191 us
  starting transfers between devices  64.4 us (34%)
  waiting for transfers between devices  58.9 us (31%)
  blocking collectives  40.4 us (21%)
  Pallas kernels  24.4 us (13%)
  other arithmetic  2.14 us (1%)
    all_to_all x1, blocking collectives, to_heads(): lax.all_to_all(blocks, GROUP, split_axis=0, concat_axis=0, tiled=True)  40.4 us
    all_to_all x2, waiting for transfers between devices, to_heads(): lax.all_to_all(blocks, GROUP, split_axis=0, concat_axis=0, tiled=True)  26.6 us
    all_to_all x2, starting transfers between devices, to_heads(): lax.all_to_all(blocks, GROUP, split_axis=0, concat_axis=0, tiled=True)  24.8 us
    pallas_call x1, Pallas kernels, attention(): pl.pallas_call(attention_kernel, out_shape=[jax.ShapeDtypeStruct((4, 2, 2...  17.4 us
    ppermute x6, starting transfers between devices, swapped(): return lax.ppermute(block, 'c', SWAP)  12.9 us
    ppermute x1, waiting for transfers between devices, per_device(): lax.ppermute(jnp.concatenate([own[3], side[3:]], axis=0), LINE, FORTH)  12 us
    ppermute x1, waiting for transfers between devices, per_device(): side = lax.ppermute(inner, Z, Z_PAIRS)  7.8 us
    ppermute x1, starting transfers between devices, per_device(): to_first = lax.ppermute(d_nxt, LINE, FORTH)  6.5 us
  transfers between devices with their start and end apart: 15, of which 7 were waited for; matrix products, arithmetic and copies ran while one was open for 0% of the time, Pallas kernels for 1%

profile of v4, /device:TPU:6, one launch (start us, length us, event | category | flops | bytes accessed | tf_op | source)
XLA Modules:
  0.0 191.3 jit_solution(1731907028470661547)
XLA Ops:
  0.6 2.2 %shard_map.76 = bf16[16,2,96,128]{3,2,1,0:T(8,128)(2,1)} custom-call(s32[1]{0:T(128)} %bitcast.zm_ref, bf16[96,2048]{1,0:T(8,128)(2,1)} %a_ref.2, bf16[96,2048]{1,0:T(8,128)(2,1)} %b_ref.2), custom_call_target="tpu_custom_call" | custom-call | bytes 1572864 | tf_op jit(solution)/shard_map/pallas_call | solution.py:43
  2.8 15.7 %all-to-all-start = ((bf16[16,2,96,128]{3,2,1,0:T(8,128)(2,1)}), bf16[16,2,96,128]{3,2,1,0:T(8,128)(2,1)S(1)}, u32[]{:S(2)}, u32[]{:S(2)}) async-start(bf16[16,2,96,128]{3,2,1,0:T(8,128)(2,1)} %shard_map.76), calls=%async_computation | async-start | bytes 1572864 | tf_op jit(solution)/shard_map/all_to_all | solution.py:258
  18.5 26.6 %all-to-all-done = bf16[16,2,96,128]{3,2,1,0:T(8,128)(2,1)S(1)} async-done(((bf16[16,2,96,128]{3,2,1,0:T(8,128)(2,1)}), bf16[16,2,96,128]{3,2,1,0:T(8,128)(2,1)S(1)}, u32[]{:S(2)}, u32[]{:S(2)}) %all-to-all-start) | async-done | bytes 786464 | tf_op jit(solution)/shard_map/all_to_all | solution.py:258
  45.1 2.3 %collective-permute-start.1 = (bf16[4,2,2,96,128]{4,3,2,1,0:T(8,128)(2,1)S(1)}, bf16[4,2,2,96,128]{4,3,2,1,0:T(8,128)(2,1)S(1)}, u32[]{:S(2)}, u32[]{:S(2)}) collective-permute-start(bf16[4,2,2,96,128]{4,3,2,1,0:T(8,128)(2,1)S(1)} %dynamic-slice_bitcast_fusion), channel_id=1, source_target_pairs={{8,16},{16,8},{40,48},{48,40},{0,56},{56,0},{32,24},{24,32},{9,17}... | collective-permute-start | bytes 1179656 | tf_op jit(solution)/shard_map/ppermute | solution.py:279
  47.4 2.2 %shard_map.77 = bf16[16,2,96,128]{3,2,1,0:T(8,128)(2,1)} custom-call(s32[1]{0:T(128)} %bitcast.zm_ref, bf16[96,2048]{1,0:T(8,128)(2,1)} %a_ref.3, bf16[96,2048]{1,0:T(8,128)(2,1)} %b_ref.3), custom_call_target="tpu_custom_call" | custom-call | bytes 1572864 | tf_op jit(solution)/shard_map/pallas_call | solution.py:43
  49.7 7.8 %collective-permute-done.1.side = bf16[4,2,2,96,128]{4,3,2,1,0:T(8,128)(2,1)S(1)} collective-permute-done((bf16[4,2,2,96,128]{4,3,2,1,0:T(8,128)(2,1)S(1)}, bf16[4,2,2,96,128]{4,3,2,1,0:T(8,128)(2,1)S(1)}, u32[]{:S(2)}, u32[]{:S(2)}) %collective-permute-start.1) | collective-permute-done | bytes 393248 | tf_op jit(solution)/shard_map/ppermute | solution.py:279
  57.4 9.1 %all-to-all-start.1 = ((bf16[16,2,96,128]{3,2,1,0:T(8,128)(2,1)}), bf16[16,2,96,128]{3,2,1,0:T(8,128)(2,1)S(1)}, u32[]{:S(2)}, u32[]{:S(2)}) async-start(bf16[16,2,96,128]{3,2,1,0:T(8,128)(2,1)} %shard_map.77), calls=%async_computation.1 | async-start | bytes 1572864 | tf_op jit(solution)/shard_map/all_to_all | solution.py:258
  66.5 0.0 copy-start.1
  66.6 1.9 %collective-permute-start = (bf16[4,2,2,2,96,128]{5,4,3,2,1,0:T(8,128)(2,1)S(1)}, bf16[4,2,2,2,96,128]{5,4,3,2,1,0:T(8,128)(2,1)S(1)}, u32[]{:S(2)}, u32[]{:S(2)}) collective-permute-start(bf16[4,2,2,2,96,128]{5,4,3,2,1,0:T(8,128)(2,1)S(1)} %bitcast.64), channel_id=1, source_target_pairs={{0,1},{1,0},{2,3},{3,2},{4,5},{5,4},{6,7},{7,6},{8,9},{9,8},{10,11... | collective-permute-start | bytes 2359304 | tf_op jit(solution)/shard_map/ppermute | solution.py:262
  68.6 1.9 %collective-permute-start.3 = (bf16[3,2,2,96,128]{4,3,2,1,0:T(8,128)(2,1)S(1)}, bf16[3,2,2,96,128]{4,3,2,1,0:T(8,128)(2,1)S(1)}, u32[]{:S(2)}, u32[]{:S(2)}) collective-permute-start(bf16[3,2,2,96,128]{4,3,2,1,0:T(8,128)(2,1)S(1)} %pad_maximum_fusion.2), channel_id=1, source_target_pairs={{0,64},{64,128},{128,192},{192,256},{256,320},{320,384},{384,448},... | collective-permute-start | bytes 884744 | tf_op jit(solution)/shard_map/ppermute | solution.py:284
  70.5 3.9 %collective-permute-start.5 = (bf16[3,2,2,96,128]{4,3,2,1,0:T(8,128)(2,1)S(1)}, bf16[3,2,2,96,128]{4,3,2,1,0:T(8,128)(2,1)}, u32[]{:S(2)}, u32[]{:S(2)}) collective-permute-start(bf16[3,2,2,96,128]{4,3,2,1,0:T(8,128)(2,1)S(1)} %pad_maximum_fusion.3), channel_id=1, source_target_pairs={{64,0},{128,64},{192,128},{256,192},{320,256},{384,320},{448,384},... | collective-permute-start | bytes 884744 | tf_op jit(solution)/shard_map/ppermute | solution.py:283
  74.5 1.9 %collective-permute-start.2 = (bf16[4,2,2,96,128]{4,3,2,1,0:T(8,128)(2,1)S(1)}, bf16[4,2,2,96,128]{4,3,2,1,0:T(8,128)(2,1)S(1)}, u32[]{:S(2)}, u32[]{:S(2)}) collective-permute-start(bf16[4,2,2,96,128]{4,3,2,1,0:T(8,128)(2,1)S(1)} %collective-permute-done.1.side), channel_id=1, source_target_pairs={{0,1},{1,0},{2,3},{3,2},{4,5},{5,4},{6,7},{7,6},{8,9},{9,8},{10,11... | collective-permute-start | bytes 1179656 | tf_op jit(solution)/shard_map/ppermute | solution.py:262
  76.4 12.0 %collective-permute-done.3.prev = bf16[3,2,2,96,128]{4,3,2,1,0:T(8,128)(2,1)S(1)} collective-permute-done((bf16[3,2,2,96,128]{4,3,2,1,0:T(8,128)(2,1)S(1)}, bf16[3,2,2,96,128]{4,3,2,1,0:T(8,128)(2,1)S(1)}, u32[]{:S(2)}, u32[]{:S(2)}) %collective-permute-start.3) | collective-permute-done | bytes 294944 | tf_op jit(solution)/shard_map/ppermute | solution.py:284
  88.4 1.9 collective-permute-start.4
  90.3 0.0 collective-permute-done.5.nxt
  90.4 2.4 %collective-permute-start.6 = (bf16[3,2,2,96,128]{4,3,2,1,0:T(8,128)(2,1)}, bf16[3,2,2,96,128]{4,3,2,1,0:T(8,128)(2,1)}, u32[]{:S(2)}, u32[]{:S(2)}) collective-permute-start(bf16[3,2,2,96,128]{4,3,2,1,0:T(8,128)(2,1)} %collective-permute-done.5.nxt), channel_id=1, source_target_pairs={{0,1},{1,0},{2,3},{3,2},{4,5},{5,4},{6,7},{7,6},{8,9},{9,8},{10,11... | collective-permute-start | bytes 884744 | tf_op jit(solution)/shard_map/ppermute | solution.py:262
  92.8 0.0 copy-done.1
  92.8 0.1 copy.8.window_ref
  92.9 0.0 collective-permute-done.2.side_s
  92.9 0.0 collective-permute-done.own_s
  92.9 0.0 collective-permute-done.4.prev_s
  92.9 1.4 collective-permute-done.6.nxt_s
  94.3 0.0 all-to-all-done.1
  94.3 17.4 %shard_map.78 = (bf16[4,2,2,96,128]{4,3,2,1,0:T(8,128)(2,1)S(1)}, bf16[6,3,2,2,96,128]{5,4,3,2,1,0:T(8,128)(2,1)}, bf16[2,3,2,2,96,128]{5,4,3,2,1,0:T(8,128)(2,1)S(1)}, bf16[4,3,2,2,96,128]{5,4,3,2,1,0:T(8,128)(2,1)}) custom-call(s32[1]{0:T(128)} %bitcast.zm_ref, s32[1]{0:T(128)} %bitcast.1.chip_ref, s32[1]{0:T(128)} %bitcast.2.line_ref, ...), custom_call_target="tpu_custom_call" | custom-call | flops 6000000000 | bytes 9000000 | tf_op jit(solution)/shard_map/pallas_call | solution.py:229
  111.7 0.0 copy-start
  111.7 2.4 %collective-permute-start.7 = (bf16[2,3,2,2,96,128]{5,4,3,2,1,0:T(8,128)(2,1)S(1)}, bf16[2,3,2,2,96,128]{5,4,3,2,1,0:T(8,128)(2,1)S(1)}, u32[]{:S(2)}, u32[]{:S(2)}) collective-permute-start(bf16[2,3,2,2,96,128]{5,4,3,2,1,0:T(8,128)(2,1)S(1)} %get-tuple-element.22), channel_id=1, source_target_pairs={{0,1},{1,0},{2,3},{3,2},{4,5},{5,4},{6,7},{7,6},{8,9},{9,8},{10,11... | collective-permute-start | bytes 1769480 | tf_op jit(solution)/shard_map/ppermute | solution.py:262
  114.1 1.6 collective-permute-done.7
  115.7 1.2 fusion.5
  116.9 2.3 %collective-permute-start.8 = (bf16[4,3,2,2,96,128]{5,4,3,2,1,0:T(8,128)(2,1)}, bf16[4,3,2,2,96,128]{5,4,3,2,1,0:T(8,128)(2,1)S(1)}, u32[]{:S(2)}, u32[]{:S(2)}) collective-permute-start(bf16[4,3,2,2,96,128]{5,4,3,2,1,0:T(8,128)(2,1)} %get-tuple-element.23), channel_id=1, source_target_pairs={{0,1},{1,0},{2,3},{3,2},{4,5},{5,4},{6,7},{7,6},{8,9},{9,8},{10,11... | collective-permute-start | bytes 3538952 | tf_op jit(solution)/shard_map/ppermute | solution.py:262
  119.2 6.5 %collective-permute-start.10 = (bf16[3,2,2,96,128]{4,3,2,1,0:T(8,128)(2,1)S(1)}, bf16[3,2,2,96,128]{4,3,2,1,0:T(8,128)(2,1)S(1)}, u32[]{:S(2)}, u32[]{:S(2)}) collective-permute-start(bf16[3,2,2,96,128]{4,3,2,1,0:T(8,128)(2,1)S(1)} %get-tuple-element.24), channel_id=1, source_target_pairs={{0,64},{64,128},{128,192},{192,256},{256,320},{320,384},{384,448},... | collective-permute-start | bytes 884744 | tf_op jit(solution)/shard_map/ppermute | solution.py:293
  125.7 1.9 %collective-permute-start.11 = (bf16[3,2,2,96,128]{4,3,2,1,0:T(8,128)(2,1)S(1)}, bf16[3,2,2,96,128]{4,3,2,1,0:T(8,128)(2,1)S(1)}, u32[]{:S(2)}, u32[]{:S(2)}) collective-permute-start(bf16[3,2,2,96,128]{4,3,2,1,0:T(8,128)(2,1)S(1)} %get-tuple-element.25), channel_id=1, source_target_pairs={{64,0},{128,64},{192,128},{256,192},{320,256},{384,320},{448,384},... | collective-permute-start | bytes 884744 | tf_op jit(solution)/shard_map/ppermute | solution.py:292
  127.7 0.0 collective-permute-done.8
  127.7 0.0 copy-done
  127.7 0.1 fusion.10
  127.8 5.1 %collective-permute-start.9 = (bf16[2,2,2,96,128]{4,3,2,1,0:T(8,128)(2,1)S(1)}, bf16[2,2,2,96,128]{4,3,2,1,0:T(8,128)(2,1)S(1)}, u32[]{:S(2)}, u32[]{:S(2)}) collective-permute-start(bf16[2,2,2,96,128]{4,3,2,1,0:T(8,128)(2,1)S(1)} %pad_maximum_fusion.4), channel_id=1, source_target_pairs={{8,16},{16,8},{40,48},{48,40},{0,56},{56,0},{32,24},{24,32},{9,17}... | collective-permute-start | bytes 589832 | tf_op jit(solution)/shard_map/ppermute | solution.py:299
  132.9 0.0 collective-permute-done.10
  132.9 5.6 %collective-permute-done.11 = bf16[3,2,2,96,128]{4,3,2,1,0:T(8,128)(2,1)S(1)} collective-permute-done((bf16[3,2,2,96,128]{4,3,2,1,0:T(8,128)(2,1)S(1)}, bf16[3,2,2,96,128]{4,3,2,1,0:T(8,128)(2,1)S(1)}, u32[]{:S(2)}, u32[]{:S(2)}) %collective-permute-start.11) | collective-permute-done | bytes 294944 | tf_op jit(solution)/shard_map/ppermute | solution.py:292
  138.5 0.0 collective-permute-done.9
  138.6 0.1 fusion.9
  138.7 5.1 %collective-permute-start.12 = (bf16[2,2,2,96,128]{4,3,2,1,0:T(8,128)(2,1)S(1)}, bf16[2,2,2,96,128]{4,3,2,1,0:T(8,128)(2,1)S(1)}, u32[]{:S(2)}, u32[]{:S(2)}) collective-permute-start(bf16[2,2,2,96,128]{4,3,2,1,0:T(8,128)(2,1)S(1)} %pad_maximum_fusion.5), channel_id=1, source_target_pairs={{8,16},{16,8},{40,48},{48,40},{0,56},{56,0},{32,24},{24,32},{9,17}... | collective-permute-start | bytes 589832 | tf_op jit(solution)/shard_map/ppermute | solution.py:302
  143.8 0.2 add_convert_fusion.3
  143.9 3.9 %collective-permute-done.12 = bf16[2,2,2,96,128]{4,3,2,1,0:T(8,128)(2,1)S(1)} collective-permute-done((bf16[2,2,2,96,128]{4,3,2,1,0:T(8,128)(2,1)S(1)}, bf16[2,2,2,96,128]{4,3,2,1,0:T(8,128)(2,1)S(1)}, u32[]{:S(2)}, u32[]{:S(2)}) %collective-permute-start.12) | collective-permute-done | bytes 196640 | tf_op jit(solution)/shard_map/ppermute | solution.py:302
  147.8 0.2 fusion.6
  148.1 0.1 pad_maximum_fusion.1
  148.2 0.1 pad_maximum_fusion
  148.3 40.4 %all_to_all.15.in_ref = bf16[16,3,96,128]{3,2,1,0:T(8,128)(2,1)} all-to-all(bf16[16,3,96,128]{3,2,1,0:T(8,128)(2,1)S(1)} %pad_maximum_fusion), channel_id=1, replica_groups=mesh['yl'=2,'x'=4,'zh'=2,'zm'=2,'zl'=2,'yhh'=2,'yhl'=2,'c'=2] {'zh','yhh..., dimensions={0} | all-to-all | bytes 2359296 | tf_op jit(solution)/shard_map/all_to_all | solution.py:258
  188.7 2.6 %shard_map.79 = (bf16[96,2048]{1,0:T(8,128)(2,1)}, bf16[96,2048]{1,0:T(8,128)(2,1)}, bf16[96,2048]{1,0:T(8,128)(2,1)}) custom-call(s32[1]{0:T(128)} %bitcast.zm_ref, bf16[16,3,96,128]{3,2,1,0:T(8,128)(2,1)} %all_to_all.15.in_ref), custom_call_target="tpu_custom_call" | custom-call | bytes 2359296 | tf_op jit(solution)/shard_map/pallas_call | solution.py:62
  (10 shorter events, 0.2 us)
Async XLA Ops:
  2.8 42.2 %all-to-all-start = ((bf16[16,2,96,128]{3,2,1,0:T(8,128)(2,1)}), bf16[16,2,96,128]{3,2,1,0:T(8,128)(2,1)S(1)}, u32[]{:S(2)}, u32[]{:S(2)}) async-start(bf16[16,2,96,128]{3,2,1,0:T(8,128)(2,1)} %shard_map.76), calls=%async_computation | async-start | bytes 1572864 | tf_op jit(solution)/shard_map/all_to_all | solution.py:258
  45.1 12.3 %collective-permute-start.1 = (bf16[4,2,2,96,128]{4,3,2,1,0:T(8,128)(2,1)S(1)}, bf16[4,2,2,96,128]{4,3,2,1,0:T(8,128)(2,1)S(1)}, u32[]{:S(2)}, u32[]{:S(2)}) collective-permute-start(bf16[4,2,2,96,128]{4,3,2,1,0:T(8,128)(2,1)S(1)} %dynamic-slice_bitcast_fusion), channel_id=1, source_target_pairs={{8,16},{16,8},{40,48},{48,40},{0,56},{56,0},{32,24},{24,32},{9,17}... | collective-permute-start | bytes 1179656 | tf_op jit(solution)/shard_map/ppermute | solution.py:279
  57.4 36.9 %all-to-all-start.1 = ((bf16[16,2,96,128]{3,2,1,0:T(8,128)(2,1)}), bf16[16,2,96,128]{3,2,1,0:T(8,128)(2,1)S(1)}, u32[]{:S(2)}, u32[]{:S(2)}) async-start(bf16[16,2,96,128]{3,2,1,0:T(8,128)(2,1)} %shard_map.77), calls=%async_computation.1 | async-start | bytes 1572864 | tf_op jit(solution)/shard_map/all_to_all | solution.py:258
  66.5 26.2 %copy-start.1 = (s32[16,2]{0,1:T(2,128)S(1)}, s32[16,2]{0,1:T(2,128)}, u32[]{:S(2)}) copy-start(s32[16,2]{0,1:T(2,128)} %param.9) | copy-start | bytes 388
  66.6 26.3 %collective-permute-start = (bf16[4,2,2,2,96,128]{5,4,3,2,1,0:T(8,128)(2,1)S(1)}, bf16[4,2,2,2,96,128]{5,4,3,2,1,0:T(8,128)(2,1)S(1)}, u32[]{:S(2)}, u32[]{:S(2)}) collective-permute-start(bf16[4,2,2,2,96,128]{5,4,3,2,1,0:T(8,128)(2,1)S(1)} %bitcast.64), channel_id=1, source_target_pairs={{0,1},{1,0},{2,3},{3,2},{4,5},{5,4},{6,7},{7,6},{8,9},{9,8},{10,11... | collective-permute-start | bytes 2359304 | tf_op jit(solution)/shard_map/ppermute | solution.py:262
  68.6 19.8 %collective-permute-start.3 = (bf16[3,2,2,96,128]{4,3,2,1,0:T(8,128)(2,1)S(1)}, bf16[3,2,2,96,128]{4,3,2,1,0:T(8,128)(2,1)S(1)}, u32[]{:S(2)}, u32[]{:S(2)}) collective-permute-start(bf16[3,2,2,96,128]{4,3,2,1,0:T(8,128)(2,1)S(1)} %pad_maximum_fusion.2), channel_id=1, source_target_pairs={{0,64},{64,128},{128,192},{192,256},{256,320},{320,384},{384,448},... | collective-permute-start | bytes 884744 | tf_op jit(solution)/shard_map/ppermute | solution.py:284
  70.5 19.8 %collective-permute-start.5 = (bf16[3,2,2,96,128]{4,3,2,1,0:T(8,128)(2,1)S(1)}, bf16[3,2,2,96,128]{4,3,2,1,0:T(8,128)(2,1)}, u32[]{:S(2)}, u32[]{:S(2)}) collective-permute-start(bf16[3,2,2,96,128]{4,3,2,1,0:T(8,128)(2,1)S(1)} %pad_maximum_fusion.3), channel_id=1, source_target_pairs={{64,0},{128,64},{192,128},{256,192},{320,256},{384,320},{448,384},... | collective-permute-start | bytes 884744 | tf_op jit(solution)/shard_map/ppermute | solution.py:283
  74.5 18.4 %collective-permute-start.2 = (bf16[4,2,2,96,128]{4,3,2,1,0:T(8,128)(2,1)S(1)}, bf16[4,2,2,96,128]{4,3,2,1,0:T(8,128)(2,1)S(1)}, u32[]{:S(2)}, u32[]{:S(2)}) collective-permute-start(bf16[4,2,2,96,128]{4,3,2,1,0:T(8,128)(2,1)S(1)} %collective-permute-done.1.side), channel_id=1, source_target_pairs={{0,1},{1,0},{2,3},{3,2},{4,5},{5,4},{6,7},{7,6},{8,9},{9,8},{10,11... | collective-permute-start | bytes 1179656 | tf_op jit(solution)/shard_map/ppermute | solution.py:262
  88.4 4.5 %collective-permute-start.4 = (bf16[3,2,2,96,128]{4,3,2,1,0:T(8,128)(2,1)S(1)}, bf16[3,2,2,96,128]{4,3,2,1,0:T(8,128)(2,1)}, u32[]{:S(2)}, u32[]{:S(2)}) collective-permute-start(bf16[3,2,2,96,128]{4,3,2,1,0:T(8,128)(2,1)S(1)} %collective-permute-done.3.prev), channel_id=1, source_target_pairs={{0,1},{1,0},{2,3},{3,2},{4,5},{5,4},{6,7},{7,6},{8,9},{9,8},{10,11... | collective-permute-start | bytes 884744 | tf_op jit(solution)/shard_map/ppermute | solution.py:262
  90.4 3.9 %collective-permute-start.6 = (bf16[3,2,2,96,128]{4,3,2,1,0:T(8,128)(2,1)}, bf16[3,2,2,96,128]{4,3,2,1,0:T(8,128)(2,1)}, u32[]{:S(2)}, u32[]{:S(2)}) collective-permute-start(bf16[3,2,2,96,128]{4,3,2,1,0:T(8,128)(2,1)} %collective-permute-done.5.nxt), channel_id=1, source_target_pairs={{0,1},{1,0},{2,3},{3,2},{4,5},{5,4},{6,7},{7,6},{8,9},{9,8},{10,11... | collective-permute-start | bytes 884744 | tf_op jit(solution)/shard_map/ppermute | solution.py:262
  111.7 16.0 %copy-start = (bf16[6,3,2,2,96,128]{5,4,3,2,1,0:T(8,128)(2,1)S(1)}, bf16[6,3,2,2,96,128]{5,4,3,2,1,0:T(8,128)(2,1)}, u32[]{:S(2)}) copy-start(bf16[6,3,2,2,96,128]{5,4,3,2,1,0:T(8,128)(2,1)} %get-tuple-element.20) | copy-start | bytes 5308420
  111.7 4.0 %collective-permute-start.7 = (bf16[2,3,2,2,96,128]{5,4,3,2,1,0:T(8,128)(2,1)S(1)}, bf16[2,3,2,2,96,128]{5,4,3,2,1,0:T(8,128)(2,1)S(1)}, u32[]{:S(2)}, u32[]{:S(2)}) collective-permute-start(bf16[2,3,2,2,96,128]{5,4,3,2,1,0:T(8,128)(2,1)S(1)} %get-tuple-element.22), channel_id=1, source_target_pairs={{0,1},{1,0},{2,3},{3,2},{4,5},{5,4},{6,7},{7,6},{8,9},{9,8},{10,11... | collective-permute-start | bytes 1769480 | tf_op jit(solution)/shard_map/ppermute | solution.py:262
  116.9 10.7 %collective-permute-start.8 = (bf16[4,3,2,2,96,128]{5,4,3,2,1,0:T(8,128)(2,1)}, bf16[4,3,2,2,96,128]{5,4,3,2,1,0:T(8,128)(2,1)S(1)}, u32[]{:S(2)}, u32[]{:S(2)}) collective-permute-start(bf16[4,3,2,2,96,128]{5,4,3,2,1,0:T(8,128)(2,1)} %get-tuple-element.23), channel_id=1, source_target_pairs={{0,1},{1,0},{2,3},{3,2},{4,5},{5,4},{6,7},{7,6},{8,9},{9,8},{10,11... | collective-permute-start | bytes 3538952 | tf_op jit(solution)/shard_map/ppermute | solution.py:262
  119.2 13.7 %collective-permute-start.10 = (bf16[3,2,2,96,128]{4,3,2,1,0:T(8,128)(2,1)S(1)}, bf16[3,2,2,96,128]{4,3,2,1,0:T(8,128)(2,1)S(1)}, u32[]{:S(2)}, u32[]{:S(2)}) collective-permute-start(bf16[3,2,2,96,128]{4,3,2,1,0:T(8,128)(2,1)S(1)} %get-tuple-element.24), channel_id=1, source_target_pairs={{0,64},{64,128},{128,192},{192,256},{256,320},{320,384},{384,448},... | collective-permute-start | bytes 884744 | tf_op jit(solution)/shard_map/ppermute | solution.py:293
  125.7 12.8 %collective-permute-start.11 = (bf16[3,2,2,96,128]{4,3,2,1,0:T(8,128)(2,1)S(1)}, bf16[3,2,2,96,128]{4,3,2,1,0:T(8,128)(2,1)S(1)}, u32[]{:S(2)}, u32[]{:S(2)}) collective-permute-start(bf16[3,2,2,96,128]{4,3,2,1,0:T(8,128)(2,1)S(1)} %get-tuple-element.25), channel_id=1, source_target_pairs={{64,0},{128,64},{192,128},{256,192},{320,256},{384,320},{448,384},... | collective-permute-start | bytes 884744 | tf_op jit(solution)/shard_map/ppermute | solution.py:292
  127.8 10.7 %collective-permute-start.9 = (bf16[2,2,2,96,128]{4,3,2,1,0:T(8,128)(2,1)S(1)}, bf16[2,2,2,96,128]{4,3,2,1,0:T(8,128)(2,1)S(1)}, u32[]{:S(2)}, u32[]{:S(2)}) collective-permute-start(bf16[2,2,2,96,128]{4,3,2,1,0:T(8,128)(2,1)S(1)} %pad_maximum_fusion.4), channel_id=1, source_target_pairs={{8,16},{16,8},{40,48},{48,40},{0,56},{56,0},{32,24},{24,32},{9,17}... | collective-permute-start | bytes 589832 | tf_op jit(solution)/shard_map/ppermute | solution.py:299
  138.7 9.1 %collective-permute-start.12 = (bf16[2,2,2,96,128]{4,3,2,1,0:T(8,128)(2,1)S(1)}, bf16[2,2,2,96,128]{4,3,2,1,0:T(8,128)(2,1)S(1)}, u32[]{:S(2)}, u32[]{:S(2)}) collective-permute-start(bf16[2,2,2,96,128]{4,3,2,1,0:T(8,128)(2,1)S(1)} %pad_maximum_fusion.5), channel_id=1, source_target_pairs={{8,16},{16,8},{40,48},{48,40},{0,56},{56,0},{32,24},{24,32},{9,17}... | collective-permute-start | bytes 589832 | tf_op jit(solution)/shard_map/ppermute | solution.py:302

commit v5 on v4

--- a/solution.py
+++ b/solution.py
@@ -288,7 +288,6 @@
     sib_edge = swapped(sib_edge)
     d_prev = (mine[0].astype(F32) + sib_edge[0].astype(F32)).astype(BF)
     d_nxt = (mine[5].astype(F32) + sib_edge[1].astype(F32)).astype(BF)
-    sib_mid, d_prev, d_nxt = lax.optimization_barrier((sib_mid, d_prev, d_nxt))
     to_last = lax.ppermute(d_prev, LINE, BACK)
     to_first = lax.ppermute(d_nxt, LINE, FORTH)
     sib_mid = swapped(sib_mid)

time: 192 us -> 193 us (level)
  the two profiles are of different devices: /device:TPU:6 before, /device:TPU:24 now
where the time goes in v5:
time: 193 us; the launch traced here: 192 us
  starting transfers between devices  62.5 us (32%)
  waiting for transfers between devices  57.7 us (30%)
  blocking collectives  44.5 us (23%)
  Pallas kernels  24.4 us (13%)
  other arithmetic  2.14 us (1%)
    all_to_all x1, blocking collectives, to_heads(): lax.all_to_all(blocks, GROUP, split_axis=0, concat_axis=0, tiled=True)  44.5 us
    all_to_all x2, waiting for transfers between devices, to_heads(): lax.all_to_all(blocks, GROUP, split_axis=0, concat_axis=0, tiled=True)  25.2 us
    all_to_all x2, starting transfers between devices, to_heads(): lax.all_to_all(blocks, GROUP, split_axis=0, concat_axis=0, tiled=True)  21.5 us
    pallas_call x1, Pallas kernels, attention(): pl.pallas_call(attention_kernel, out_shape=[jax.ShapeDtypeStruct((4, 2, 2...  17.4 us
    ppermute x6, starting transfers between devices, swapped(): return lax.ppermute(block, 'c', SWAP)  12.8 us
    ppermute x1, waiting for transfers between devices, per_device(): lax.ppermute(jnp.concatenate([own[3], side[3:]], axis=0), LINE, FORTH)  12 us
    ppermute x1, waiting for transfers between devices, per_device(): side = lax.ppermute(inner, Z, Z_PAIRS)  8.91 us
    ppermute x1, starting transfers between devices, per_device(): nxt = lax.ppermute(jnp.concatenate([own[0], side[:1]], axis=0), LINE, BACK)  6.29 us
  transfers between devices with their start and end apart: 15, of which 9 were waited for; matrix products, arithmetic and copies ran while one was open for 1% of the time, Pallas kernels for 1%

profile of v5, /device:TPU:24, one launch (start us, length us, event | category | flops | bytes accessed | tf_op | source)
XLA Modules:
  0.0 192.4 jit_solution(1866618564704958302)
XLA Ops:
  0.6 2.2 %shard_map.76 = bf16[16,2,96,128]{3,2,1,0:T(8,128)(2,1)} custom-call(s32[1]{0:T(128)} %bitcast.zm_ref, bf16[96,2048]{1,0:T(8,128)(2,1)} %a_ref.2, bf16[96,2048]{1,0:T(8,128)(2,1)} %b_ref.2), custom_call_target="tpu_custom_call" | custom-call | bytes 1572864 | tf_op jit(solution)/shard_map/pallas_call | solution.py:43
  2.8 15.0 %all-to-all-start = ((bf16[16,2,96,128]{3,2,1,0:T(8,128)(2,1)}), bf16[16,2,96,128]{3,2,1,0:T(8,128)(2,1)S(1)}, u32[]{:S(2)}, u32[]{:S(2)}) async-start(bf16[16,2,96,128]{3,2,1,0:T(8,128)(2,1)} %shard_map.76), calls=%async_computation | async-start | bytes 1572864 | tf_op jit(solution)/shard_map/all_to_all | solution.py:258
  17.9 25.1 %all-to-all-done = bf16[16,2,96,128]{3,2,1,0:T(8,128)(2,1)S(1)} async-done(((bf16[16,2,96,128]{3,2,1,0:T(8,128)(2,1)}), bf16[16,2,96,128]{3,2,1,0:T(8,128)(2,1)S(1)}, u32[]{:S(2)}, u32[]{:S(2)}) %all-to-all-start) | async-done | bytes 786464 | tf_op jit(solution)/shard_map/all_to_all | solution.py:258
  43.0 2.9 %collective-permute-start.1 = (bf16[4,2,2,96,128]{4,3,2,1,0:T(8,128)(2,1)S(1)}, bf16[4,2,2,96,128]{4,3,2,1,0:T(8,128)(2,1)S(1)}, u32[]{:S(2)}, u32[]{:S(2)}) collective-permute-start(bf16[4,2,2,96,128]{4,3,2,1,0:T(8,128)(2,1)S(1)} %dynamic-slice_bitcast_fusion), channel_id=1, source_target_pairs={{8,16},{16,8},{40,48},{48,40},{0,56},{56,0},{32,24},{24,32},{9,17}... | collective-permute-start | bytes 1179656 | tf_op jit(solution)/shard_map/ppermute | solution.py:279
  45.9 2.2 %shard_map.77 = bf16[16,2,96,128]{3,2,1,0:T(8,128)(2,1)} custom-call(s32[1]{0:T(128)} %bitcast.zm_ref, bf16[96,2048]{1,0:T(8,128)(2,1)} %a_ref.3, bf16[96,2048]{1,0:T(8,128)(2,1)} %b_ref.3), custom_call_target="tpu_custom_call" | custom-call | bytes 1572864 | tf_op jit(solution)/shard_map/pallas_call | solution.py:43
  48.1 8.9 %collective-permute-done.1.side = bf16[4,2,2,96,128]{4,3,2,1,0:T(8,128)(2,1)S(1)} collective-permute-done((bf16[4,2,2,96,128]{4,3,2,1,0:T(8,128)(2,1)S(1)}, bf16[4,2,2,96,128]{4,3,2,1,0:T(8,128)(2,1)S(1)}, u32[]{:S(2)}, u32[]{:S(2)}) %collective-permute-start.1) | collective-permute-done | bytes 393248 | tf_op jit(solution)/shard_map/ppermute | solution.py:279
  57.0 6.5 %all-to-all-start.1 = ((bf16[16,2,96,128]{3,2,1,0:T(8,128)(2,1)}), bf16[16,2,96,128]{3,2,1,0:T(8,128)(2,1)S(1)}, u32[]{:S(2)}, u32[]{:S(2)}) async-start(bf16[16,2,96,128]{3,2,1,0:T(8,128)(2,1)} %shard_map.77), calls=%async_computation.1 | async-start | bytes 1572864 | tf_op jit(solution)/shard_map/all_to_all | solution.py:258
  63.6 0.0 copy-start.1
  63.6 1.9 collective-permute-start
  65.6 3.4 %collective-permute-start.3 = (bf16[3,2,2,96,128]{4,3,2,1,0:T(8,128)(2,1)S(1)}, bf16[3,2,2,96,128]{4,3,2,1,0:T(8,128)(2,1)S(1)}, u32[]{:S(2)}, u32[]{:S(2)}) collective-permute-start(bf16[3,2,2,96,128]{4,3,2,1,0:T(8,128)(2,1)S(1)} %pad_maximum_fusion.2), channel_id=1, source_target_pairs={{0,64},{64,128},{128,192},{192,256},{256,320},{320,384},{384,448},... | collective-permute-start | bytes 884744 | tf_op jit(solution)/shard_map/ppermute | solution.py:284
  69.0 6.3 %collective-permute-start.5 = (bf16[3,2,2,96,128]{4,3,2,1,0:T(8,128)(2,1)S(1)}, bf16[3,2,2,96,128]{4,3,2,1,0:T(8,128)(2,1)}, u32[]{:S(2)}, u32[]{:S(2)}) collective-permute-start(bf16[3,2,2,96,128]{4,3,2,1,0:T(8,128)(2,1)S(1)} %pad_maximum_fusion.3), channel_id=1, source_target_pairs={{64,0},{128,64},{192,128},{256,192},{320,256},{384,320},{448,384},... | collective-permute-start | bytes 884744 | tf_op jit(solution)/shard_map/ppermute | solution.py:283
  75.3 2.1 %collective-permute-start.2 = (bf16[4,2,2,96,128]{4,3,2,1,0:T(8,128)(2,1)S(1)}, bf16[4,2,2,96,128]{4,3,2,1,0:T(8,128)(2,1)S(1)}, u32[]{:S(2)}, u32[]{:S(2)}) collective-permute-start(bf16[4,2,2,96,128]{4,3,2,1,0:T(8,128)(2,1)S(1)} %collective-permute-done.1.side), channel_id=1, source_target_pairs={{0,1},{1,0},{2,3},{3,2},{4,5},{5,4},{6,7},{7,6},{8,9},{9,8},{10,11... | collective-permute-start | bytes 1179656 | tf_op jit(solution)/shard_map/ppermute | solution.py:262
  77.5 12.0 %collective-permute-done.3.prev = bf16[3,2,2,96,128]{4,3,2,1,0:T(8,128)(2,1)S(1)} collective-permute-done((bf16[3,2,2,96,128]{4,3,2,1,0:T(8,128)(2,1)S(1)}, bf16[3,2,2,96,128]{4,3,2,1,0:T(8,128)(2,1)S(1)}, u32[]{:S(2)}, u32[]{:S(2)}) %collective-permute-start.3) | collective-permute-done | bytes 294944 | tf_op jit(solution)/shard_map/ppermute | solution.py:284
  89.5 1.9 collective-permute-start.4
  91.4 0.0 collective-permute-done.5.nxt
  91.4 2.4 %collective-permute-start.6 = (bf16[3,2,2,96,128]{4,3,2,1,0:T(8,128)(2,1)}, bf16[3,2,2,96,128]{4,3,2,1,0:T(8,128)(2,1)}, u32[]{:S(2)}, u32[]{:S(2)}) collective-permute-start(bf16[3,2,2,96,128]{4,3,2,1,0:T(8,128)(2,1)} %collective-permute-done.5.nxt), channel_id=1, source_target_pairs={{0,1},{1,0},{2,3},{3,2},{4,5},{5,4},{6,7},{7,6},{8,9},{9,8},{10,11... | collective-permute-start | bytes 884744 | tf_op jit(solution)/shard_map/ppermute | solution.py:262
  93.9 0.0 copy-done.1
  93.9 0.1 copy.8.window_ref
  93.9 0.0 collective-permute-done.2.side_s
  94.0 0.0 collective-permute-done.own_s
  94.0 0.0 collective-permute-done.4.prev_s
  94.0 1.4 collective-permute-done.6.nxt_s
  95.4 0.0 all-to-all-done.1
  95.4 17.4 %shard_map.78 = (bf16[4,2,2,96,128]{4,3,2,1,0:T(8,128)(2,1)S(1)}, bf16[6,3,2,2,96,128]{5,4,3,2,1,0:T(8,128)(2,1)}, bf16[2,3,2,2,96,128]{5,4,3,2,1,0:T(8,128)(2,1)S(1)}, bf16[4,3,2,2,96,128]{5,4,3,2,1,0:T(8,128)(2,1)}) custom-call(s32[1]{0:T(128)} %bitcast.zm_ref, s32[1]{0:T(128)} %bitcast.1.chip_ref, s32[1]{0:T(128)} %bitcast.2.line_ref, ...), custom_call_target="tpu_custom_call" | custom-call | flops 6000000000 | bytes 9000000 | tf_op jit(solution)/shard_map/pallas_call | solution.py:229
  112.8 0.0 copy-start
  112.8 2.4 %collective-permute-start.7 = (bf16[4,3,2,2,96,128]{5,4,3,2,1,0:T(8,128)(2,1)}, bf16[4,3,2,2,96,128]{5,4,3,2,1,0:T(8,128)(2,1)S(1)}, u32[]{:S(2)}, u32[]{:S(2)}) collective-permute-start(bf16[4,3,2,2,96,128]{5,4,3,2,1,0:T(8,128)(2,1)} %get-tuple-element.18), channel_id=1, source_target_pairs={{0,1},{1,0},{2,3},{3,2},{4,5},{5,4},{6,7},{7,6},{8,9},{9,8},{10,11... | collective-permute-start | bytes 3538952 | tf_op jit(solution)/shard_map/ppermute | solution.py:262
  115.2 2.0 %collective-permute-start.9 = (bf16[2,3,2,2,96,128]{5,4,3,2,1,0:T(8,128)(2,1)S(1)}, bf16[2,3,2,2,96,128]{5,4,3,2,1,0:T(8,128)(2,1)S(1)}, u32[]{:S(2)}, u32[]{:S(2)}) collective-permute-start(bf16[2,3,2,2,96,128]{5,4,3,2,1,0:T(8,128)(2,1)S(1)} %get-tuple-element.19), channel_id=1, source_target_pairs={{0,1},{1,0},{2,3},{3,2},{4,5},{5,4},{6,7},{7,6},{8,9},{9,8},{10,11... | collective-permute-start | bytes 1769480 | tf_op jit(solution)/shard_map/ppermute | solution.py:262
  117.2 1.8 collective-permute-done.9
  119.1 1.2 fusion.5
  120.3 1.9 collective-permute-start.11
  122.2 3.9 %collective-permute-start.10 = (bf16[3,2,2,96,128]{4,3,2,1,0:T(8,128)(2,1)S(1)}, bf16[3,2,2,96,128]{4,3,2,1,0:T(8,128)(2,1)S(1)}, u32[]{:S(2)}, u32[]{:S(2)}) collective-permute-start(bf16[3,2,2,96,128]{4,3,2,1,0:T(8,128)(2,1)S(1)} %get-tuple-element.36), channel_id=1, source_target_pairs={{0,64},{64,128},{128,192},{192,256},{256,320},{320,384},{384,448},... | collective-permute-start | bytes 884744 | tf_op jit(solution)/shard_map/ppermute | solution.py:292
  126.2 0.0 collective-permute-done.7
  126.2 0.0 copy-done
  126.2 0.1 fusion.10
  126.3 4.9 %collective-permute-start.8 = (bf16[2,2,2,96,128]{4,3,2,1,0:T(8,128)(2,1)S(1)}, bf16[2,2,2,96,128]{4,3,2,1,0:T(8,128)(2,1)S(1)}, u32[]{:S(2)}, u32[]{:S(2)}) collective-permute-start(bf16[2,2,2,96,128]{4,3,2,1,0:T(8,128)(2,1)S(1)} %pad_maximum_fusion.4), channel_id=1, source_target_pairs={{8,16},{16,8},{40,48},{48,40},{0,56},{56,0},{32,24},{24,32},{9,17}... | collective-permute-start | bytes 589832 | tf_op jit(solution)/shard_map/ppermute | solution.py:298
  131.2 0.1 collective-permute-done.11
  131.3 4.0 %collective-permute-done.10 = bf16[3,2,2,96,128]{4,3,2,1,0:T(8,128)(2,1)S(1)} collective-permute-done((bf16[3,2,2,96,128]{4,3,2,1,0:T(8,128)(2,1)S(1)}, bf16[3,2,2,96,128]{4,3,2,1,0:T(8,128)(2,1)S(1)}, u32[]{:S(2)}, u32[]{:S(2)}) %collective-permute-start.10) | collective-permute-done | bytes 294944 | tf_op jit(solution)/shard_map/ppermute | solution.py:292
  135.3 0.5 collective-permute-done.8
  135.8 0.1 fusion.9
  135.9 4.9 %collective-permute-start.12 = (bf16[2,2,2,96,128]{4,3,2,1,0:T(8,128)(2,1)S(1)}, bf16[2,2,2,96,128]{4,3,2,1,0:T(8,128)(2,1)S(1)}, u32[]{:S(2)}, u32[]{:S(2)}) collective-permute-start(bf16[2,2,2,96,128]{4,3,2,1,0:T(8,128)(2,1)S(1)} %pad_maximum_fusion.5), channel_id=1, source_target_pairs={{8,16},{16,8},{40,48},{48,40},{0,56},{56,0},{32,24},{24,32},{9,17}... | collective-permute-start | bytes 589832 | tf_op jit(solution)/shard_map/ppermute | solution.py:301
  140.8 0.2 add_convert_fusion.3
  141.0 3.7 %collective-permute-done.12 = bf16[2,2,2,96,128]{4,3,2,1,0:T(8,128)(2,1)S(1)} collective-permute-done((bf16[2,2,2,96,128]{4,3,2,1,0:T(8,128)(2,1)S(1)}, bf16[2,2,2,96,128]{4,3,2,1,0:T(8,128)(2,1)S(1)}, u32[]{:S(2)}, u32[]{:S(2)}) %collective-permute-start.12) | collective-permute-done | bytes 196640 | tf_op jit(solution)/shard_map/ppermute | solution.py:301
  144.7 0.2 fusion.6
  145.0 0.1 pad_maximum_fusion.1
  145.1 0.1 pad_maximum_fusion
  145.2 44.5 %all_to_all.15.in_ref = bf16[16,3,96,128]{3,2,1,0:T(8,128)(2,1)} all-to-all(bf16[16,3,96,128]{3,2,1,0:T(8,128)(2,1)S(1)} %pad_maximum_fusion), channel_id=1, replica_groups=mesh['yl'=2,'x'=4,'zh'=2,'zm'=2,'zl'=2,'yhh'=2,'yhl'=2,'c'=2] {'zh','yhh..., dimensions={0} | all-to-all | bytes 2359296 | tf_op jit(solution)/shard_map/all_to_all | solution.py:258
  189.8 2.6 %shard_map.79 = (bf16[96,2048]{1,0:T(8,128)(2,1)}, bf16[96,2048]{1,0:T(8,128)(2,1)}, bf16[96,2048]{1,0:T(8,128)(2,1)}) custom-call(s32[1]{0:T(128)} %bitcast.zm_ref, bf16[16,3,96,128]{3,2,1,0:T(8,128)(2,1)} %all_to_all.15.in_ref), custom_call_target="tpu_custom_call" | custom-call | bytes 2359296 | tf_op jit(solution)/shard_map/pallas_call | solution.py:62
  (10 shorter events, 0.2 us)
Async XLA Ops:
  2.8 40.2 %all-to-all-start = ((bf16[16,2,96,128]{3,2,1,0:T(8,128)(2,1)}), bf16[16,2,96,128]{3,2,1,0:T(8,128)(2,1)S(1)}, u32[]{:S(2)}, u32[]{:S(2)}) async-start(bf16[16,2,96,128]{3,2,1,0:T(8,128)(2,1)} %shard_map.76), calls=%async_computation | async-start | bytes 1572864 | tf_op jit(solution)/shard_map/all_to_all | solution.py:258
  43.0 14.0 %collective-permute-start.1 = (bf16[4,2,2,96,128]{4,3,2,1,0:T(8,128)(2,1)S(1)}, bf16[4,2,2,96,128]{4,3,2,1,0:T(8,128)(2,1)S(1)}, u32[]{:S(2)}, u32[]{:S(2)}) collective-permute-start(bf16[4,2,2,96,128]{4,3,2,1,0:T(8,128)(2,1)S(1)} %dynamic-slice_bitcast_fusion), channel_id=1, source_target_pairs={{8,16},{16,8},{40,48},{48,40},{0,56},{56,0},{32,24},{24,32},{9,17}... | collective-permute-start | bytes 1179656 | tf_op jit(solution)/shard_map/ppermute | solution.py:279
  57.0 38.3 %all-to-all-start.1 = ((bf16[16,2,96,128]{3,2,1,0:T(8,128)(2,1)}), bf16[16,2,96,128]{3,2,1,0:T(8,128)(2,1)S(1)}, u32[]{:S(2)}, u32[]{:S(2)}) async-start(bf16[16,2,96,128]{3,2,1,0:T(8,128)(2,1)} %shard_map.77), calls=%async_computation.1 | async-start | bytes 1572864 | tf_op jit(solution)/shard_map/all_to_all | solution.py:258
  63.6 30.3 %copy-start.1 = (s32[16,2]{0,1:T(2,128)S(1)}, s32[16,2]{0,1:T(2,128)}, u32[]{:S(2)}) copy-start(s32[16,2]{0,1:T(2,128)} %param.9) | copy-start | bytes 388
  63.6 30.4 %collective-permute-start = (bf16[4,2,2,2,96,128]{5,4,3,2,1,0:T(8,128)(2,1)S(1)}, bf16[4,2,2,2,96,128]{5,4,3,2,1,0:T(8,128)(2,1)S(1)}, u32[]{:S(2)}, u32[]{:S(2)}) collective-permute-start(bf16[4,2,2,2,96,128]{5,4,3,2,1,0:T(8,128)(2,1)S(1)} %bitcast.64), channel_id=1, source_target_pairs={{0,1},{1,0},{2,3},{3,2},{4,5},{5,4},{6,7},{7,6},{8,9},{9,8},{10,11... | collective-permute-start | bytes 2359304 | tf_op jit(solution)/shard_map/ppermute | solution.py:262
  65.6 23.9 %collective-permute-start.3 = (bf16[3,2,2,96,128]{4,3,2,1,0:T(8,128)(2,1)S(1)}, bf16[3,2,2,96,128]{4,3,2,1,0:T(8,128)(2,1)S(1)}, u32[]{:S(2)}, u32[]{:S(2)}) collective-permute-start(bf16[3,2,2,96,128]{4,3,2,1,0:T(8,128)(2,1)S(1)} %pad_maximum_fusion.2), channel_id=1, source_target_pairs={{0,64},{64,128},{128,192},{192,256},{256,320},{320,384},{384,448},... | collective-permute-start | bytes 884744 | tf_op jit(solution)/shard_map/ppermute | solution.py:284
  69.0 22.4 %collective-permute-start.5 = (bf16[3,2,2,96,128]{4,3,2,1,0:T(8,128)(2,1)S(1)}, bf16[3,2,2,96,128]{4,3,2,1,0:T(8,128)(2,1)}, u32[]{:S(2)}, u32[]{:S(2)}) collective-permute-start(bf16[3,2,2,96,128]{4,3,2,1,0:T(8,128)(2,1)S(1)} %pad_maximum_fusion.3), channel_id=1, source_target_pairs={{64,0},{128,64},{192,128},{256,192},{320,256},{384,320},{448,384},... | collective-permute-start | bytes 884744 | tf_op jit(solution)/shard_map/ppermute | solution.py:283
  75.3 18.6 %collective-permute-start.2 = (bf16[4,2,2,96,128]{4,3,2,1,0:T(8,128)(2,1)S(1)}, bf16[4,2,2,96,128]{4,3,2,1,0:T(8,128)(2,1)S(1)}, u32[]{:S(2)}, u32[]{:S(2)}) collective-permute-start(bf16[4,2,2,96,128]{4,3,2,1,0:T(8,128)(2,1)S(1)} %collective-permute-done.1.side), channel_id=1, source_target_pairs={{0,1},{1,0},{2,3},{3,2},{4,5},{5,4},{6,7},{7,6},{8,9},{9,8},{10,11... | collective-permute-start | bytes 1179656 | tf_op jit(solution)/shard_map/ppermute | solution.py:262
  89.5 4.5 %collective-permute-start.4 = (bf16[3,2,2,96,128]{4,3,2,1,0:T(8,128)(2,1)S(1)}, bf16[3,2,2,96,128]{4,3,2,1,0:T(8,128)(2,1)}, u32[]{:S(2)}, u32[]{:S(2)}) collective-permute-start(bf16[3,2,2,96,128]{4,3,2,1,0:T(8,128)(2,1)S(1)} %collective-permute-done.3.prev), channel_id=1, source_target_pairs={{0,1},{1,0},{2,3},{3,2},{4,5},{5,4},{6,7},{7,6},{8,9},{9,8},{10,11... | collective-permute-start | bytes 884744 | tf_op jit(solution)/shard_map/ppermute | solution.py:262
  91.4 3.9 %collective-permute-start.6 = (bf16[3,2,2,96,128]{4,3,2,1,0:T(8,128)(2,1)}, bf16[3,2,2,96,128]{4,3,2,1,0:T(8,128)(2,1)}, u32[]{:S(2)}, u32[]{:S(2)}) collective-permute-start(bf16[3,2,2,96,128]{4,3,2,1,0:T(8,128)(2,1)} %collective-permute-done.5.nxt), channel_id=1, source_target_pairs={{0,1},{1,0},{2,3},{3,2},{4,5},{5,4},{6,7},{7,6},{8,9},{9,8},{10,11... | collective-permute-start | bytes 884744 | tf_op jit(solution)/shard_map/ppermute | solution.py:262
  112.8 13.4 %copy-start = (bf16[6,3,2,2,96,128]{5,4,3,2,1,0:T(8,128)(2,1)S(1)}, bf16[6,3,2,2,96,128]{5,4,3,2,1,0:T(8,128)(2,1)}, u32[]{:S(2)}) copy-start(bf16[6,3,2,2,96,128]{5,4,3,2,1,0:T(8,128)(2,1)} %get-tuple-element.17) | copy-start | bytes 5308420
  112.8 13.4 %collective-permute-start.7 = (bf16[4,3,2,2,96,128]{5,4,3,2,1,0:T(8,128)(2,1)}, bf16[4,3,2,2,96,128]{5,4,3,2,1,0:T(8,128)(2,1)S(1)}, u32[]{:S(2)}, u32[]{:S(2)}) collective-permute-start(bf16[4,3,2,2,96,128]{5,4,3,2,1,0:T(8,128)(2,1)} %get-tuple-element.18), channel_id=1, source_target_pairs={{0,1},{1,0},{2,3},{3,2},{4,5},{5,4},{6,7},{7,6},{8,9},{9,8},{10,11... | collective-permute-start | bytes 3538952 | tf_op jit(solution)/shard_map/ppermute | solution.py:262
  115.2 3.9 %collective-permute-start.9 = (bf16[2,3,2,2,96,128]{5,4,3,2,1,0:T(8,128)(2,1)S(1)}, bf16[2,3,2,2,96,128]{5,4,3,2,1,0:T(8,128)(2,1)S(1)}, u32[]{:S(2)}, u32[]{:S(2)}) collective-permute-start(bf16[2,3,2,2,96,128]{5,4,3,2,1,0:T(8,128)(2,1)S(1)} %get-tuple-element.19), channel_id=1, source_target_pairs={{0,1},{1,0},{2,3},{3,2},{4,5},{5,4},{6,7},{7,6},{8,9},{9,8},{10,11... | collective-permute-start | bytes 1769480 | tf_op jit(solution)/shard_map/ppermute | solution.py:262
  120.3 10.9 %collective-permute-start.11 = (bf16[3,2,2,96,128]{4,3,2,1,0:T(8,128)(2,1)S(1)}, bf16[3,2,2,96,128]{4,3,2,1,0:T(8,128)(2,1)S(1)}, u32[]{:S(2)}, u32[]{:S(2)}) collective-permute-start(bf16[3,2,2,96,128]{4,3,2,1,0:T(8,128)(2,1)S(1)} %get-tuple-element.35), channel_id=1, source_target_pairs={{64,0},{128,64},{192,128},{256,192},{320,256},{384,320},{448,384},... | collective-permute-start | bytes 884744 | tf_op jit(solution)/shard_map/ppermute | solution.py:291
  122.2 13.1 %collective-permute-start.10 = (bf16[3,2,2,96,128]{4,3,2,1,0:T(8,128)(2,1)S(1)}, bf16[3,2,2,96,128]{4,3,2,1,0:T(8,128)(2,1)S(1)}, u32[]{:S(2)}, u32[]{:S(2)}) collective-permute-start(bf16[3,2,2,96,128]{4,3,2,1,0:T(8,128)(2,1)S(1)} %get-tuple-element.36), channel_id=1, source_target_pairs={{0,64},{64,128},{128,192},{192,256},{256,320},{320,384},{384,448},... | collective-permute-start | bytes 884744 | tf_op jit(solution)/shard_map/ppermute | solution.py:292
  126.3 9.5 %collective-permute-start.8 = (bf16[2,2,2,96,128]{4,3,2,1,0:T(8,128)(2,1)S(1)}, bf16[2,2,2,96,128]{4,3,2,1,0:T(8,128)(2,1)S(1)}, u32[]{:S(2)}, u32[]{:S(2)}) collective-permute-start(bf16[2,2,2,96,128]{4,3,2,1,0:T(8,128)(2,1)S(1)} %pad_maximum_fusion.4), channel_id=1, source_target_pairs={{8,16},{16,8},{40,48},{48,40},{0,56},{56,0},{32,24},{24,32},{9,17}... | collective-permute-start | bytes 589832 | tf_op jit(solution)/shard_map/ppermute | solution.py:298
  135.9 8.8 %collective-permute-start.12 = (bf16[2,2,2,96,128]{4,3,2,1,0:T(8,128)(2,1)S(1)}, bf16[2,2,2,96,128]{4,3,2,1,0:T(8,128)(2,1)S(1)}, u32[]{:S(2)}, u32[]{:S(2)}) collective-permute-start(bf16[2,2,2,96,128]{4,3,2,1,0:T(8,128)(2,1)S(1)} %pad_maximum_fusion.5), channel_id=1, source_target_pairs={{8,16},{16,8},{40,48},{48,40},{0,56},{56,0},{32,24},{24,32},{9,17}... | collective-permute-start | bytes 589832 | tf_op jit(solution)/shard_map/ppermute | solution.py:301
